TPU v7x, 256 devices: a whole 4x4x8 slice. The times are simulated.
256 devices in a mesh: region: 8 (over z), cell: 32 (over x, y, core).
Axes of the slice: x: 4, y: 4, z: 8, core: 2. Of those that a mesh axis runs over, the one named last changes fastest.
Arguments:
- positions: float32 [3, 1024, 512], P(None, ('region', 'cell')), may hold values from 0 to 1
- velocities: float32 [3, 1024, 512], P(None, ('region', 'cell')), may hold values from -6 to 6
- mass: float32 [1024, 512], P(('region', 'cell')), may hold values from 0.0002 to 0.001
- smoothing: float32 [1024, 512], P(('region', 'cell')), may hold values from 0.25 to 0.5
- energy: float32 [1024, 512], P(('region', 'cell')), may hold values from 0.5 to 2
- counts: int32 [1024], P(('region', 'cell')), may hold values from 128 to 512
- send_cells: int32 [8, 32, 32, 1], P('region', 'cell'), may hold values from -1 to 3, as said below
- local_pairs: int32 [8, 32, 4, 2], P('region', 'cell'), may hold values from 0 to 3, as said below
- edge_cells: int32 [8, 32, 2], P('region', 'cell'), may hold values from 0 to 3
Outputs:
- density: float32 [1024, 512], P(('region', 'cell'))
- accel: float32 [3, 1024, 512], P(None, ('region', 'cell'))
- energy_rate: float32 [1024, 512], P(('region', 'cell'))
Inputs may be any that keep to these rules, and one draw needn't show every extreme that they name: send_cells[r, c, c2, s] is a local cell index of device (r, c), or -1 for an empty slot; slot s is empty from c to c2 exactly when it is empty from c2 to c, and always empty for c2 = c. `local_pairs`: each row holds two different local cell indices of the device.
All inputs are finite; a program needn't handle non-finite values.
Results may differ from a plain program's by a relative error of at most 0.0003.
Values sent between devices are 32-bit elements; how exact they have to be, the bound alone decides.
A program may use at most 64 MiB of HBM per device.

v0:
```python
import math

import jax
import jax.numpy as jnp
from jax import lax
from jax.sharding import PartitionSpec as P

SLOT = 1
EB = 1


GAMMA = 5.0 / 3.0


def extended(cells, sides, width):
    for axis, dim in sides:
        count = lax.axis_size(axis)
        ends = count - 1
        head = lax.slice_in_dim(cells, 0, width, axis=dim)
        tail = lax.slice_in_dim(cells, cells.shape[dim] - width, cells.shape[dim], axis=dim)
        cells = jnp.concatenate(
            [
                lax.ppermute(tail, axis, [(i, (i + 1) % count) for i in range(ends)]),
                cells,
                lax.ppermute(head, axis, [((i + 1) % count, i) for i in range(ends)]),
            ],
            axis=dim,
        )
    return cells


def spline(distance, support_raw):
    support = jnp.where(support_raw > 0.0, support_raw, 1.0)
    scaled = distance / support
    norm_factor = 8.0 / (math.pi * support * support * support)
    inside = scaled < 0.5
    within = scaled < 1.0
    profile = jnp.where(
        inside,
        1.0 - 6.0 * scaled * scaled + 6.0 * scaled * scaled * scaled,
        jnp.where(within, 2.0 * (1.0 - scaled) ** 3, 0.0),
    )
    slope_term = jnp.where(
        inside,
        -12.0 + 18.0 * scaled,
        jnp.where(within, -6.0 * (1.0 - scaled) ** 2 / jnp.maximum(scaled, 0.5), 0.0),
    )
    return (norm_factor * profile, norm_factor * slope_term / (support * support))


def separation(target, source):
    apart_x = target[0][:, None] - source[0][None, :]
    apart_y = target[1][:, None] - source[1][None, :]
    apart_z = target[2][:, None] - source[2][None, :]
    distance = jnp.sqrt(apart_x * apart_x + apart_y * apart_y + apart_z * apart_z)
    return (apart_x, apart_y, apart_z, distance)


def density_tile(target, source):
    apart_x, apart_y, apart_z, distance = separation(target, source)
    kernel_value, _ = spline(distance, target[7][:, None])
    return jnp.sum(kernel_value * source[6][None, :], axis=1)


def force_tile(target, source):
    apart_x, apart_y, apart_z, distance = separation(target, source)
    _, own_slope = spline(distance, target[7][:, None])
    _, other_slope = spline(distance, source[7][None, :])
    weighted = source[6][None, :] * 0.5 * (own_slope + other_slope)
    coupled = weighted * (target[8][:, None] + source[8][None, :])
    accel_x = -jnp.sum(coupled * apart_x, axis=1)
    accel_y = -jnp.sum(coupled * apart_y, axis=1)
    accel_z = -jnp.sum(coupled * apart_z, axis=1)
    closing = (
        (target[3][:, None] - source[3][None, :]) * apart_x
        + (target[4][:, None] - source[4][None, :]) * apart_y
        + (target[5][:, None] - source[5][None, :]) * apart_z
    )
    heating = target[8] * jnp.sum(weighted * closing, axis=1)
    return jnp.stack([accel_x, accel_y, accel_z, heating])


def run_tiles(worker, targets, sources):
    total = targets.shape[0]
    block_count = total // 4
    target_blocks = targets.reshape((block_count, 4) + targets.shape[1:])
    source_blocks = sources.reshape((block_count, 4) + sources.shape[1:])
    results = lax.map(
        lambda block_pair: jax.vmap(worker)(block_pair[0], block_pair[1]),
        (target_blocks, source_blocks),
    )
    return results.reshape((total,) + results.shape[2:])


def tile_index(cell_pairs, send_list, edge_list, cell_count, peer_count):
    own_cells = jnp.arange(cell_count, dtype=jnp.int32)
    picked = jnp.clip(send_list, 0, cell_count - 1).reshape(-1)
    edge_base = cell_count + peer_count * SLOT
    edge_slots = jnp.arange(EB, dtype=jnp.int32)
    target_ids = jnp.concatenate(
        [
            own_cells,
            cell_pairs[:, 0],
            cell_pairs[:, 1],
            picked,
            jnp.repeat(edge_list[:EB], EB),
            jnp.repeat(edge_list[EB:], EB),
        ]
    )
    source_ids = jnp.concatenate(
        [
            own_cells,
            cell_pairs[:, 1],
            cell_pairs[:, 0],
            cell_count + jnp.arange(peer_count * SLOT, dtype=jnp.int32),
            edge_base + jnp.tile(edge_slots, EB),
            edge_base + EB + jnp.tile(edge_slots, EB),
        ]
    )
    used = 3 * cell_count + peer_count * SLOT + 2 * EB * EB
    padding = -used % 4
    weights = jnp.concatenate([jnp.ones((used,), jnp.float32), jnp.zeros((padding,), jnp.float32)])
    target_ids = jnp.concatenate([target_ids, jnp.zeros((padding,), jnp.int32)])
    source_ids = jnp.concatenate([source_ids, jnp.zeros((padding,), jnp.int32)])
    return (target_ids, source_ids, weights)


def on_device(
    positions, velocities, mass, smoothing, energy, counts, send_cells, local_pairs, edge_cells
):
    cell_count = mass.shape[0]
    slot_count = mass.shape[1]
    peer_count = send_cells.shape[2]
    pair_total = peer_count * SLOT
    slot_ids = lax.broadcasted_iota(jnp.int32, (cell_count, slot_count), 1)
    occupied = (slot_ids < counts[:, None]).astype(jnp.float32)
    state_rows = jnp.concatenate(
        [
            jnp.transpose(positions, (1, 0, 2)),
            jnp.transpose(velocities, (1, 0, 2)),
            (mass * occupied)[:, None],
            smoothing[:, None],
        ],
        axis=1,
    )
    send_list = send_cells[0, 0]
    edge_list = edge_cells[0, 0]
    alive = (send_list >= 0).astype(jnp.float32)
    picked = jnp.clip(send_list, 0, cell_count - 1)
    payload = state_rows[picked] * alive[:, :, None, None]
    received = lax.all_to_all(payload, "cell", split_axis=0, concat_axis=0, tiled=True)
    received_rows = received.reshape((pair_total,) + state_rows.shape[1:])
    bordered = extended(state_rows[edge_list], (("region", 0),), EB)
    outside = jnp.concatenate([bordered[:EB], bordered[3 * EB :]])
    table = jnp.concatenate([state_rows, received_rows, outside])
    target_ids, source_ids, weights = tile_index(
        local_pairs[0, 0], send_list, edge_list, cell_count, peer_count
    )
    assign = (target_ids[:, None] == jnp.arange(cell_count, dtype=jnp.int32)[None, :]).astype(
        jnp.float32
    ) * weights[:, None]
    density_terms = run_tiles(density_tile, state_rows[target_ids], table[source_ids])
    rho = jnp.dot(assign.T, density_terms, precision=lax.Precision.HIGHEST)
    pressure_term = occupied * (GAMMA - 1.0) * energy / (rho + 1.0 - occupied)
    force_rows = jnp.concatenate([state_rows, pressure_term[:, None]], axis=1)
    whole_payload = force_rows[picked] * alive[:, :, None, None]
    whole_received = lax.all_to_all(whole_payload, "cell", split_axis=0, concat_axis=0, tiled=True)
    whole_border = extended(force_rows[edge_list], (("region", 0),), EB)
    force_table = jnp.concatenate(
        [
            force_rows,
            whole_received.reshape((pair_total,) + force_rows.shape[1:]),
            whole_border[:EB],
            whole_border[3 * EB :],
        ]
    )
    force_terms = run_tiles(force_tile, force_rows[target_ids], force_table[source_ids])
    totals = jnp.einsum("tc,tkp->kcp", assign, force_terms, precision=lax.Precision.HIGHEST)
    return (rho * occupied, totals[:3] * occupied[None], totals[3] * occupied)


def solution(mesh):
    placed = (
        P(None, ("region", "cell"), None),
        P(None, ("region", "cell"), None),
        P(("region", "cell"), None),
        P(("region", "cell"), None),
        P(("region", "cell"), None),
        P(("region", "cell")),
        P("region", "cell", None, None),
        P("region", "cell", None, None),
        P("region", "cell", None),
    )
    return jax.shard_map(
        on_device,
        mesh=mesh,
        in_specs=placed,
        out_specs=(
            P(("region", "cell"), None),
            P(None, ("region", "cell"), None),
            P(("region", "cell"), None),
        ),
        check_vma=False,
    )
```

profile of v0, /device:TPU:1, one launch (start us, length us, event | category | flops | bytes accessed | tf_op | source)
XLA Modules:
  0.0 360.0 jit_solution(18426187996310046863)
XLA Ops:
  5.8 8.6 %all-to-all-start = ((f32[32,1,8,512]{3,2,1,0:T(8,128)}), f32[32,1,8,512]{3,2,1,0:T(8,128)S(1)}, u32[]{:S(2)}, u32[]{:S(2)}) async-start(f32[32,1,8,512]{3,2,1,0:T(8,128)} %fusion.26), calls=%async_computation | async-start | bytes 1048576 | tf_op jit(solution)/shard_map/all_to_all | solution.py:151
  15.0 3.5 collective-permute-start
  20.6 1.4 concatenate.75
  22.7 1.4 concatenate.69
  24.1 2.0 all-to-all-done
  26.8 63.2 %while.20 = (s32[]{:T(128)}, f32[12,4,512]{2,1,0:T(4,128)S(1)}, f32[12,4,8,512]{3,2,1,0:T(8,128)S(1)}, f32[12,4,8,512]{3,2,1,0:T(8,128)S(1)}, s32[]{:T(128)}) while((s32[]{:T(128)}, f32[12,4,512]{2,1,0:T(4,128)S(1)}, f32[12,4,8,512]{3,2,1,0:T(8,128)S(1)}, f32[12,4,8,512]{3,2,1,0:T(8,128)S(1)}, s32[]{:T(128)}) %tuple.101), condition=%wide.region_2.3_spmd, body=%wide.region_0.2_spmd.sunk | while | flops 26224640 | bytes 761925 | solution.py:88
  26.9 5.1 %fusion.61 = f32[4,512]{1,0:T(4,128)S(1)} fusion(f32[4,512]{1,0:T(4,128)S(1)} %get-tuple-element.218, f32[4,512]{1,0:T(4,128)S(1)} %get-tuple-element.220, f32[4,512]{1,0:T(4,128)S(1)} %get-tuple-element.221, f32[4,512]{1,0:T(4,128)S(1)} %get-tuple-element.222, f32[4,512]{1,0:T(4,128)S(1)} %get-tuple-element.223, ...), kind=kLoop, calls=%fused_computation.16.clone.1 | loop fusion | flops 26212352 | bytes 81920 | tf_op jit(solution)/shard_map/while/body/eval_jaxpr/vmap()/reduce_sum | solution.py:62
  32.2 5.1 %fusion.61 = f32[4,512]{1,0:T(4,128)S(1)} fusion(f32[4,512]{1,0:T(4,128)S(1)} %get-tuple-element.218, f32[4,512]{1,0:T(4,128)S(1)} %get-tuple-element.220, f32[4,512]{1,0:T(4,128)S(1)} %get-tuple-element.221, f32[4,512]{1,0:T(4,128)S(1)} %get-tuple-element.222, f32[4,512]{1,0:T(4,128)S(1)} %get-tuple-element.223, ...), kind=kLoop, calls=%fused_computation.16.clone.1 | loop fusion | flops 26212352 | bytes 81920 | tf_op jit(solution)/shard_map/while/body/eval_jaxpr/vmap()/reduce_sum | solution.py:62
  37.5 5.1 %fusion.61 = f32[4,512]{1,0:T(4,128)S(1)} fusion(f32[4,512]{1,0:T(4,128)S(1)} %get-tuple-element.218, f32[4,512]{1,0:T(4,128)S(1)} %get-tuple-element.220, f32[4,512]{1,0:T(4,128)S(1)} %get-tuple-element.221, f32[4,512]{1,0:T(4,128)S(1)} %get-tuple-element.222, f32[4,512]{1,0:T(4,128)S(1)} %get-tuple-element.223, ...), kind=kLoop, calls=%fused_computation.16.clone.1 | loop fusion | flops 26212352 | bytes 81920 | tf_op jit(solution)/shard_map/while/body/eval_jaxpr/vmap()/reduce_sum | solution.py:62
  42.8 5.1 %fusion.61 = f32[4,512]{1,0:T(4,128)S(1)} fusion(f32[4,512]{1,0:T(4,128)S(1)} %get-tuple-element.218, f32[4,512]{1,0:T(4,128)S(1)} %get-tuple-element.220, f32[4,512]{1,0:T(4,128)S(1)} %get-tuple-element.221, f32[4,512]{1,0:T(4,128)S(1)} %get-tuple-element.222, f32[4,512]{1,0:T(4,128)S(1)} %get-tuple-element.223, ...), kind=kLoop, calls=%fused_computation.16.clone.1 | loop fusion | flops 26212352 | bytes 81920 | tf_op jit(solution)/shard_map/while/body/eval_jaxpr/vmap()/reduce_sum | solution.py:62
  48.0 5.1 %fusion.61 = f32[4,512]{1,0:T(4,128)S(1)} fusion(f32[4,512]{1,0:T(4,128)S(1)} %get-tuple-element.218, f32[4,512]{1,0:T(4,128)S(1)} %get-tuple-element.220, f32[4,512]{1,0:T(4,128)S(1)} %get-tuple-element.221, f32[4,512]{1,0:T(4,128)S(1)} %get-tuple-element.222, f32[4,512]{1,0:T(4,128)S(1)} %get-tuple-element.223, ...), kind=kLoop, calls=%fused_computation.16.clone.1 | loop fusion | flops 26212352 | bytes 81920 | tf_op jit(solution)/shard_map/while/body/eval_jaxpr/vmap()/reduce_sum | solution.py:62
  53.3 5.1 %fusion.61 = f32[4,512]{1,0:T(4,128)S(1)} fusion(f32[4,512]{1,0:T(4,128)S(1)} %get-tuple-element.218, f32[4,512]{1,0:T(4,128)S(1)} %get-tuple-element.220, f32[4,512]{1,0:T(4,128)S(1)} %get-tuple-element.221, f32[4,512]{1,0:T(4,128)S(1)} %get-tuple-element.222, f32[4,512]{1,0:T(4,128)S(1)} %get-tuple-element.223, ...), kind=kLoop, calls=%fused_computation.16.clone.1 | loop fusion | flops 26212352 | bytes 81920 | tf_op jit(solution)/shard_map/while/body/eval_jaxpr/vmap()/reduce_sum | solution.py:62
  58.6 5.1 %fusion.61 = f32[4,512]{1,0:T(4,128)S(1)} fusion(f32[4,512]{1,0:T(4,128)S(1)} %get-tuple-element.218, f32[4,512]{1,0:T(4,128)S(1)} %get-tuple-element.220, f32[4,512]{1,0:T(4,128)S(1)} %get-tuple-element.221, f32[4,512]{1,0:T(4,128)S(1)} %get-tuple-element.222, f32[4,512]{1,0:T(4,128)S(1)} %get-tuple-element.223, ...), kind=kLoop, calls=%fused_computation.16.clone.1 | loop fusion | flops 26212352 | bytes 81920 | tf_op jit(solution)/shard_map/while/body/eval_jaxpr/vmap()/reduce_sum | solution.py:62
  63.8 5.1 %fusion.61 = f32[4,512]{1,0:T(4,128)S(1)} fusion(f32[4,512]{1,0:T(4,128)S(1)} %get-tuple-element.218, f32[4,512]{1,0:T(4,128)S(1)} %get-tuple-element.220, f32[4,512]{1,0:T(4,128)S(1)} %get-tuple-element.221, f32[4,512]{1,0:T(4,128)S(1)} %get-tuple-element.222, f32[4,512]{1,0:T(4,128)S(1)} %get-tuple-element.223, ...), kind=kLoop, calls=%fused_computation.16.clone.1 | loop fusion | flops 26212352 | bytes 81920 | tf_op jit(solution)/shard_map/while/body/eval_jaxpr/vmap()/reduce_sum | solution.py:62
  69.1 5.1 %fusion.61 = f32[4,512]{1,0:T(4,128)S(1)} fusion(f32[4,512]{1,0:T(4,128)S(1)} %get-tuple-element.218, f32[4,512]{1,0:T(4,128)S(1)} %get-tuple-element.220, f32[4,512]{1,0:T(4,128)S(1)} %get-tuple-element.221, f32[4,512]{1,0:T(4,128)S(1)} %get-tuple-element.222, f32[4,512]{1,0:T(4,128)S(1)} %get-tuple-element.223, ...), kind=kLoop, calls=%fused_computation.16.clone.1 | loop fusion | flops 26212352 | bytes 81920 | tf_op jit(solution)/shard_map/while/body/eval_jaxpr/vmap()/reduce_sum | solution.py:62
  74.4 5.1 %fusion.61 = f32[4,512]{1,0:T(4,128)S(1)} fusion(f32[4,512]{1,0:T(4,128)S(1)} %get-tuple-element.218, f32[4,512]{1,0:T(4,128)S(1)} %get-tuple-element.220, f32[4,512]{1,0:T(4,128)S(1)} %get-tuple-element.221, f32[4,512]{1,0:T(4,128)S(1)} %get-tuple-element.222, f32[4,512]{1,0:T(4,128)S(1)} %get-tuple-element.223, ...), kind=kLoop, calls=%fused_computation.16.clone.1 | loop fusion | flops 26212352 | bytes 81920 | tf_op jit(solution)/shard_map/while/body/eval_jaxpr/vmap()/reduce_sum | solution.py:62
  79.6 5.1 %fusion.61 = f32[4,512]{1,0:T(4,128)S(1)} fusion(f32[4,512]{1,0:T(4,128)S(1)} %get-tuple-element.218, f32[4,512]{1,0:T(4,128)S(1)} %get-tuple-element.220, f32[4,512]{1,0:T(4,128)S(1)} %get-tuple-element.221, f32[4,512]{1,0:T(4,128)S(1)} %get-tuple-element.222, f32[4,512]{1,0:T(4,128)S(1)} %get-tuple-element.223, ...), kind=kLoop, calls=%fused_computation.16.clone.1 | loop fusion | flops 26212352 | bytes 81920 | tf_op jit(solution)/shard_map/while/body/eval_jaxpr/vmap()/reduce_sum | solution.py:62
  84.9 5.1 %fusion.61 = f32[4,512]{1,0:T(4,128)S(1)} fusion(f32[4,512]{1,0:T(4,128)S(1)} %get-tuple-element.218, f32[4,512]{1,0:T(4,128)S(1)} %get-tuple-element.220, f32[4,512]{1,0:T(4,128)S(1)} %get-tuple-element.221, f32[4,512]{1,0:T(4,128)S(1)} %get-tuple-element.222, f32[4,512]{1,0:T(4,128)S(1)} %get-tuple-element.223, ...), kind=kLoop, calls=%fused_computation.16.clone.1 | loop fusion | flops 26212352 | bytes 81920 | tf_op jit(solution)/shard_map/while/body/eval_jaxpr/vmap()/reduce_sum | solution.py:62
  91.7 1.5 copy.62
  93.2 5.8 %all-to-all-start.1 = ((f32[32,1,9,512]{3,1,2,0:T(1,128)}), f32[32,1,9,512]{3,1,2,0:T(1,128)S(1)}, u32[]{:S(2)}, u32[]{:S(2)}) async-start(f32[32,1,9,512]{3,1,2,0:T(1,128)} %copy.62), calls=%async_computation.1 | async-start | bytes 1179648 | tf_op jit(solution)/shard_map/all_to_all | solution.py:167
  99.6 4.1 %collective-permute-start.2 = (f32[1,9,512]{2,1,0:T(8,128)S(1)}, f32[1,9,512]{2,1,0:T(8,128)S(1)}, u32[]{:S(2)}, u32[]{:S(2)}) collective-permute-start(f32[1,9,512]{2,1,0:T(8,128)S(1)} %get-tuple-element.118), channel_id=1, source_target_pairs={{0,32},{32,64},{64,96},{96,128},{128,160},{160,192},{192,224},{1,3... | collective-permute-start | bytes 55304 | tf_op jit(solution)/shard_map/ppermute | solution.py:23
  105.8 1.5 copy.66
  107.3 4.0 %all-to-all-done.1 = f32[32,1,9,512]{3,1,2,0:T(1,128)S(1)} async-done(((f32[32,1,9,512]{3,1,2,0:T(1,128)}), f32[32,1,9,512]{3,1,2,0:T(1,128)S(1)}, u32[]{:S(2)}, u32[]{:S(2)}) %all-to-all-start.1) | async-done | bytes 589856 | tf_op jit(solution)/shard_map/all_to_all | solution.py:167
  112.8 245.4 %while.21 = (s32[]{:T(128)}, f32[12,4,4,512]{3,2,1,0:T(4,128)S(1)}, f32[12,4,9,512]{3,1,2,0:T(4,128)S(1)}, f32[12,4,9,512]{3,1,2,0:T(4,128)}, s32[]{:T(128)}) while((s32[]{:T(128)}, f32[12,4,4,512]{3,2,1,0:T(4,128)S(1)}, f32[12,4,9,512]{3,1,2,0:T(4,128)S(1)}, f32[12,4,9,512]{3,1,2,0:T(4,128)}, s32[]{:T(128)}) %tuple.97), condition=%wide.region_8.9_spmd, body=%wide.region_3.8_spmd.sunk | while | flops 98621440 | bytes 1122373 | solution.py:88
  113.8 9.3 %fusion.64 = (f32[4,512]{1,0:T(4,128)S(1)}, f32[4,512]{1,0:T(4,128)S(1)}, f32[4,512]{1,0:T(4,128)S(1)}) fusion(f32[4,512]{1,0:T(4,128)S(1)} %get-tuple-element.253, f32[4,512]{1,0:T(4,128)S(1)} %get-tuple-element.254, f32[4,512]{1,0:T(4,128)S(1)} %get-tuple-element.244, f32[4,512]{1,0:T(4,128)S(1)} %get-tuple-element.245, ...), kind=kLoop, calls=%fused_computation.48.clone.1 | loop fusion | flops 48228352 | bytes 147456 | tf_op jit(solution)/shard_map/while/body/eval_jaxpr/vmap()/reduce_sum | solution.py:71
  123.2 10.1 %fusion.63 = f32[4,512]{1,0:T(4,128)S(1)} fusion(f32[4,512]{1,0:T(4,128)S(1)} %get-tuple-element.233, f32[4,512]{1,0:T(4,128)S(1)} %get-tuple-element.235, f32[4,512]{1,0:T(4,128)S(1)} %get-tuple-element.236, f32[4,512]{1,0:T(4,128)S(1)} %get-tuple-element.237, f32[4,512]{1,0:T(4,128)S(1)} %get-tuple-element.238, ...), kind=kLoop, calls=%fused_computation.52.clone.1 | loop fusion | flops 50329600 | bytes 163840 | tf_op jit(solution)/shard_map/while/body/eval_jaxpr/vmap()/reduce_sum | solution.py:79
  134.3 9.3 %fusion.64 = (f32[4,512]{1,0:T(4,128)S(1)}, f32[4,512]{1,0:T(4,128)S(1)}, f32[4,512]{1,0:T(4,128)S(1)}) fusion(f32[4,512]{1,0:T(4,128)S(1)} %get-tuple-element.253, f32[4,512]{1,0:T(4,128)S(1)} %get-tuple-element.254, f32[4,512]{1,0:T(4,128)S(1)} %get-tuple-element.244, f32[4,512]{1,0:T(4,128)S(1)} %get-tuple-element.245, ...), kind=kLoop, calls=%fused_computation.48.clone.1 | loop fusion | flops 48228352 | bytes 147456 | tf_op jit(solution)/shard_map/while/body/eval_jaxpr/vmap()/reduce_sum | solution.py:71
  143.6 10.1 %fusion.63 = f32[4,512]{1,0:T(4,128)S(1)} fusion(f32[4,512]{1,0:T(4,128)S(1)} %get-tuple-element.233, f32[4,512]{1,0:T(4,128)S(1)} %get-tuple-element.235, f32[4,512]{1,0:T(4,128)S(1)} %get-tuple-element.236, f32[4,512]{1,0:T(4,128)S(1)} %get-tuple-element.237, f32[4,512]{1,0:T(4,128)S(1)} %get-tuple-element.238, ...), kind=kLoop, calls=%fused_computation.52.clone.1 | loop fusion | flops 50329600 | bytes 163840 | tf_op jit(solution)/shard_map/while/body/eval_jaxpr/vmap()/reduce_sum | solution.py:79
  154.7 9.3 %fusion.64 = (f32[4,512]{1,0:T(4,128)S(1)}, f32[4,512]{1,0:T(4,128)S(1)}, f32[4,512]{1,0:T(4,128)S(1)}) fusion(f32[4,512]{1,0:T(4,128)S(1)} %get-tuple-element.253, f32[4,512]{1,0:T(4,128)S(1)} %get-tuple-element.254, f32[4,512]{1,0:T(4,128)S(1)} %get-tuple-element.244, f32[4,512]{1,0:T(4,128)S(1)} %get-tuple-element.245, ...), kind=kLoop, calls=%fused_computation.48.clone.1 | loop fusion | flops 48228352 | bytes 147456 | tf_op jit(solution)/shard_map/while/body/eval_jaxpr/vmap()/reduce_sum | solution.py:71
  164.1 10.1 %fusion.63 = f32[4,512]{1,0:T(4,128)S(1)} fusion(f32[4,512]{1,0:T(4,128)S(1)} %get-tuple-element.233, f32[4,512]{1,0:T(4,128)S(1)} %get-tuple-element.235, f32[4,512]{1,0:T(4,128)S(1)} %get-tuple-element.236, f32[4,512]{1,0:T(4,128)S(1)} %get-tuple-element.237, f32[4,512]{1,0:T(4,128)S(1)} %get-tuple-element.238, ...), kind=kLoop, calls=%fused_computation.52.clone.1 | loop fusion | flops 50329600 | bytes 163840 | tf_op jit(solution)/shard_map/while/body/eval_jaxpr/vmap()/reduce_sum | solution.py:79
  175.2 9.3 %fusion.64 = (f32[4,512]{1,0:T(4,128)S(1)}, f32[4,512]{1,0:T(4,128)S(1)}, f32[4,512]{1,0:T(4,128)S(1)}) fusion(f32[4,512]{1,0:T(4,128)S(1)} %get-tuple-element.253, f32[4,512]{1,0:T(4,128)S(1)} %get-tuple-element.254, f32[4,512]{1,0:T(4,128)S(1)} %get-tuple-element.244, f32[4,512]{1,0:T(4,128)S(1)} %get-tuple-element.245, ...), kind=kLoop, calls=%fused_computation.48.clone.1 | loop fusion | flops 48228352 | bytes 147456 | tf_op jit(solution)/shard_map/while/body/eval_jaxpr/vmap()/reduce_sum | solution.py:71
  184.5 10.1 %fusion.63 = f32[4,512]{1,0:T(4,128)S(1)} fusion(f32[4,512]{1,0:T(4,128)S(1)} %get-tuple-element.233, f32[4,512]{1,0:T(4,128)S(1)} %get-tuple-element.235, f32[4,512]{1,0:T(4,128)S(1)} %get-tuple-element.236, f32[4,512]{1,0:T(4,128)S(1)} %get-tuple-element.237, f32[4,512]{1,0:T(4,128)S(1)} %get-tuple-element.238, ...), kind=kLoop, calls=%fused_computation.52.clone.1 | loop fusion | flops 50329600 | bytes 163840 | tf_op jit(solution)/shard_map/while/body/eval_jaxpr/vmap()/reduce_sum | solution.py:79
  195.6 9.3 %fusion.64 = (f32[4,512]{1,0:T(4,128)S(1)}, f32[4,512]{1,0:T(4,128)S(1)}, f32[4,512]{1,0:T(4,128)S(1)}) fusion(f32[4,512]{1,0:T(4,128)S(1)} %get-tuple-element.253, f32[4,512]{1,0:T(4,128)S(1)} %get-tuple-element.254, f32[4,512]{1,0:T(4,128)S(1)} %get-tuple-element.244, f32[4,512]{1,0:T(4,128)S(1)} %get-tuple-element.245, ...), kind=kLoop, calls=%fused_computation.48.clone.1 | loop fusion | flops 48228352 | bytes 147456 | tf_op jit(solution)/shard_map/while/body/eval_jaxpr/vmap()/reduce_sum | solution.py:71
  205.0 10.1 %fusion.63 = f32[4,512]{1,0:T(4,128)S(1)} fusion(f32[4,512]{1,0:T(4,128)S(1)} %get-tuple-element.233, f32[4,512]{1,0:T(4,128)S(1)} %get-tuple-element.235, f32[4,512]{1,0:T(4,128)S(1)} %get-tuple-element.236, f32[4,512]{1,0:T(4,128)S(1)} %get-tuple-element.237, f32[4,512]{1,0:T(4,128)S(1)} %get-tuple-element.238, ...), kind=kLoop, calls=%fused_computation.52.clone.1 | loop fusion | flops 50329600 | bytes 163840 | tf_op jit(solution)/shard_map/while/body/eval_jaxpr/vmap()/reduce_sum | solution.py:79
  216.1 9.3 %fusion.64 = (f32[4,512]{1,0:T(4,128)S(1)}, f32[4,512]{1,0:T(4,128)S(1)}, f32[4,512]{1,0:T(4,128)S(1)}) fusion(f32[4,512]{1,0:T(4,128)S(1)} %get-tuple-element.253, f32[4,512]{1,0:T(4,128)S(1)} %get-tuple-element.254, f32[4,512]{1,0:T(4,128)S(1)} %get-tuple-element.244, f32[4,512]{1,0:T(4,128)S(1)} %get-tuple-element.245, ...), kind=kLoop, calls=%fused_computation.48.clone.1 | loop fusion | flops 48228352 | bytes 147456 | tf_op jit(solution)/shard_map/while/body/eval_jaxpr/vmap()/reduce_sum | solution.py:71
  225.4 10.1 %fusion.63 = f32[4,512]{1,0:T(4,128)S(1)} fusion(f32[4,512]{1,0:T(4,128)S(1)} %get-tuple-element.233, f32[4,512]{1,0:T(4,128)S(1)} %get-tuple-element.235, f32[4,512]{1,0:T(4,128)S(1)} %get-tuple-element.236, f32[4,512]{1,0:T(4,128)S(1)} %get-tuple-element.237, f32[4,512]{1,0:T(4,128)S(1)} %get-tuple-element.238, ...), kind=kLoop, calls=%fused_computation.52.clone.1 | loop fusion | flops 50329600 | bytes 163840 | tf_op jit(solution)/shard_map/while/body/eval_jaxpr/vmap()/reduce_sum | solution.py:79
  236.5 9.3 %fusion.64 = (f32[4,512]{1,0:T(4,128)S(1)}, f32[4,512]{1,0:T(4,128)S(1)}, f32[4,512]{1,0:T(4,128)S(1)}) fusion(f32[4,512]{1,0:T(4,128)S(1)} %get-tuple-element.253, f32[4,512]{1,0:T(4,128)S(1)} %get-tuple-element.254, f32[4,512]{1,0:T(4,128)S(1)} %get-tuple-element.244, f32[4,512]{1,0:T(4,128)S(1)} %get-tuple-element.245, ...), kind=kLoop, calls=%fused_computation.48.clone.1 | loop fusion | flops 48228352 | bytes 147456 | tf_op jit(solution)/shard_map/while/body/eval_jaxpr/vmap()/reduce_sum | solution.py:71
  245.9 10.1 %fusion.63 = f32[4,512]{1,0:T(4,128)S(1)} fusion(f32[4,512]{1,0:T(4,128)S(1)} %get-tuple-element.233, f32[4,512]{1,0:T(4,128)S(1)} %get-tuple-element.235, f32[4,512]{1,0:T(4,128)S(1)} %get-tuple-element.236, f32[4,512]{1,0:T(4,128)S(1)} %get-tuple-element.237, f32[4,512]{1,0:T(4,128)S(1)} %get-tuple-element.238, ...), kind=kLoop, calls=%fused_computation.52.clone.1 | loop fusion | flops 50329600 | bytes 163840 | tf_op jit(solution)/shard_map/while/body/eval_jaxpr/vmap()/reduce_sum | solution.py:79
  257.0 9.3 %fusion.64 = (f32[4,512]{1,0:T(4,128)S(1)}, f32[4,512]{1,0:T(4,128)S(1)}, f32[4,512]{1,0:T(4,128)S(1)}) fusion(f32[4,512]{1,0:T(4,128)S(1)} %get-tuple-element.253, f32[4,512]{1,0:T(4,128)S(1)} %get-tuple-element.254, f32[4,512]{1,0:T(4,128)S(1)} %get-tuple-element.244, f32[4,512]{1,0:T(4,128)S(1)} %get-tuple-element.245, ...), kind=kLoop, calls=%fused_computation.48.clone.1 | loop fusion | flops 48228352 | bytes 147456 | tf_op jit(solution)/shard_map/while/body/eval_jaxpr/vmap()/reduce_sum | solution.py:71
  266.3 10.1 %fusion.63 = f32[4,512]{1,0:T(4,128)S(1)} fusion(f32[4,512]{1,0:T(4,128)S(1)} %get-tuple-element.233, f32[4,512]{1,0:T(4,128)S(1)} %get-tuple-element.235, f32[4,512]{1,0:T(4,128)S(1)} %get-tuple-element.236, f32[4,512]{1,0:T(4,128)S(1)} %get-tuple-element.237, f32[4,512]{1,0:T(4,128)S(1)} %get-tuple-element.238, ...), kind=kLoop, calls=%fused_computation.52.clone.1 | loop fusion | flops 50329600 | bytes 163840 | tf_op jit(solution)/shard_map/while/body/eval_jaxpr/vmap()/reduce_sum | solution.py:79
  277.4 9.3 %fusion.64 = (f32[4,512]{1,0:T(4,128)S(1)}, f32[4,512]{1,0:T(4,128)S(1)}, f32[4,512]{1,0:T(4,128)S(1)}) fusion(f32[4,512]{1,0:T(4,128)S(1)} %get-tuple-element.253, f32[4,512]{1,0:T(4,128)S(1)} %get-tuple-element.254, f32[4,512]{1,0:T(4,128)S(1)} %get-tuple-element.244, f32[4,512]{1,0:T(4,128)S(1)} %get-tuple-element.245, ...), kind=kLoop, calls=%fused_computation.48.clone.1 | loop fusion | flops 48228352 | bytes 147456 | tf_op jit(solution)/shard_map/while/body/eval_jaxpr/vmap()/reduce_sum | solution.py:71
  286.8 10.1 %fusion.63 = f32[4,512]{1,0:T(4,128)S(1)} fusion(f32[4,512]{1,0:T(4,128)S(1)} %get-tuple-element.233, f32[4,512]{1,0:T(4,128)S(1)} %get-tuple-element.235, f32[4,512]{1,0:T(4,128)S(1)} %get-tuple-element.236, f32[4,512]{1,0:T(4,128)S(1)} %get-tuple-element.237, f32[4,512]{1,0:T(4,128)S(1)} %get-tuple-element.238, ...), kind=kLoop, calls=%fused_computation.52.clone.1 | loop fusion | flops 50329600 | bytes 163840 | tf_op jit(solution)/shard_map/while/body/eval_jaxpr/vmap()/reduce_sum | solution.py:79
  297.9 9.3 %fusion.64 = (f32[4,512]{1,0:T(4,128)S(1)}, f32[4,512]{1,0:T(4,128)S(1)}, f32[4,512]{1,0:T(4,128)S(1)}) fusion(f32[4,512]{1,0:T(4,128)S(1)} %get-tuple-element.253, f32[4,512]{1,0:T(4,128)S(1)} %get-tuple-element.254, f32[4,512]{1,0:T(4,128)S(1)} %get-tuple-element.244, f32[4,512]{1,0:T(4,128)S(1)} %get-tuple-element.245, ...), kind=kLoop, calls=%fused_computation.48.clone.1 | loop fusion | flops 48228352 | bytes 147456 | tf_op jit(solution)/shard_map/while/body/eval_jaxpr/vmap()/reduce_sum | solution.py:71
  307.2 10.1 %fusion.63 = f32[4,512]{1,0:T(4,128)S(1)} fusion(f32[4,512]{1,0:T(4,128)S(1)} %get-tuple-element.233, f32[4,512]{1,0:T(4,128)S(1)} %get-tuple-element.235, f32[4,512]{1,0:T(4,128)S(1)} %get-tuple-element.236, f32[4,512]{1,0:T(4,128)S(1)} %get-tuple-element.237, f32[4,512]{1,0:T(4,128)S(1)} %get-tuple-element.238, ...), kind=kLoop, calls=%fused_computation.52.clone.1 | loop fusion | flops 50329600 | bytes 163840 | tf_op jit(solution)/shard_map/while/body/eval_jaxpr/vmap()/reduce_sum | solution.py:79
  318.3 9.3 %fusion.64 = (f32[4,512]{1,0:T(4,128)S(1)}, f32[4,512]{1,0:T(4,128)S(1)}, f32[4,512]{1,0:T(4,128)S(1)}) fusion(f32[4,512]{1,0:T(4,128)S(1)} %get-tuple-element.253, f32[4,512]{1,0:T(4,128)S(1)} %get-tuple-element.254, f32[4,512]{1,0:T(4,128)S(1)} %get-tuple-element.244, f32[4,512]{1,0:T(4,128)S(1)} %get-tuple-element.245, ...), kind=kLoop, calls=%fused_computation.48.clone.1 | loop fusion | flops 48228352 | bytes 147456 | tf_op jit(solution)/shard_map/while/body/eval_jaxpr/vmap()/reduce_sum | solution.py:71
  327.7 10.1 %fusion.63 = f32[4,512]{1,0:T(4,128)S(1)} fusion(f32[4,512]{1,0:T(4,128)S(1)} %get-tuple-element.233, f32[4,512]{1,0:T(4,128)S(1)} %get-tuple-element.235, f32[4,512]{1,0:T(4,128)S(1)} %get-tuple-element.236, f32[4,512]{1,0:T(4,128)S(1)} %get-tuple-element.237, f32[4,512]{1,0:T(4,128)S(1)} %get-tuple-element.238, ...), kind=kLoop, calls=%fused_computation.52.clone.1 | loop fusion | flops 50329600 | bytes 163840 | tf_op jit(solution)/shard_map/while/body/eval_jaxpr/vmap()/reduce_sum | solution.py:79
  338.8 9.3 %fusion.64 = (f32[4,512]{1,0:T(4,128)S(1)}, f32[4,512]{1,0:T(4,128)S(1)}, f32[4,512]{1,0:T(4,128)S(1)}) fusion(f32[4,512]{1,0:T(4,128)S(1)} %get-tuple-element.253, f32[4,512]{1,0:T(4,128)S(1)} %get-tuple-element.254, f32[4,512]{1,0:T(4,128)S(1)} %get-tuple-element.244, f32[4,512]{1,0:T(4,128)S(1)} %get-tuple-element.245, ...), kind=kLoop, calls=%fused_computation.48.clone.1 | loop fusion | flops 48228352 | bytes 147456 | tf_op jit(solution)/shard_map/while/body/eval_jaxpr/vmap()/reduce_sum | solution.py:71
  348.1 10.1 %fusion.63 = f32[4,512]{1,0:T(4,128)S(1)} fusion(f32[4,512]{1,0:T(4,128)S(1)} %get-tuple-element.233, f32[4,512]{1,0:T(4,128)S(1)} %get-tuple-element.235, f32[4,512]{1,0:T(4,128)S(1)} %get-tuple-element.236, f32[4,512]{1,0:T(4,128)S(1)} %get-tuple-element.237, f32[4,512]{1,0:T(4,128)S(1)} %get-tuple-element.238, ...), kind=kLoop, calls=%fused_computation.52.clone.1 | loop fusion | flops 50329600 | bytes 163840 | tf_op jit(solution)/shard_map/while/body/eval_jaxpr/vmap()/reduce_sum | solution.py:79
  (272 shorter events, 30.2 us)
Async XLA Ops:
  4.3 10.1 %copy-start.3 = (s32[1,1,2]{2,1,0:T(1,128)S(1)}, s32[1,1,2]{2,1,0:T(1,128)}, u32[]{:S(2)}) copy-start(s32[1,1,2]{2,1,0:T(1,128)} %param.21) | copy-start | bytes 28
  4.3 15.6 %copy-start.5 = (s32[1,1,32,1]{2,3,1,0:T(1,128)S(1)}, s32[1,1,32,1]{2,3,1,0:T(1,128)}, u32[]{:S(2)}) copy-start(s32[1,1,32,1]{2,3,1,0:T(1,128)} %param.19) | copy-start | bytes 388
  4.3 15.6 %copy-start.4 = (s32[1,1,4,2]{2,3,1,0:T(2,128)S(1)}, s32[1,1,4,2]{2,3,1,0:T(2,128)}, u32[]{:S(2)}) copy-start(s32[1,1,4,2]{2,3,1,0:T(2,128)} %param.20) | copy-start | bytes 100
  5.8 20.2 %all-to-all-start = ((f32[32,1,8,512]{3,2,1,0:T(8,128)}), f32[32,1,8,512]{3,2,1,0:T(8,128)S(1)}, u32[]{:S(2)}, u32[]{:S(2)}) async-start(f32[32,1,8,512]{3,2,1,0:T(8,128)} %fusion.26), calls=%async_computation | async-start | bytes 1048576 | tf_op jit(solution)/shard_map/all_to_all | solution.py:151
  15.0 9.0 %collective-permute-start = (f32[1,8,512]{2,1,0:T(8,128)S(1)}, f32[1,8,512]{2,1,0:T(8,128)S(1)}, u32[]{:S(2)}, u32[]{:S(2)}) collective-permute-start(f32[1,8,512]{2,1,0:T(8,128)S(1)} %get-tuple-element.120), channel_id=1, source_target_pairs={{0,32},{32,64},{64,96},{96,128},{128,160},{160,192},{192,224},{1,3... | collective-permute-start | bytes 49160 | tf_op jit(solution)/shard_map/ppermute | solution.py:23
  18.6 5.5 %collective-permute-start.1 = (f32[1,8,512]{2,1,0:T(8,128)S(1)}, f32[1,8,512]{2,1,0:T(8,128)S(1)}, u32[]{:S(2)}, u32[]{:S(2)}) collective-permute-start(f32[1,8,512]{2,1,0:T(8,128)S(1)} %get-tuple-element.121), channel_id=1, source_target_pairs={{32,0},{64,32},{96,64},{128,96},{160,128},{192,160},{224,192},{33,... | collective-permute-start | bytes 49160 | tf_op jit(solution)/shard_map/ppermute | solution.py:25
  26.7 63.3 %copy-start = (s32[4]{0:T(128)S(1)}, s32[4]{0:T(128)}, u32[]{:S(2)}) copy-start(s32[4]{0:T(128)} %param.18) | copy-start | bytes 52
  26.7 63.3 %copy-start.1 = (f32[4,512]{1,0:T(4,128)S(1)}, f32[4,512]{1,0:T(4,128)}, u32[]{:S(2)}) copy-start(f32[4,512]{1,0:T(4,128)} %param.17) | copy-start | bytes 24580
  26.7 63.3 %copy-start.2 = (f32[48]{0:T(128)S(1)}, f32[48]{0:T(128)}, u32[]{:S(2)}) copy-start(f32[48]{0:T(128)} %constant.54.clone.1) | copy-start | bytes 580
  93.2 18.1 %all-to-all-start.1 = ((f32[32,1,9,512]{3,1,2,0:T(1,128)}), f32[32,1,9,512]{3,1,2,0:T(1,128)S(1)}, u32[]{:S(2)}, u32[]{:S(2)}) async-start(f32[32,1,9,512]{3,1,2,0:T(1,128)} %copy.62), calls=%async_computation.1 | async-start | bytes 1179648 | tf_op jit(solution)/shard_map/all_to_all | solution.py:167
  99.6 11.8 %collective-permute-start.2 = (f32[1,9,512]{2,1,0:T(8,128)S(1)}, f32[1,9,512]{2,1,0:T(8,128)S(1)}, u32[]{:S(2)}, u32[]{:S(2)}) collective-permute-start(f32[1,9,512]{2,1,0:T(8,128)S(1)} %get-tuple-element.118), channel_id=1, source_target_pairs={{0,32},{32,64},{64,96},{96,128},{128,160},{160,192},{192,224},{1,3... | collective-permute-start | bytes 55304 | tf_op jit(solution)/shard_map/ppermute | solution.py:23
  103.7 7.7 %collective-permute-start.3 = (f32[1,9,512]{2,1,0:T(8,128)S(1)}, f32[1,9,512]{2,1,0:T(8,128)S(1)}, u32[]{:S(2)}, u32[]{:S(2)}) collective-permute-start(f32[1,9,512]{2,1,0:T(8,128)S(1)} %get-tuple-element.119), channel_id=1, source_target_pairs={{32,0},{64,32},{96,64},{128,96},{160,128},{192,160},{224,192},{33,... | collective-permute-start | bytes 55304 | tf_op jit(solution)/shard_map/ppermute | solution.py:25
where the time goes:
time: 363 us; the launch traced here: 360 us
  other arithmetic  299 us (82%)
  local copies, waits for them, and re-layouts  26.4 us (7%)
  starting transfers between devices  24.7 us (7%)
  waiting for transfers between devices  6 us (2%)
    reduce_sum x12, other arithmetic, force_tile(): heating = target[8] * jnp.sum(weighted * closing, axis=1)  121 us
    reduce_sum x12, other arithmetic, force_tile(): accel_x = -jnp.sum(coupled * apart_x, axis=1)  112 us
    reduce_sum x12, other arithmetic, density_tile(): return jnp.sum(kernel_value * source[6][None, :], axis=1)  60.7 us
    squeeze x12, local copies, waits for them, and re-layouts, run_tiles(): lax.map(lambda block_pair: jax.vmap(worker)(block_pair[0], block_pair[1])...  10.8 us
    all_to_all x1, starting transfers between devices, on_device(): lax.all_to_all(payload, 'cell', split_axis=0, concat_axis=0, tiled=True)  8.59 us
    ppermute x2, starting transfers between devices, extended(): lax.ppermute(tail, axis, [(i, (i + 1) % count) for i in range(ends)])  7.68 us
  transfers between devices with their start and end apart: 6, of which 2 were waited for; matrix products, arithmetic and copies ran while one was open for 2% of the time, Pallas kernels for 0%

commit v1 on v0

v1 whole, which is shorter than its diff:
```python
import math
import jax
import jax.numpy as jnp
from jax import lax
from jax.experimental import pallas as pl
from jax.experimental.pallas import tpu as pltpu
from jax.sharding import PartitionSpec as P

GAMMA = 5.0 / 3.0
F32, BF16 = jnp.float32, jnp.bfloat16
U = 3
NSLOT = 38
OWN = 34
MAXT = 46
GBLK = MAXT * 16 + 20 + 6 * U
ROOT = math.sqrt(24.0 / math.pi)


def halves(v):
    hi = v.astype(BF16).astype(F32)
    return hi, v - hi


def thirds(v):
    first, rest = halves(v)
    second, third = halves(rest)
    return first, second, third


def nt(a, b):
    return lax.dot_general(a, b, (((1,), (1,)), ((), ())), preferred_element_type=F32)


def nn(a, b):
    return lax.dot_general(a, b, (((1,), (0,)), ((), ())), preferred_element_type=F32)


def compute_kernel(n_ref, send_ref, pair_ref, edge_ref, table, energy, rho_out, acc_out, er_out, t_out,
                   ta, ts, feat_s, rows_s, lane_s, feat_o, s_o, near_a, near_b, gst, acc_g, acc_w, q_rows):
    row = lax.broadcasted_iota(jnp.int32, (8, 512), 0)

    def blocks(s):
        return (n_ref[s] + 127) >> 7

    def add(count, a, s):
        ta[count] = a
        ts[count] = s
        return count + (n_ref[s] > 0).astype(jnp.int32)
    for k in range(4):
        ta[k] = k
        ts[k] = OWN + k
    for k in range(4):
        a, b = pair_ref[2 * k], pair_ref[2 * k + 1]
        ta[4 + 2 * k] = a
        ts[4 + 2 * k] = OWN + b
        ta[5 + 2 * k] = b
        ts[5 + 2 * k] = OWN + a
    count = lax.fori_loop(0, 32, lambda s, cnt: add(cnt, jnp.maximum(send_ref[s], 0), s), jnp.int32(12))
    count = add(count, edge_ref[0], jnp.int32(32))
    count = add(count, edge_ref[1], jnp.int32(33))
    ta[count] = 0
    ts[count] = OWN
    total = lax.fori_loop(0, count, lambda k, v: v + blocks(OWN + ta[k]) * blocks(ts[k]), jnp.int32(0))

    def source(s):
        st = table[s]
        x = st[1:2]
        y = st[2:3]
        z = st[3:4]
        sq = x * x + y * y + z * z
        hinv = 1.0 / st[7:8]
        sj = ROOT * hinv * hinv
        tj = sj * hinv
        f = jnp.where(row == 0, sq, jnp.where(row <= 3, st, jnp.where(row == 4, 1.0, jnp.where(row == 5, tj, 0.0))))
        f1, f2, f3 = thirds(f)
        feats = jnp.concatenate([f1, f1, f2, f2, f1, f3], axis=0)
        five = lax.broadcasted_iota(jnp.int32, (48, 512), 0) % 8 == 5
        near = jnp.where(five, 0.0, feats).astype(BF16)
        ratio = jnp.where(five, feats, 0.0).astype(BF16)
        vx = x * st[4:5] + y * st[5:6] + z * st[6:7]
        r = jnp.where(row == 0, 1.0, jnp.where(row == 7, vx, st)) * st[0:1]
        r1, r2 = halves(r)
        rows = jnp.concatenate([r1, r2], axis=0).astype(BF16)
        lane = jnp.where(row == 0, sj, st[0:1])
        for jb in range(4):
            cut = slice(jb * 128, (jb + 1) * 128)
            feat_s[s * 4 + jb, :, 0:128] = near[:, cut]
            feat_s[s * 4 + jb, :, 128:256] = ratio[:, cut]
            rows_s[s * 4 + jb, :, 0:128] = rows[:, cut]
            rows_s[s * 4 + jb, :, 128:256] = rows[:, cut]
            lane_s[s * 4 + jb] = lane[:, cut]

    def source_loop(g, _):
        source(2 * g)
        source(2 * g + 1)
        return 0
    lax.fori_loop(0, NSLOT // 2, source_loop, 0)

    eye = (lax.broadcasted_iota(jnp.int32, (128, 128), 0) == lax.broadcasted_iota(jnp.int32, (128, 128), 1))
    eye = eye.astype(F32).astype(BF16)
    pick = (lax.broadcasted_iota(jnp.int32, (64, 128), 0) >= 48).astype(F32).astype(BF16)
    for a in range(4):
        st = table[OWN + a]
        x = st[1:2]
        y = st[2:3]
        z = st[3:4]
        sq = x * x + y * y + z * z
        h = st[7:8]
        hinv = 1.0 / h
        si = ROOT * hinv * hinv
        tt = si * si * hinv * hinv
        f = jnp.where(row == 0, 1.0, jnp.where(row <= 3, -2.0 * st, jnp.where(row == 4, sq, 0.0)))
        f = jnp.where(row == 5, h * h * h * (1.0 / ROOT), f * tt)
        f1, f2, f3 = thirds(f)
        s1, s2, s3 = thirds(si)
        s_rows = jnp.where(row == 0, s1, jnp.where(row == 1, s2, jnp.where(row == 2, s3, 0.0)))
        whole = jnp.concatenate([f1, f2, f1, f2, f3, f1, s_rows, jnp.zeros((8, 512), F32)], axis=0).astype(BF16)
        for ib in range(4):
            part = nt(eye, whole[:, ib * 128:(ib + 1) * 128]).astype(BF16)
            feat_o[a * 4 + ib] = part[:, :48]
            s_o[a * 4 + ib] = nn(part, pick)

    acc_g[...] = jnp.zeros_like(acc_g)
    acc_w[...] = jnp.zeros_like(acc_w)
    for u in range(U):
        gst[u] = jnp.zeros((128, 256), BF16)

    def at(tile):
        a, s = ta[tile], ts[tile]
        return a, s, blocks(OWN + a), blocks(s)

    def advance(state):
        tile, ib, jb, a, s, ni, nj = state
        ib = ib + 1
        wrap_i = ib >= ni
        ib = jnp.where(wrap_i, 0, ib)
        jb = jnp.where(wrap_i, jb + 1, jb)
        wrap_j = jb >= nj
        jb = jnp.where(wrap_j, 0, jb)
        tile = jnp.where(wrap_j, jnp.minimum(tile + 1, count), tile)
        return (tile, ib, jb) + at(tile)

    def group(state):
        out = []
        for _ in range(U):
            out.append((state[3] * 4 + state[1], state[4] * 4 + state[2]))
            state = advance(state)
        return state, tuple(out)

    def distances(buf, where):
        for u in range(U):
            buf[u] = nn(feat_o[where[u][0]], feat_s[where[u][1]])

    def elements(buf, where, base):
        for u in range(U):
            oi, sj_ = where[u]
            live = (base + u < total).astype(F32)
            sj = lane_s[sj_][0:1]
            mass = lane_s[sj_][1:2] * live
            d2 = jnp.maximum(buf[u, :, 0:128], 1e-6)
            inv = lax.rsqrt(d2)
            pi = d2 * inv
            pj = pi * buf[u, :, 128:256]
            ai = jnp.maximum(s_o[oi] - pi, 0.0)
            ci = jnp.maximum(ai - pi, 0.0)
            qa = ai * ai
            qc = ci * ci
            acc_w[oi] += ((ai + ai) * qa - qc * ci) * mass
            aj = jnp.maximum(sj - pj, 0.0)
            mj = jnp.minimum(pj, aj)
            g = (qa - qc + mj * (aj + aj - mj)) * inv
            hi = g.astype(BF16)
            gst[base + U + u, :, 0:128] = hi
            gst[base + U + u, :, 128:256] = (g - hi.astype(F32)).astype(BF16)

    def products(where, base):
        return [nt(rows_s[where[u][1]], gst[base + U + u]) for u in range(U)]

    def collect(sums, where, base):
        for u in range(U):
            acc_g[where[u][0]] += jnp.where(base + u < total, sums[u], 0.0)

    zero = jnp.int32(0)
    walk, first = group((zero, zero, zero) + at(zero))
    walk, second = group(walk)
    distances(near_a, first)

    def body(n, carry):
        walk, prev, now, later = carry
        base = n * (2 * U)
        sums = products(prev, base - U)
        elements(near_a, now, base)
        distances(near_b, later)
        collect(sums, prev, base - U)
        walk, after = group(walk)
        sums = products(now, base)
        elements(near_b, later, base + U)
        distances(near_a, after)
        collect(sums, now, base)
        walk, last = group(walk)
        return walk, later, after, last

    steps = (total + 2 * U - 1) // (2 * U)
    lax.fori_loop(0, steps + 1, body, (walk, first, first, second))

    def clear(k, _):
        gst[(2 * steps + 3) * U + k] = jnp.zeros((128, 256), BF16)
        return 0
    lax.fori_loop(0, 17, clear, 0)

    lane_id = lax.broadcasted_iota(jnp.int32, (1, 512), 1)
    for a in range(4):
        st = table[OWN + a]
        h = st[7:8]
        h3 = h * h * h
        ti = ROOT / h3
        sums = jnp.concatenate([acc_g[a * 4 + ib] for ib in range(4)], axis=1)
        sums = (sums[:8] + sums[8:]) * ti
        wsum = jnp.concatenate([jnp.sum(acc_w[a * 4 + ib].T, axis=0, keepdims=True) for ib in range(4)], axis=1)
        rho = wsum * (h3 * (8.0 / math.pi / ROOT ** 3))
        live = lane_id < n_ref[OWN + a]
        press = jnp.where(live, (GAMMA - 1.0) * energy[a:a + 1] / jnp.where(live, rho, 1.0), 0.0)
        rho_out[a:a + 1] = jnp.where(live, rho, 0.0)
        dx = [st[1 + k:2 + k] * sums[0:1] - sums[1 + k:2 + k] for k in range(3)]
        heat = sums[7:8]
        for k in range(3):
            heat = heat + st[4 + k:5 + k] * dx[k] - st[1 + k:2 + k] * sums[4 + k:5 + k]
            acc_out[k, a:a + 1] = jnp.where(live, press * dx[k], 0.0)
        er_out[a:a + 1] = jnp.where(live, -press * heat, 0.0)
        q = jnp.where(row == 0, 1.0, jnp.where(row <= 3, st, 0.0)) * (st[0:1] * press * ti)
        q1, q2 = halves(q)
        q_rows[a] = jnp.concatenate([q1, q2], axis=0).astype(BF16)

    t_out[...] = jnp.zeros_like(t_out)

    def mirror(tile, base):
        a, s, ni, nj = at(tile)
        q = q_rows[a]
        st = table[s]
        for jb in range(4):
            first = base + jb * ni
            g = gst[pl.ds(first, 4)].reshape(512, 256)
            o = nn(q, g)
            o = o[:8] + o[8:]
            o = o[:, :128] + o[:, 128:]
            cut = slice(jb * 128, (jb + 1) * 128)
            add_ = st[:, cut] * o[0:1] - o
            t_out[s, :, cut] += add_[0:4]
        return base + ni * nj
    lax.fori_loop(0, count, mirror, jnp.int32(U))

    for a in range(4):
        live = lane_id < n_ref[OWN + a]
        for k in range(3):
            acc_out[k, a:a + 1] += jnp.where(live, t_out[OWN + a, 1 + k:2 + k], 0.0)


def compute(counts, send, pairs, edge, table, energy):
    smem = pl.BlockSpec(memory_space=pltpu.SMEM)
    vmem = pl.BlockSpec(memory_space=pltpu.VMEM)
    return pl.pallas_call(
        compute_kernel,
        out_shape=(
            jax.ShapeDtypeStruct((4, 512), F32),
            jax.ShapeDtypeStruct((3, 4, 512), F32),
            jax.ShapeDtypeStruct((4, 512), F32),
            jax.ShapeDtypeStruct((NSLOT, 4, 512), F32),
        ),
        in_specs=[smem] * 4 + [vmem] * 2,
        out_specs=(vmem,) * 4,
        scratch_shapes=[
            pltpu.SMEM((MAXT + 2,), jnp.int32),
            pltpu.SMEM((MAXT + 2,), jnp.int32),
            pltpu.VMEM((NSLOT * 4, 48, 256), BF16),
            pltpu.VMEM((NSLOT * 4, 16, 256), BF16),
            pltpu.VMEM((NSLOT * 4, 8, 128), F32),
            pltpu.VMEM((16, 128, 48), BF16),
            pltpu.VMEM((16, 128, 128), F32),
            pltpu.VMEM((U, 128, 256), F32),
            pltpu.VMEM((U, 128, 256), F32),
            pltpu.VMEM((GBLK, 128, 256), BF16),
            pltpu.VMEM((16, 16, 128), F32),
            pltpu.VMEM((16, 128, 128), F32),
            pltpu.VMEM((4, 16, 512), BF16),
        ],
        compiler_params=pltpu.CompilerParams(vmem_limit_bytes=63 * 1024 * 1024),
        name="tiles",
    )(counts, send, pairs, edge, table, energy)


def shifted(down, up):
    count = lax.axis_size("region")
    from_lower = lax.ppermute(up, "region", [(i, i + 1) for i in range(count - 1)])
    from_upper = lax.ppermute(down, "region", [(i + 1, i) for i in range(count - 1)])
    return from_lower, from_upper


def on_device(
    positions, velocities, mass, smoothing, energy, counts, send_cells, local_pairs, edge_cells
):
    slot_ids = lax.broadcasted_iota(jnp.int32, (4, 512), 1)
    occupied = slot_ids < counts[:, None]
    rows = jnp.concatenate(
        [
            jnp.where(occupied, mass, 0.0)[:, None],
            jnp.transpose(positions, (1, 0, 2)) - 0.5,
            jnp.transpose(velocities, (1, 0, 2)),
            smoothing[:, None],
        ],
        axis=1,
    )
    send = send_cells[0, 0, :, 0]
    edge = edge_cells[0, 0]
    payload = jnp.where((send >= 0)[:, None, None], rows[jnp.maximum(send, 0)], 0.0)
    received = lax.all_to_all(payload, "cell", split_axis=0, concat_axis=0, tiled=True)
    lower, upper = shifted(rows[edge[0]], rows[edge[1]])
    table = jnp.concatenate([received, lower[None], upper[None], rows], axis=0)
    n = jnp.sum((table[:, 0] > 0.0).astype(jnp.int32), axis=1)
    density, accel, heat, back = compute(n, send, local_pairs[0, 0].reshape(8), edge, table, energy)
    returned = lax.all_to_all(back[:32], "cell", split_axis=0, concat_axis=0, tiled=True)
    lower, upper = shifted(back[32], back[33])
    whole = jnp.concatenate([returned, lower[None], upper[None]], axis=0)
    target = jnp.concatenate([send, edge])
    own = jnp.arange(4, dtype=jnp.int32)
    hit = (target[None, :] == own[:, None]).astype(jnp.float32)
    extra = jnp.sum(hit[:, :, None, None] * whole[None, :, 1:4], axis=1)
    extra = jnp.where(occupied[None], jnp.transpose(extra, (1, 0, 2)), 0.0)
    return density, accel + extra, heat


def solution(mesh):
    placed = (
        P(None, ("region", "cell"), None),
        P(None, ("region", "cell"), None),
        P(("region", "cell"), None),
        P(("region", "cell"), None),
        P(("region", "cell"), None),
        P(("region", "cell")),
        P("region", "cell", None, None),
        P("region", "cell", None, None),
        P("region", "cell", None),
    )
    return jax.shard_map(
        on_device,
        mesh=mesh,
        in_specs=placed,
        out_specs=(
            P(("region", "cell"), None),
            P(None, ("region", "cell"), None),
            P(("region", "cell"), None),
        ),
        check_vma=False,
    )
```

time: 363 us -> 98 us (0.27)
  other arithmetic: 299 us -> 5.02 us
  Pallas kernels: 0 us -> 39.5 us
  local copies, waits for them, and re-layouts: 26.4 us -> 5.42 us
  starting transfers between devices: 24.7 us -> 33 us
  between operations: 1.05 us -> 4.72 us
    reduce_sum x36 -> x2, other arithmetic: 293 us -> 1.54 us  [the longest x1 1.31 us: on_device(): n = jnp.sum((table[:, 0] > 0.0).astype(jnp.int32), axis=1)]
    pallas_call x0 -> x1, Pallas kernels: none -> 39.5 us  [compute(): pl.pallas_call(compute_kernel, out_shape=(jax.ShapeDtypeStruct((4, 512),...]
    squeeze x13 -> x2, local copies, waits for them, and re-layouts: 10.8 us -> 0.73 us  [the longest x1 0.72 us: on_device(): lower, upper = shifted(back[32], back[33])]
    ppermute x4, waiting for transfers between devices: 0.01 us -> 9.31 us  [the longest x2 9.3 us: shifted(): lax.ppermute(down, 'region', [(i + 1, i) for i in range(count - 1)])]
    all_to_all x1, starting transfers between devices: 5.84 us -> 12.8 us  [on_device(): lax.all_to_all(back[:32], 'cell', split_axis=0, concat_axis=0, tiled=True)]
    gather x8 -> x1, local copies, waits for them, and re-layouts: 4.82 us -> 0.59 us  [on_device(): rows[jnp.maximum(send, 0)]]
    all_to_all x1, waiting for transfers between devices: 4.03 us -> 0.01 us  [on_device(): lax.all_to_all(back[:32], 'cell', split_axis=0, concat_axis=0, tiled=True)]
where the time goes in v1:
time: 98 us; the launch traced here: 96.9 us
  Pallas kernels  39.5 us (40%)
  starting transfers between devices  33 us (34%)
  waiting for transfers between devices  9.31 us (10%)
  local copies, waits for them, and re-layouts  5.42 us (6%)
  other arithmetic  5.02 us (5%)
  between operations  4.72 us (5%)
    pallas_call x1, Pallas kernels, compute(): pl.pallas_call(compute_kernel, out_shape=(jax.ShapeDtypeStruct((4, 512),...  39.5 us
    all_to_all x1, starting transfers between devices, on_device(): lax.all_to_all(back[:32], 'cell', split_axis=0, concat_axis=0, tiled=True)  12.8 us
    ppermute x2, waiting for transfers between devices, shifted(): lax.ppermute(down, 'region', [(i + 1, i) for i in range(count - 1)])  9.3 us
    ppermute x2, starting transfers between devices, shifted(): lax.ppermute(up, 'region', [(i, i + 1) for i in range(count - 1)])  8.8 us
    all_to_all x1, starting transfers between devices, on_device(): lax.all_to_all(payload, 'cell', split_axis=0, concat_axis=0, tiled=True)  8.72 us
    ppermute x2, starting transfers between devices, shifted(): lax.ppermute(down, 'region', [(i + 1, i) for i in range(count - 1)])  2.58 us
  transfers between devices with their start and end apart: 6, of which 2 were waited for; matrix products, arithmetic and copies ran while one was open for 2% of the time, Pallas kernels for 0%

profile of v1, /device:TPU:1, one launch (start us, length us, event | category | flops | bytes accessed | tf_op | source)
XLA Modules:
  0.0 96.9 jit_solution(10875974310567034567)
XLA Ops:
  0.6 0.0 copy-start.8
  0.6 0.0 copy-start.4
  0.7 0.7 maximum_bitcast_fusion
  1.4 0.0 copy-done.8
  1.4 0.0 copy-start.1
  1.4 0.0 copy-start.2
  1.4 0.8 broadcast_select_fusion.1
  2.2 0.0 copy-done.4
  2.2 0.0 copy-done.1
  2.2 0.0 copy-done.2
  2.3 0.6 gather_fusion
  2.9 0.9 broadcast_select_fusion
  3.8 0.0 copy-start.5
  3.8 8.7 %all-to-all-start = ((f32[32,8,512]{2,1,0:T(8,128)}), f32[32,8,512]{2,1,0:T(8,128)S(1)}, u32[]{:S(2)}, u32[]{:S(2)}) async-start(f32[32,8,512]{2,1,0:T(8,128)} %broadcast_select_fusion), calls=%async_computation | async-start | bytes 1048576 | tf_op jit(solution)/shard_map/all_to_all | solution.py:315
  12.6 0.0 copy-done.5
  12.6 0.6 fusion.3
  17.0 3.5 %collective-permute-start = (f32[8,512]{1,0:T(8,128)S(1)}, f32[8,512]{1,0:T(8,128)S(1)}, u32[]{:S(2)}, u32[]{:S(2)}) collective-permute-start(f32[8,512]{1,0:T(8,128)S(1)} %get-tuple-element.13), channel_id=1, source_target_pairs={{0,32},{32,64},{64,96},{96,128},{128,160},{160,192},{192,224},{1,3... | collective-permute-start | bytes 49160 | tf_op jit(solution)/shard_map/ppermute | solution.py:293
  20.6 1.3 %collective-permute-start.1 = (f32[8,512]{1,0:T(8,128)S(1)}, f32[8,512]{1,0:T(8,128)S(1)}, u32[]{:S(2)}, u32[]{:S(2)}) collective-permute-start(f32[8,512]{1,0:T(8,128)S(1)} %get-tuple-element.14), channel_id=1, source_target_pairs={{32,0},{64,32},{96,64},{128,96},{160,128},{192,160},{224,192},{33,... | collective-permute-start | bytes 49160 | tf_op jit(solution)/shard_map/ppermute | solution.py:294
  21.9 0.1 pad_add_fusion
  22.0 0.0 copy-start.7
  22.0 0.1 fusion.2
  22.1 0.6 copy-done.7
  22.7 0.1 copy.24
  22.7 0.6 reshape_squeeze.3.pair_ref
  23.4 0.0 collective-permute-done
  23.4 1.9 %collective-permute-done.1 = f32[8,512]{1,0:T(8,128)S(1)} collective-permute-done((f32[8,512]{1,0:T(8,128)S(1)}, f32[8,512]{1,0:T(8,128)S(1)}, u32[]{:S(2)}, u32[]{:S(2)}) %collective-permute-start.1) | collective-permute-done | bytes 16416 | tf_op jit(solution)/shard_map/ppermute | solution.py:294
  25.3 0.0 all-to-all-done
  25.3 0.1 maximum_maximum_fusion.table
  25.3 0.0 copy-start
  25.4 1.3 %fusion.n_ref = s32[38]{0:T(128)} fusion(f32[38,8,512]{2,1,0:T(8,128)S(1)} %maximum_maximum_fusion.table), kind=kLoop, calls=%fused_computation.7 | loop fusion | flops 58330 | bytes 77976 | tf_op jit(solution)/shard_map/reduce_sum | solution.py:318
  26.7 0.0 copy-done
  26.7 39.5 %tiles.1 = (f32[4,512]{1,0:T(4,128)}, f32[3,4,512]{2,1,0:T(4,128)}, f32[4,512]{1,0:T(4,128)}, f32[38,4,512]{2,1,0:T(4,128)}) custom-call(s32[38]{0:T(128)} %fusion.n_ref, s32[32]{0:T(128)} %bitcast.31, s32[8]{0:T(128)} %reshape_squeeze.3.pair_ref, s32[2]{0:T(128)} %bitcast.29, f32[38,8,512]{2,1,0:T(8,128)} %copy-done, f32[4,512]{1,0:T(4,128)} %energy.1), custom_call_target="tpu_custom_call" | custom-call | tf_op jit(solution)/shard_map/tiles/pallas_call | solution.py:261
  66.2 1.7 %slice.26 = f32[32,4,512]{2,1,0:T(4,128)} slice(f32[38,4,512]{2,1,0:T(4,128)} %get-tuple-element.9), slice={[0:32], [0:4], [0:512]} | slice | bytes 524288 | tf_op jit(solution)/shard_map/slice | solution.py:320
  67.8 12.8 %all-to-all-start.1 = ((f32[32,4,512]{2,1,0:T(4,128)}), f32[32,4,512]{2,1,0:T(4,128)S(1)}, u32[]{:S(2)}, u32[]{:S(2)}) async-start(f32[32,4,512]{2,1,0:T(4,128)} %slice.26), calls=%async_computation.1 | async-start | bytes 524288 | tf_op jit(solution)/shard_map/all_to_all | solution.py:320
  80.7 0.7 slice_bitcast_fusion.1
  81.4 0.0 copy-start.6
  81.4 5.3 %collective-permute-start.2 = (f32[4,512]{1,0:T(4,128)S(1)}, f32[4,512]{1,0:T(4,128)S(1)}, u32[]{:S(2)}, u32[]{:S(2)}) collective-permute-start(f32[4,512]{1,0:T(4,128)S(1)} %get-tuple-element.11), channel_id=1, source_target_pairs={{0,32},{32,64},{64,96},{96,128},{128,160},{160,192},{192,224},{1,3... | collective-permute-start | bytes 24584 | tf_op jit(solution)/shard_map/ppermute | solution.py:293
  86.7 1.3 %collective-permute-start.3 = (f32[4,512]{1,0:T(4,128)S(1)}, f32[4,512]{1,0:T(4,128)S(1)}, u32[]{:S(2)}, u32[]{:S(2)}) collective-permute-start(f32[4,512]{1,0:T(4,128)S(1)} %get-tuple-element.12), channel_id=1, source_target_pairs={{32,0},{64,32},{96,64},{128,96},{160,128},{192,160},{224,192},{33,... | collective-permute-start | bytes 24584 | tf_op jit(solution)/shard_map/ppermute | solution.py:294
  88.0 0.0 copy-done.6
  88.0 0.1 iota_compare_fusion.1
  88.0 0.0 collective-permute-done.2
  88.1 7.4 %collective-permute-done.3 = f32[4,512]{1,0:T(4,128)S(1)} collective-permute-done((f32[4,512]{1,0:T(4,128)S(1)}, f32[4,512]{1,0:T(4,128)S(1)}, u32[]{:S(2)}, u32[]{:S(2)}) %collective-permute-start.3) | collective-permute-done | bytes 8224 | tf_op jit(solution)/shard_map/ppermute | solution.py:294
  95.5 0.0 all-to-all-done.1
  95.5 0.1 pad_maximum_fusion
  95.6 0.0 copy-start.3
  95.6 0.2 multiply_reduce_fusion
  95.8 0.5 copy-done.3
  96.3 0.6 bitcast_add_fusion
  (7 shorter events, 0.1 us)
Async XLA Ops:
  0.6 0.7 copy-start.8
  0.6 1.5 %copy-start.4 = (f32[4,512]{1,0:T(4,128)S(1)}, f32[4,512]{1,0:T(4,128)}, u32[]{:S(2)}) copy-start(f32[4,512]{1,0:T(4,128)} %param.12) | copy-start | bytes 24580
  1.4 0.9 copy-start.1
  1.4 0.9 copy-start.2
  3.8 8.7 %copy-start.5 = (s32[1,1,2]{2,1,0:T(1,128)S(1)}, s32[1,1,2]{2,1,0:T(1,128)}, u32[]{:S(2)}) copy-start(s32[1,1,2]{2,1,0:T(1,128)} %param.17) | copy-start | bytes 28
  3.8 21.4 %all-to-all-start = ((f32[32,8,512]{2,1,0:T(8,128)}), f32[32,8,512]{2,1,0:T(8,128)S(1)}, u32[]{:S(2)}, u32[]{:S(2)}) async-start(f32[32,8,512]{2,1,0:T(8,128)} %broadcast_select_fusion), calls=%async_computation | async-start | bytes 1048576 | tf_op jit(solution)/shard_map/all_to_all | solution.py:315
  17.0 6.3 %collective-permute-start = (f32[8,512]{1,0:T(8,128)S(1)}, f32[8,512]{1,0:T(8,128)S(1)}, u32[]{:S(2)}, u32[]{:S(2)}) collective-permute-start(f32[8,512]{1,0:T(8,128)S(1)} %get-tuple-element.13), channel_id=1, source_target_pairs={{0,32},{32,64},{64,96},{96,128},{128,160},{160,192},{192,224},{1,3... | collective-permute-start | bytes 49160 | tf_op jit(solution)/shard_map/ppermute | solution.py:293
  20.6 4.7 %collective-permute-start.1 = (f32[8,512]{1,0:T(8,128)S(1)}, f32[8,512]{1,0:T(8,128)S(1)}, u32[]{:S(2)}, u32[]{:S(2)}) collective-permute-start(f32[8,512]{1,0:T(8,128)S(1)} %get-tuple-element.14), channel_id=1, source_target_pairs={{32,0},{64,32},{96,64},{128,96},{160,128},{192,160},{224,192},{33,... | collective-permute-start | bytes 49160 | tf_op jit(solution)/shard_map/ppermute | solution.py:294
  22.0 0.7 copy-start.7
  25.3 1.3 %copy-start = (f32[38,8,512]{2,1,0:T(8,128)}, f32[38,8,512]{2,1,0:T(8,128)S(1)}, u32[]{:S(2)}) copy-start(f32[38,8,512]{2,1,0:T(8,128)S(1)} %maximum_maximum_fusion.table) | copy-start | bytes 1867780
  67.8 27.6 %all-to-all-start.1 = ((f32[32,4,512]{2,1,0:T(4,128)}), f32[32,4,512]{2,1,0:T(4,128)S(1)}, u32[]{:S(2)}, u32[]{:S(2)}) async-start(f32[32,4,512]{2,1,0:T(4,128)} %slice.26), calls=%async_computation.1 | async-start | bytes 524288 | tf_op jit(solution)/shard_map/all_to_all | solution.py:320
  81.4 6.6 %copy-start.6 = (s32[4]{0:T(128)S(1)}, s32[4]{0:T(128)}, u32[]{:S(2)}) copy-start(s32[4]{0:T(128)} %param.14) | copy-start | bytes 52
  81.4 6.7 %collective-permute-start.2 = (f32[4,512]{1,0:T(4,128)S(1)}, f32[4,512]{1,0:T(4,128)S(1)}, u32[]{:S(2)}, u32[]{:S(2)}) collective-permute-start(f32[4,512]{1,0:T(4,128)S(1)} %get-tuple-element.11), channel_id=1, source_target_pairs={{0,32},{32,64},{64,96},{96,128},{128,160},{160,192},{192,224},{1,3... | collective-permute-start | bytes 24584 | tf_op jit(solution)/shard_map/ppermute | solution.py:293
  86.7 8.8 %collective-permute-start.3 = (f32[4,512]{1,0:T(4,128)S(1)}, f32[4,512]{1,0:T(4,128)S(1)}, u32[]{:S(2)}, u32[]{:S(2)}) collective-permute-start(f32[4,512]{1,0:T(4,128)S(1)} %get-tuple-element.12), channel_id=1, source_target_pairs={{32,0},{64,32},{96,64},{128,96},{160,128},{192,160},{224,192},{33,... | collective-permute-start | bytes 24584 | tf_op jit(solution)/shard_map/ppermute | solution.py:294
  95.6 0.7 copy-start.3

commit v2 on v1

--- a/solution.py
+++ b/solution.py
@@ -35,32 +35,17 @@
     return lax.dot_general(a, b, (((1,), (0,)), ((), ())), preferred_element_type=F32)
 
 
-def compute_kernel(n_ref, send_ref, pair_ref, edge_ref, table, energy, rho_out, acc_out, er_out, t_out,
-                   ta, ts, feat_s, rows_s, lane_s, feat_o, s_o, near_a, near_b, gst, acc_g, acc_w, q_rows):
+def compute_kernel(send_ref, pair_ref, edge_ref, table, energy, rho_out, acc_out, er_out, t_out,
+                   ta, ts, feat_s, rows_s, lane_s, feat_o, s_o, near_a, near_b, gst, acc_g, acc_w, q_rows,
+                   cnt_v, n_ref, cnt_sem):
+    found = jnp.sum((table[:, 0, :] > 0.0).astype(F32), axis=1, keepdims=True)
+    cnt_v[...] = jnp.broadcast_to(found, (NSLOT, 128)).astype(jnp.int32)
+    fetch = pltpu.make_async_copy(cnt_v, n_ref, cnt_sem)
+    fetch.start()
     row = lax.broadcasted_iota(jnp.int32, (8, 512), 0)
 
     def blocks(s):
-        return (n_ref[s] + 127) >> 7
-
-    def add(count, a, s):
-        ta[count] = a
-        ts[count] = s
-        return count + (n_ref[s] > 0).astype(jnp.int32)
-    for k in range(4):
-        ta[k] = k
-        ts[k] = OWN + k
-    for k in range(4):
-        a, b = pair_ref[2 * k], pair_ref[2 * k + 1]
-        ta[4 + 2 * k] = a
-        ts[4 + 2 * k] = OWN + b
-        ta[5 + 2 * k] = b
-        ts[5 + 2 * k] = OWN + a
-    count = lax.fori_loop(0, 32, lambda s, cnt: add(cnt, jnp.maximum(send_ref[s], 0), s), jnp.int32(12))
-    count = add(count, edge_ref[0], jnp.int32(32))
-    count = add(count, edge_ref[1], jnp.int32(33))
-    ta[count] = 0
-    ts[count] = OWN
-    total = lax.fori_loop(0, count, lambda k, v: v + blocks(OWN + ta[k]) * blocks(ts[k]), jnp.int32(0))
+        return (n_ref[s, 0] + 127) >> 7
 
     def source(s):
         st = table[s]
@@ -95,6 +80,28 @@
         source(2 * g + 1)
         return 0
     lax.fori_loop(0, NSLOT // 2, source_loop, 0)
+    fetch.wait()
+
+    def add(count, a, s):
+        ta[count] = a
+        ts[count] = s
+        return count + (n_ref[s, 0] > 0).astype(jnp.int32)
+    for k in range(4):
+        ta[k] = k
+        ts[k] = OWN + k
+    for k in range(4):
+        a, b = pair_ref[2 * k], pair_ref[2 * k + 1]
+        ta[4 + 2 * k] = a
+        ts[4 + 2 * k] = OWN + b
+        ta[5 + 2 * k] = b
+        ts[5 + 2 * k] = OWN + a
+    count = lax.fori_loop(0, 32, lambda s, cnt: add(cnt, jnp.maximum(send_ref[s], 0), s), jnp.int32(12))
+    count = add(count, edge_ref[0], jnp.int32(32))
+    count = add(count, edge_ref[1], jnp.int32(33))
+    ta[count] = 0
+    ts[count] = OWN
+    total = lax.fori_loop(0, count, lambda k, v: v + blocks(OWN + ta[k]) * blocks(ts[k]), jnp.int32(0))
+
 
     eye = (lax.broadcasted_iota(jnp.int32, (128, 128), 0) == lax.broadcasted_iota(jnp.int32, (128, 128), 1))
     eye = eye.astype(F32).astype(BF16)
@@ -218,7 +225,7 @@
         sums = (sums[:8] + sums[8:]) * ti
         wsum = jnp.concatenate([jnp.sum(acc_w[a * 4 + ib].T, axis=0, keepdims=True) for ib in range(4)], axis=1)
         rho = wsum * (h3 * (8.0 / math.pi / ROOT ** 3))
-        live = lane_id < n_ref[OWN + a]
+        live = lane_id < n_ref[OWN + a, 0]
         press = jnp.where(live, (GAMMA - 1.0) * energy[a:a + 1] / jnp.where(live, rho, 1.0), 0.0)
         rho_out[a:a + 1] = jnp.where(live, rho, 0.0)
         dx = [st[1 + k:2 + k] * sums[0:1] - sums[1 + k:2 + k] for k in range(3)]
@@ -250,12 +257,12 @@
     lax.fori_loop(0, count, mirror, jnp.int32(U))
 
     for a in range(4):
-        live = lane_id < n_ref[OWN + a]
+        live = lane_id < n_ref[OWN + a, 0]
         for k in range(3):
             acc_out[k, a:a + 1] += jnp.where(live, t_out[OWN + a, 1 + k:2 + k], 0.0)
 
 
-def compute(counts, send, pairs, edge, table, energy):
+def compute(send, pairs, edge, table, energy):
     smem = pl.BlockSpec(memory_space=pltpu.SMEM)
     vmem = pl.BlockSpec(memory_space=pltpu.VMEM)
     return pl.pallas_call(
@@ -266,7 +273,7 @@
             jax.ShapeDtypeStruct((4, 512), F32),
             jax.ShapeDtypeStruct((NSLOT, 4, 512), F32),
         ),
-        in_specs=[smem] * 4 + [vmem] * 2,
+        in_specs=[smem] * 3 + [vmem] * 2,
         out_specs=(vmem,) * 4,
         scratch_shapes=[
             pltpu.SMEM((MAXT + 2,), jnp.int32),
@@ -282,50 +289,188 @@
             pltpu.VMEM((16, 16, 128), F32),
             pltpu.VMEM((16, 128, 128), F32),
             pltpu.VMEM((4, 16, 512), BF16),
+            pltpu.VMEM((NSLOT, 128), jnp.int32),
+            pltpu.SMEM((NSLOT, 128), jnp.int32),
+            pltpu.SemaphoreType.DMA,
         ],
         compiler_params=pltpu.CompilerParams(vmem_limit_bytes=63 * 1024 * 1024),
         name="tiles",
-    )(counts, send, pairs, edge, table, energy)
-
-
-def shifted(down, up):
+    )(send, pairs, edge, table, energy)
+
+
+MESH = pl.DeviceIdType.MESH
+PEERS = 32
+LOWER, UPPER = 32, 33
+
+
+def place():
+    region, cell = lax.axis_index("region"), lax.axis_index("cell")
     count = lax.axis_size("region")
-    from_lower = lax.ppermute(up, "region", [(i, i + 1) for i in range(count - 1)])
-    from_upper = lax.ppermute(down, "region", [(i + 1, i) for i in range(count - 1)])
-    return from_lower, from_upper
+    return region, cell, lax.rem(region + count - 1, count), lax.rem(region + 1, count)
+
+
+def greet():
+    region, cell, below, above = place()
+    barrier = pltpu.get_barrier_semaphore()
+
+    def one(k, _):
+        peer = lax.rem(cell + k, PEERS)
+        pl.semaphore_signal(barrier, inc=1, device_id=(region, peer), device_id_type=MESH)
+        return 0
+    lax.fori_loop(1, PEERS, one, 0)
+    pl.semaphore_signal(barrier, inc=1, device_id=(below, cell), device_id_type=MESH)
+    pl.semaphore_signal(barrier, inc=1, device_id=(above, cell), device_id_type=MESH)
+    return barrier
+
+
+def remote(src, dst, send_sem, recv_sem, slot, mine, device):
+    return pltpu.make_async_remote_copy(
+        src_ref=src.at[slot],
+        dst_ref=dst.at[mine],
+        send_sem=send_sem.at[slot],
+        recv_sem=recv_sem.at[mine],
+        device_id=device,
+        device_id_type=MESH,
+    )
+
+
+def exchange_kernel(counts, send_ref, edge_ref, positions, velocities, mass, smoothing, table,
+                    own, payload, send_sem, recv_sem, local_sem):
+    region, cell, below, above = place()
+    barrier = greet()
+    lane_id = lax.broadcasted_iota(jnp.int32, (1, 512), 1)
+    for k in range(4):
+        live = lane_id < counts[k]
+        own[k] = jnp.concatenate(
+            [jnp.where(live, mass[k:k + 1], 0.0)]
+            + [positions[i, k:k + 1] - 0.5 for i in range(3)]
+            + [velocities[i, k:k + 1] for i in range(3)]
+            + [smoothing[k:k + 1]],
+            axis=0,
+        )
+        pltpu.make_async_copy(own.at[k], table.at[OWN + k], local_sem.at[k]).start()
+    low = (region > 0).astype(F32)
+    high = (region < lax.axis_size("region") - 1).astype(F32)
+    payload[LOWER] = own[edge_ref[0]] * low
+    payload[UPPER] = own[edge_ref[1]] * high
+    payload[cell] = jnp.zeros((8, 512), F32)
+    pltpu.make_async_copy(payload.at[cell], table.at[cell], local_sem.at[4]).start()
+    pl.semaphore_wait(barrier, PEERS + 1)
+    remote(payload, table, send_sem, recv_sem, LOWER, UPPER, (below, cell)).start()
+    remote(payload, table, send_sem, recv_sem, UPPER, LOWER, (above, cell)).start()
+
+    def push(k, _):
+        peer = lax.rem(cell + k, PEERS)
+        pick = send_ref[peer]
+        payload[peer] = jnp.where(pick >= 0, own[jnp.maximum(pick, 0)], 0.0)
+        remote(payload, table, send_sem, recv_sem, peer, cell, (region, peer)).start()
+        return 0
+    lax.fori_loop(1, PEERS, push, 0)
+    for k in range(4):
+        pltpu.make_async_copy(own.at[k], table.at[OWN + k], local_sem.at[k]).wait()
+    pltpu.make_async_copy(payload.at[cell], table.at[cell], local_sem.at[4]).wait()
+
+    def finish(k, _):
+        peer = lax.rem(cell + k, PEERS)
+        copy = remote(payload, table, send_sem, recv_sem, peer, peer, (region, peer))
+        copy.wait_recv()
+        copy.wait_send()
+        return 0
+    lax.fori_loop(1, PEERS, finish, 0)
+    for slot, device in ((LOWER, (below, cell)), (UPPER, (above, cell))):
+        copy = remote(payload, table, send_sem, recv_sem, slot, slot, device)
+        copy.wait_recv()
+        copy.wait_send()
+
+
+def exchange(counts, send, edge, positions, velocities, mass, smoothing):
+    smem = pl.BlockSpec(memory_space=pltpu.SMEM)
+    vmem = pl.BlockSpec(memory_space=pltpu.VMEM)
+    return pl.pallas_call(
+        exchange_kernel,
+        out_shape=jax.ShapeDtypeStruct((NSLOT, 8, 512), F32),
+        in_specs=[smem] * 3 + [vmem] * 4,
+        out_specs=pl.BlockSpec(memory_space=pl.ANY),
+        scratch_shapes=[
+            pltpu.VMEM((4, 8, 512), F32),
+            pltpu.VMEM((34, 8, 512), F32),
+            pltpu.SemaphoreType.DMA((34,)),
+            pltpu.SemaphoreType.DMA((34,)),
+            pltpu.SemaphoreType.DMA((5,)),
+        ],
+        compiler_params=pltpu.CompilerParams(
+            collective_id=0, has_side_effects=True, vmem_limit_bytes=60 * 1024 * 1024
+        ),
+        name="exchange",
+    )(counts, send, edge, positions, velocities, mass, smoothing)
+
+
+def return_kernel(counts, send_ref, edge_ref, back, part, accel, inbox, total, send_sem, recv_sem):
+    region, cell, below, above = place()
+    barrier = greet()
+    pl.semaphore_wait(barrier, PEERS + 1)
+
+    def push(k, _):
+        peer = lax.rem(cell + k, PEERS)
+        remote(back, inbox, send_sem, recv_sem, peer, cell, (region, peer)).start()
+        return 0
+    lax.fori_loop(1, PEERS, push, 0)
+    remote(back, inbox, send_sem, recv_sem, LOWER, UPPER, (below, cell)).start()
+    remote(back, inbox, send_sem, recv_sem, UPPER, LOWER, (above, cell)).start()
+    total[...] = jnp.zeros_like(total)
+
+    def gather(slot, device, target):
+        copy = remote(back, inbox, send_sem, recv_sem, slot, slot, device)
+        copy.wait_recv()
+        copy.wait_send()
+        rows = inbox[slot]
+        for a in range(4):
+            total[a] += jnp.where(target == a, rows, 0.0)
+
+    def finish(k, _):
+        peer = lax.rem(cell + k, PEERS)
+        gather(peer, (region, peer), send_ref[peer])
+        return 0
+    lax.fori_loop(1, PEERS, finish, 0)
+    gather(LOWER, (below, cell), edge_ref[0])
+    gather(UPPER, (above, cell), edge_ref[1])
+    lane_id = lax.broadcasted_iota(jnp.int32, (1, 512), 1)
+    for a in range(4):
+        live = lane_id < counts[a]
+        for k in range(3):
+            accel[k, a:a + 1] = part[k, a:a + 1] + jnp.where(live, total[a, 1 + k:2 + k], 0.0)
+
+
+def give_back(counts, send, edge, back, part):
+    smem = pl.BlockSpec(memory_space=pltpu.SMEM)
+    vmem = pl.BlockSpec(memory_space=pltpu.VMEM)
+    return pl.pallas_call(
+        return_kernel,
+        out_shape=jax.ShapeDtypeStruct((3, 4, 512), F32),
+        in_specs=[smem] * 3 + [pl.BlockSpec(memory_space=pl.ANY), vmem],
+        out_specs=vmem,
+        scratch_shapes=[
+            pltpu.VMEM((34, 4, 512), F32),
+            pltpu.VMEM((4, 4, 512), F32),
+            pltpu.SemaphoreType.DMA((34,)),
+            pltpu.SemaphoreType.DMA((34,)),
+        ],
+        compiler_params=pltpu.CompilerParams(
+            collective_id=1, has_side_effects=True, vmem_limit_bytes=60 * 1024 * 1024
+        ),
+        name="give_back",
+    )(counts, send, edge, back, part)
 
 
 def on_device(
     positions, velocities, mass, smoothing, energy, counts, send_cells, local_pairs, edge_cells
 ):
-    slot_ids = lax.broadcasted_iota(jnp.int32, (4, 512), 1)
-    occupied = slot_ids < counts[:, None]
-    rows = jnp.concatenate(
-        [
-            jnp.where(occupied, mass, 0.0)[:, None],
-            jnp.transpose(positions, (1, 0, 2)) - 0.5,
-            jnp.transpose(velocities, (1, 0, 2)),
-            smoothing[:, None],
-        ],
-        axis=1,
-    )
-    send = send_cells[0, 0, :, 0]
-    edge = edge_cells[0, 0]
-    payload = jnp.where((send >= 0)[:, None, None], rows[jnp.maximum(send, 0)], 0.0)
-    received = lax.all_to_all(payload, "cell", split_axis=0, concat_axis=0, tiled=True)
-    lower, upper = shifted(rows[edge[0]], rows[edge[1]])
-    table = jnp.concatenate([received, lower[None], upper[None], rows], axis=0)
-    n = jnp.sum((table[:, 0] > 0.0).astype(jnp.int32), axis=1)
-    density, accel, heat, back = compute(n, send, local_pairs[0, 0].reshape(8), edge, table, energy)
-    returned = lax.all_to_all(back[:32], "cell", split_axis=0, concat_axis=0, tiled=True)
-    lower, upper = shifted(back[32], back[33])
-    whole = jnp.concatenate([returned, lower[None], upper[None]], axis=0)
-    target = jnp.concatenate([send, edge])
-    own = jnp.arange(4, dtype=jnp.int32)
-    hit = (target[None, :] == own[:, None]).astype(jnp.float32)
-    extra = jnp.sum(hit[:, :, None, None] * whole[None, :, 1:4], axis=1)
-    extra = jnp.where(occupied[None], jnp.transpose(extra, (1, 0, 2)), 0.0)
-    return density, accel + extra, heat
+    send = send_cells.reshape(32)
+    edge = edge_cells.reshape(2)
+    table = exchange(counts, send, edge, positions, velocities, mass, smoothing)
+    density, part, heat, back = compute(send, local_pairs.reshape(8), edge, table, energy)
+    accel = give_back(counts, send, edge, back, part)
+    return density, accel, heat
 
 
 def solution(mesh):

time: 98 us -> 89.2 us (0.910)
  the two profiles are of different devices: /device:TPU:1 before, /device:TPU:193 now
where the time goes in v2:
time: 89.2 us; the launch traced here: 88.8 us
  Pallas kernels  85.4 us (96%)
  local copies, waits for them, and re-layouts  2.74 us (3%)
    pallas_call x1, Pallas kernels, compute(): pl.pallas_call(compute_kernel, out_shape=(jax.ShapeDtypeStruct((4, 512),...  38.7 us
    pallas_call x1, Pallas kernels, give_back(): pl.pallas_call(return_kernel, out_shape=jax.ShapeDtypeStruct((3, 4, 512),...  30.9 us
    pallas_call x1, Pallas kernels, exchange(): pl.pallas_call(exchange_kernel, out_shape=jax.ShapeDtypeStruct((NSLOT, 8,...  15.9 us
    unnamed x4, local copies, waits for them, and re-layouts  2.11 us

profile of v2, /device:TPU:193, one launch (start us, length us, event | category | flops | bytes accessed | tf_op | source)
XLA Modules:
  0.0 88.8 jit_solution(9393073061097627849)
XLA Ops:
  0.6 0.0 copy-start
  0.6 0.7 copy-done
  1.3 0.1 copy.13
  1.4 0.6 reshape.16.pair_ref
  2.0 15.9 %exchange.1.table = f32[38,8,512]{2,1,0:T(8,128)} custom-call(s32[4]{0:T(128)} %counts.3, s32[32]{0:T(128)} %bitcast.2, s32[2]{0:T(128)} %bitcast.5, f32[3,4,512]{2,1,0:T(4,128)} %positions.1, f32[3,4,512]{2,1,0:T(4,128)} %velocities.1, f32[4,512]{1,0:T(4,128)} %mass.1, f32[4,512]{1,0:T(4,128)} %smoothing.1), custom_call_target="tpu_custom_call" | custom-call | tf_op jit(solution)/shard_map/exchange/pallas_call | solution.py:389
  17.9 38.7 %tiles.1 = (f32[4,512]{1,0:T(4,128)}, f32[3,4,512]{2,1,0:T(4,128)}, f32[4,512]{1,0:T(4,128)}, f32[38,4,512]{2,1,0:T(4,128)}) custom-call(s32[32]{0:T(128)} %bitcast.3, s32[8]{0:T(128)} %reshape.16.pair_ref, s32[2]{0:T(128)} %bitcast.6, f32[38,8,512]{2,1,0:T(8,128)} %exchange.1.table, f32[4,512]{1,0:T(4,128)} %energy.1), custom_call_target="tpu_custom_call" | custom-call | tf_op jit(solution)/shard_map/tiles/pallas_call | solution.py:268
  56.6 30.9 %give_back.1 = f32[3,4,512]{2,1,0:T(4,128)} custom-call(s32[4]{0:T(128)} %counts.3, s32[32]{0:T(128)} %bitcast.4, s32[2]{0:T(128)} %bitcast.7, f32[38,4,512]{2,1,0:T(4,128)} %get-tuple-element.8.back, f32[3,4,512]{2,1,0:T(4,128)} %get-tuple-element.9.part), custom_call_target="tpu_custom_call" | custom-call | tf_op jit(solution)/shard_map/give_back/pallas_call | solution.py:447
  87.5 1.3 %copy.15 = f32[3,4,512]{2,1,0:T(4,128)} copy(f32[3,4,512]{2,1,0:T(4,128)} %give_back.1) | data formatting | bytes 49152
Async XLA Ops:
  0.6 0.7 copy-start

commit v3 on v2

v3 whole, which is shorter than its diff:
```python
import math
import jax
import jax.numpy as jnp
from jax import lax
from jax.experimental import pallas as pl
from jax.experimental.pallas import tpu as pltpu
from jax.sharding import PartitionSpec as P

GAMMA = 5.0 / 3.0
F32, BF16, I32 = jnp.float32, jnp.bfloat16, jnp.int32
U = 3
UL = 2
PEERS = 32
LOWER, UPPER, OWN, NSLOT = 32, 33, 34, 38
MAXT = 34
LOCAL = 104
GBLK = LOCAL + MAXT * 16 + 20 + 6 * U
ROOT = math.sqrt(24.0 / math.pi)
MIB = 1024 * 1024
MESH = pl.DeviceIdType.MESH


def halves(v):
    hi = v.astype(BF16).astype(F32)
    return hi, v - hi


def thirds(v):
    first, rest = halves(v)
    second, third = halves(rest)
    return first, second, third


def nt(a, b):
    return lax.dot_general(a, b, (((1,), (1,)), ((), ())), preferred_element_type=F32)


def nn(a, b):
    return lax.dot_general(a, b, (((1,), (0,)), ((), ())), preferred_element_type=F32)


def row_ids():
    return lax.broadcasted_iota(I32, (8, 512), 0)


def square(st):
    x = st[1:2]
    y = st[2:3]
    z = st[3:4]
    return x * x + y * y + z * z


def moments(st):
    row = row_ids()
    vx = st[1:2] * st[4:5] + st[2:3] * st[5:6] + st[3:4] * st[6:7]
    return jnp.where(row == 0, 1.0, jnp.where(row == 7, vx, st)) * st[0:1]


def pair_rows(v):
    first, second = halves(v)
    return jnp.concatenate([first, second], axis=0).astype(BF16)


def store_source(st, base, feat_s, rows_s, lane_s):
    row = row_ids()
    hinv = 1.0 / st[7:8]
    sj = ROOT * hinv * hinv
    f = jnp.where(row == 0, square(st), jnp.where(row <= 3, st, jnp.where(row == 4, 1.0, 0.0)))
    f1, f2, f3 = thirds(f)
    t1, t2, t3 = thirds(sj * hinv)
    t1 = jnp.where(row == 5, t1, 0.0)
    t2 = jnp.where(row == 5, t2, 0.0)
    t3 = jnp.where(row == 5, t3, 0.0)
    near = jnp.concatenate([f1, f1, f2, f2, f1, f3], axis=0).astype(BF16)
    ratio = jnp.concatenate([t1, t1, t2, t2, t1, t3], axis=0).astype(BF16)
    rows = pair_rows(moments(st))
    lane = jnp.where(row == 0, sj, st[0:1])
    for jb in range(4):
        cut = slice(jb * 128, (jb + 1) * 128)
        feat_s[base + jb, :, 0:128] = near[:, cut]
        feat_s[base + jb, :, 128:256] = ratio[:, cut]
        rows_s[base + jb, :, 0:128] = rows[:, cut]
        rows_s[base + jb, :, 128:256] = rows[:, cut]
        lane_s[base + jb] = lane[:, cut]


def store_target(st, base, feat_o, s_o, m_o, rows_o):
    row = row_ids()
    h = st[7:8]
    hinv = 1.0 / h
    si = ROOT * hinv * hinv
    ti = si * hinv
    f = jnp.where(row == 0, 1.0, jnp.where(row <= 3, -2.0 * st, jnp.where(row == 4, square(st), 0.0)))
    f = jnp.where(row == 5, h * h * h * (1.0 / ROOT), f * (ti * ti))
    f1, f2, f3 = thirds(f)
    s1, s2, s3 = thirds(si)
    m1, m2, m3 = thirds(st[0:1])
    extra = jnp.where(row == 0, s1, jnp.where(row == 1, s2, jnp.where(row == 2, s3, 0.0)))
    extra = jnp.where(row == 3, m1, jnp.where(row == 4, m2, jnp.where(row == 5, m3, extra)))
    whole = jnp.concatenate([f1, f2, f1, f2, f3, f1, extra, jnp.zeros((8, 512), F32)], axis=0).astype(BF16)
    rows = pair_rows(moments(st) * ti)
    size = (128, 128)
    eye = (lax.broadcasted_iota(I32, size, 0) == lax.broadcasted_iota(I32, size, 1)).astype(F32).astype(BF16)
    at = lax.broadcasted_iota(I32, (64, 256), 0)
    side = lax.broadcasted_iota(I32, (64, 256), 1) >= 128
    lowest = jnp.where(side, 51, 48)
    pick = ((at >= lowest) & (at < lowest + 3)).astype(F32).astype(BF16)
    for ib in range(4):
        cut = slice(ib * 128, (ib + 1) * 128)
        part = nt(eye, whole[:, cut]).astype(BF16)
        feat_o[base + ib] = part[:, :48]
        wide = nn(part, pick)
        s_o[base + ib] = wide[:, :128]
        m_o[base + ib] = wide[:, 128:]
        rows_o[base + ib] = rows[:, cut]


def split_store(gst, at, g):
    hi = g.astype(BF16)
    gst[at, :, 0:128] = hi
    gst[at, :, 128:256] = (g - hi.astype(F32)).astype(BF16)


def fold(v):
    return v[:, :128] + v[:, 128:]


def local_tiles(pair_ref, own, feat_s, rows_s, lane_s, feat_o, s_o, m_o, rows_o, near_a, near_b,
                gst, acc_w, row_w, acc_g, row_g):
    for a in range(4):
        store_source(own[a], a * 4, feat_s, rows_s, lane_s)
        store_target(own[a], a * 4, feat_o, s_o, m_o, rows_o)
    acc_w[...] = jnp.zeros_like(acc_w)
    row_w[...] = jnp.zeros_like(row_w)
    acc_g[...] = jnp.zeros_like(acc_g)
    row_g[...] = jnp.zeros_like(row_g)
    for u in range(UL):
        gst[LOCAL + 2 * UL + u] = jnp.zeros((128, 256), BF16)

    def where(n):
        n = jnp.minimum(n, LOCAL - 1)
        t = lax.rem(n, 10)
        j1 = (t >= 1).astype(I32) + (t >= 3).astype(I32) + (t >= 6).astype(I32)
        i1 = t - (j1 * (j1 + 1)) // 2
        m = jnp.maximum(n - 40, 0)
        k = m // 16
        self_ = n < 40
        ib = jnp.where(self_, i1, lax.rem(m, 4))
        jb = jnp.where(self_, j1, lax.rem(m // 4, 4))
        a = jnp.where(self_, n // 10, pair_ref[0, k])
        b = jnp.where(self_, n // 10, pair_ref[1, k])
        group = jnp.where(self_, n // 10, 4 + k)
        both = jnp.where(self_ & (i1 == j1), 0.0, 1.0)
        return a * 4 + ib, b * 4 + jb, group * 4 + ib, group * 4 + jb, both

    def distances(buf, n):
        for u in range(UL):
            oi, sj, _, _, _ = where(n + u)
            buf[u] = nn(feat_o[oi], feat_s[sj])

    def elements(buf, n):
        for u in range(UL):
            oi, si, gi, gj, both = where(n + u)
            both = jnp.where(n + u < LOCAL, both, 0.0)
            sj = lane_s[si][0:1]
            mass = jnp.where(n + u < LOCAL, lane_s[si][1:2], 0.0)
            d2 = jnp.maximum(buf[u, :, 0:128], 1e-6)
            inv = lax.rsqrt(d2)
            pi = d2 * inv
            pj = pi * buf[u, :, 128:256]
            ai = jnp.maximum(s_o[oi] - pi, 0.0)
            ci = jnp.maximum(ai - pi, 0.0)
            aj = jnp.maximum(sj - pj, 0.0)
            cj = jnp.maximum(aj - pj, 0.0)
            qa = ai * ai
            qc = ci * ci
            ra = aj * aj
            rc = cj * cj
            acc_w[gi] += ((ai + ai) * qa - qc * ci) * mass
            back = ((aj + aj) * ra - rc * cj) * m_o[oi]
            row_w[gj] += both * jnp.sum(back.reshape(16, 8, 128), axis=0)
            split_store(gst, n + u, (qa - qc + ra - rc) * inv)

    def products(n, slot):
        out = []
        for u in range(UL):
            oi, sj, _, _, _ = where(jnp.maximum(n + u, 0))
            g = gst[slot + u]
            out.append((nt(rows_s[sj], g), fold(nn(rows_o[oi], g))))
        return out

    def collect(sums, n):
        for u in range(UL):
            _, _, gi, gj, both = where(jnp.maximum(n + u, 0))
            good = (n + u >= 0) & (n + u < LOCAL)
            acc_g[gi] += jnp.where(good, sums[u][0], 0.0)
            row_g[gj] += jnp.where(good, sums[u][1], 0.0) * both

    distances(near_a, 0)
    step = 2 * UL

    def body(n, _):
        base = n * step
        before = jnp.where(n == 0, LOCAL + 2 * UL, base - UL)
        sums = products(base - UL, before)
        elements(near_a, base)
        distances(near_b, base + UL)
        collect(sums, base - UL)
        sums = products(base, base)
        elements(near_b, base + UL)
        distances(near_a, base + step)
        collect(sums, base)
        return 0
    lax.fori_loop(0, LOCAL // step, body, 0)
    sums = products(LOCAL - UL, LOCAL - UL)
    collect(sums, LOCAL - UL)


LOCAL_SCRATCH = [
    pltpu.VMEM((16, 48, 256), BF16),
    pltpu.VMEM((16, 16, 256), BF16),
    pltpu.VMEM((16, 8, 128), F32),
    pltpu.VMEM((16, 128, 48), BF16),
    pltpu.VMEM((16, 128, 128), F32),
    pltpu.VMEM((16, 128, 128), F32),
    pltpu.VMEM((16, 16, 128), BF16),
    pltpu.VMEM((UL, 128, 256), F32),
    pltpu.VMEM((UL, 128, 256), F32),
    pltpu.VMEM((LOCAL + 3 * UL, 128, 256), BF16),
    pltpu.VMEM((32, 128, 128), F32),
    pltpu.VMEM((32, 8, 128), F32),
    pltpu.VMEM((32, 16, 128), F32),
    pltpu.VMEM((32, 16, 128), F32),
]
LOCAL_OUT = (
    jax.ShapeDtypeStruct((LOCAL, 128, 256), BF16),
    jax.ShapeDtypeStruct((32, 128, 128), F32),
    jax.ShapeDtypeStruct((32, 8, 128), F32),
    jax.ShapeDtypeStruct((32, 16, 128), F32),
    jax.ShapeDtypeStruct((32, 16, 128), F32),
    jax.ShapeDtypeStruct((16, 128, 48), BF16),
    jax.ShapeDtypeStruct((16, 128, 128), F32),
)
NLOCAL = len(LOCAL_OUT)


def local_results(scratch):
    feat_o, s_o = scratch[3], scratch[4]
    gst, acc_w, row_w, acc_g, row_g = scratch[9:14]
    return gst.at[pl.ds(0, LOCAL)], acc_w, row_w, acc_g, row_g, feat_o, s_o


def compute_kernel(send_ref, pair_ref, edge_ref, table, energy, g_in, w_in, roww_in, gg_in, rowg_in, feat_o, s_o,
                   rho_out, acc_out, er_out, t_out,
                   ta, ts, feat_s, rows_s, lane_s, near_a, near_b, gst, acc_g, acc_w, q_rows, q_wide,
                   cnt_v, n_ref, w_pair, cnt_sem, g_sem, w_sem):
    found = jnp.sum((table[:, 0, :] > 0.0).astype(F32), axis=1, keepdims=True)
    cnt_v[...] = jnp.broadcast_to(found, (NSLOT, 128)).astype(I32)
    fetch = pltpu.make_async_copy(cnt_v, n_ref, cnt_sem)
    fetch.start()
    get_g = pltpu.make_async_copy(g_in, gst.at[pl.ds(0, LOCAL)], g_sem)
    get_w = pltpu.make_async_copy(w_in.at[pl.ds(0, 16)], acc_w, w_sem.at[0])
    get_p = pltpu.make_async_copy(w_in.at[pl.ds(16, 16)], w_pair, w_sem.at[1])
    get_w.start()
    get_p.start()
    get_g.start()
    row = row_ids()
    for k in range(16):
        acc_g[k] = gg_in[k]
    for u in range(U):
        gst[LOCAL + u] = jnp.zeros((128, 256), BF16)
    t_out[...] = jnp.zeros_like(t_out)
    fetch.wait()

    def blocks(s):
        return (n_ref[s, 0] + 127) >> 7

    def add(count, a, s):
        ta[count] = a
        ts[count] = s
        return count + (n_ref[s, 0] > 0).astype(I32)
    count = lax.fori_loop(0, 32, lambda s, cnt: add(cnt, jnp.maximum(send_ref[s], 0), s), I32(0))
    count = add(count, edge_ref[0], I32(LOWER))
    count = add(count, edge_ref[1], I32(UPPER))
    ta[count] = ta[0]
    ts[count] = ts[0]
    total = lax.fori_loop(0, count, lambda k, v: v + blocks(OWN + ta[k]) * blocks(ts[k]), I32(0))

    def source_loop(k, _):
        for u in range(2):
            s = ts[2 * k + u]
            store_source(table[s], s * 4, feat_s, rows_s, lane_s)
        return 0
    lax.fori_loop(0, (count + 1) // 2, source_loop, 0)
    get_w.wait()

    def at(tile):
        a, s = ta[tile], ts[tile]
        return a, s, blocks(OWN + a), blocks(s)

    def advance(state):
        tile, ib, jb, a, s, ni, nj = state
        ib = ib + 1
        wrap_i = ib >= ni
        ib = jnp.where(wrap_i, 0, ib)
        jb = jnp.where(wrap_i, jb + 1, jb)
        wrap_j = jb >= nj
        jb = jnp.where(wrap_j, 0, jb)
        tile = jnp.where(wrap_j, jnp.minimum(tile + 1, count), tile)
        return (tile, ib, jb) + at(tile)

    def group(state):
        out = []
        for _ in range(U):
            out.append((state[3] * 4 + state[1], state[4] * 4 + state[2]))
            state = advance(state)
        return state, tuple(out)

    def distances(buf, where):
        for u in range(U):
            buf[u] = nn(feat_o[where[u][0]], feat_s[where[u][1]])

    def elements(buf, where, base):
        for u in range(U):
            oi, si = where[u]
            sj = lane_s[si][0:1]
            mass = lane_s[si][1:2] * (base + u < total).astype(F32)
            d2 = jnp.maximum(buf[u, :, 0:128], 1e-6)
            inv = lax.rsqrt(d2)
            pi = d2 * inv
            pj = pi * buf[u, :, 128:256]
            ai = jnp.maximum(s_o[oi] - pi, 0.0)
            ci = jnp.maximum(ai - pi, 0.0)
            qa = ai * ai
            qc = ci * ci
            acc_w[oi] += ((ai + ai) * qa - qc * ci) * mass
            aj = jnp.maximum(sj - pj, 0.0)
            mj = jnp.minimum(pj, aj)
            split_store(gst, LOCAL + base + U + u, (qa - qc + mj * (aj + aj - mj)) * inv)

    def products(where, base):
        return [nt(rows_s[where[u][1]], gst[LOCAL + base + U + u]) for u in range(U)]

    def collect(sums, where, base):
        for u in range(U):
            acc_g[where[u][0]] += jnp.where(base + u < total, sums[u], 0.0)

    zero = I32(0)
    walk, first = group((zero, zero, zero) + at(zero))
    walk, second = group(walk)
    distances(near_a, first)

    def body(n, carry):
        walk, prev, now, later = carry
        base = n * (2 * U)
        sums = products(prev, base - U)
        elements(near_a, now, base)
        distances(near_b, later)
        collect(sums, prev, base - U)
        walk, after = group(walk)
        sums = products(now, base)
        elements(near_b, later, base + U)
        distances(near_a, after)
        collect(sums, now, base)
        walk, last = group(walk)
        return walk, later, after, last

    steps = (total + 2 * U - 1) // (2 * U)
    lax.fori_loop(0, steps + 1, body, (walk, first, first, second))

    def clear(k, _):
        gst[LOCAL + (2 * steps + 3) * U + k] = jnp.zeros((128, 256), BF16)
        return 0
    lax.fori_loop(0, 17, clear, 0)

    get_p.wait()
    lane_id = lax.broadcasted_iota(I32, (1, 512), 1)
    row_sum = [None] * 4
    flat = [None] * 4
    for a in range(4):
        row_sum[a] = jnp.concatenate([roww_in[a * 4 + b] for b in range(4)], axis=1)
        flat[a] = jnp.concatenate([rowg_in[a * 4 + b] for b in range(4)], axis=1)
    for k in range(4):
        ka, kb = pair_ref[0, k], pair_ref[1, k]
        rw = jnp.concatenate([roww_in[16 + k * 4 + b] for b in range(4)], axis=1)
        rg = jnp.concatenate([rowg_in[16 + k * 4 + b] for b in range(4)], axis=1)
        for a in range(4):
            row_sum[a] = row_sum[a] + jnp.where(kb == a, rw, 0.0)
            flat[a] = flat[a] + jnp.where(kb == a, rg, 0.0)
        for b in range(4):
            acc_g[ka * 4 + b] += gg_in[16 + k * 4 + b]
            acc_w[ka * 4 + b] += w_pair[k * 4 + b]

    for a in range(4):
        st = table[OWN + a]
        h = st[7:8]
        h3 = h * h * h
        ti = ROOT / h3
        sums = jnp.concatenate([acc_g[a * 4 + ib] for ib in range(4)], axis=1)
        sums = (sums[:8] + sums[8:]) * ti + flat[a][:8] + flat[a][8:]
        wsum = jnp.concatenate([jnp.sum(acc_w[a * 4 + ib].T, axis=0, keepdims=True) for ib in range(4)], axis=1)
        wsum = wsum + jnp.sum(row_sum[a], axis=0, keepdims=True)
        rho = wsum * (h3 * (8.0 / math.pi / ROOT ** 3))
        live = lane_id < n_ref[OWN + a, 0]
        press = jnp.where(live, (GAMMA - 1.0) * energy[a:a + 1] / jnp.where(live, rho, 1.0), 0.0)
        rho_out[a:a + 1] = jnp.where(live, rho, 0.0)
        dx = [st[1 + k:2 + k] * sums[0:1] - sums[1 + k:2 + k] for k in range(3)]
        heat = sums[7:8]
        for k in range(3):
            heat = heat + st[4 + k:5 + k] * dx[k] - st[1 + k:2 + k] * sums[4 + k:5 + k]
            acc_out[k, a:a + 1] = jnp.where(live, press * dx[k], 0.0)
        er_out[a:a + 1] = jnp.where(live, -press * heat, 0.0)
        q = jnp.where(row == 0, 1.0, jnp.where(row <= 3, st, 0.0)) * (st[0:1] * press)
        q_rows[a] = pair_rows(q * ti)
        plain = pair_rows(q)
        for jb in range(4):
            cut = slice(jb * 128, (jb + 1) * 128)
            q_wide[a * 4 + jb, :, 0:128] = plain[:, cut]
            q_wide[a * 4 + jb, :, 128:256] = plain[:, cut]
    get_g.wait()

    def settle(s, cut, o, good):
        o = o[:8] + o[8:]
        st = table[s][:, cut]
        extra = st * o[0:1] - o
        t_out[s, :, cut] += jnp.where(good, extra[0:4], 0.0)

    def mirror(step, base):
        for u in range(2):
            tile = 2 * step + u
            a, s, ni, nj = at(tile)
            q = q_rows[a]
            for jb in range(4):
                g = gst[pl.ds(LOCAL + base + jb * ni, 4)].reshape(512, 256)
                settle(s, slice(jb * 128, (jb + 1) * 128), fold(nn(q, g)), tile < count)
            base = base + ni * nj
        return base
    lax.fori_loop(0, (count + 1) // 2, mirror, I32(U))

    for a in range(4):
        ti = ROOT / (table[OWN + a][7:8] * table[OWN + a][7:8] * table[OWN + a][7:8])
        for jb in range(4):
            first = a * 10 + (jb * (jb + 1)) // 2
            cut = slice(jb * 128, (jb + 1) * 128)
            g = gst[pl.ds(first, jb + 1)].reshape((jb + 1) * 128, 256)
            o = fold(nn(q_rows[a, :, 0:(jb + 1) * 128], g))
            for other in range(jb + 1, 4):
                at_ = a * 10 + (other * (other + 1)) // 2 + jb
                o = o + nt(q_wide[a * 4 + other], gst[at_]) * ti[:, cut]
            settle(OWN + a, cut, o, True)
    for k in range(4):
        ka, kb = pair_ref[0, k], pair_ref[1, k]
        hk = table[OWN + ka][7:8]
        ti = ROOT / (hk * hk * hk)
        for jb in range(4):
            cut = slice(jb * 128, (jb + 1) * 128)
            first = 40 + k * 16
            g = gst[pl.ds(first + jb * 4, 4)].reshape(512, 256)
            settle(OWN + kb, cut, fold(nn(q_rows[ka], g)), True)
            o = nt(q_wide[kb * 4], gst[first + jb])
            for other in range(1, 4):
                o = o + nt(q_wide[kb * 4 + other], gst[first + other * 4 + jb])
            settle(OWN + ka, cut, o * ti[:, cut], True)

    for a in range(4):
        live = lane_id < n_ref[OWN + a, 0]
        for k in range(3):
            acc_out[k, a:a + 1] += jnp.where(live, t_out[OWN + a, 1 + k:2 + k], 0.0)


def compute(send, pairs, edge, table, energy, local):
    smem = pl.BlockSpec(memory_space=pltpu.SMEM)
    vmem = pl.BlockSpec(memory_space=pltpu.VMEM)
    hbm = pl.BlockSpec(memory_space=pl.ANY)
    return pl.pallas_call(
        compute_kernel,
        out_shape=(
            jax.ShapeDtypeStruct((4, 512), F32),
            jax.ShapeDtypeStruct((3, 4, 512), F32),
            jax.ShapeDtypeStruct((4, 512), F32),
            jax.ShapeDtypeStruct((NSLOT, 4, 512), F32),
        ),
        in_specs=[smem] * 3 + [vmem] * 2 + [hbm] * 2 + [vmem] * 5,
        out_specs=(vmem,) * 4,
        scratch_shapes=[
            pltpu.SMEM((MAXT + 2,), I32),
            pltpu.SMEM((MAXT + 2,), I32),
            pltpu.VMEM((34 * 4, 48, 256), BF16),
            pltpu.VMEM((34 * 4, 16, 256), BF16),
            pltpu.VMEM((34 * 4, 8, 128), F32),
            pltpu.VMEM((U, 128, 256), F32),
            pltpu.VMEM((U, 128, 256), F32),
            pltpu.VMEM((GBLK, 128, 256), BF16),
            pltpu.VMEM((16, 16, 128), F32),
            pltpu.VMEM((16, 128, 128), F32),
            pltpu.VMEM((4, 16, 512), BF16),
            pltpu.VMEM((16, 16, 256), BF16),
            pltpu.VMEM((NSLOT, 128), I32),
            pltpu.SMEM((NSLOT, 128), I32),
            pltpu.VMEM((16, 128, 128), F32),
            pltpu.SemaphoreType.DMA,
            pltpu.SemaphoreType.DMA,
            pltpu.SemaphoreType.DMA((2,)),
        ],
        compiler_params=pltpu.CompilerParams(vmem_limit_bytes=62 * MIB),
        name="tiles",
    )(send, pairs, edge, table, energy, *local)


def place():
    region, cell = lax.axis_index("region"), lax.axis_index("cell")
    count = lax.axis_size("region")
    return region, cell, lax.rem(region + count - 1, count), lax.rem(region + 1, count)


def greet():
    region, cell, below, above = place()
    barrier = pltpu.get_barrier_semaphore()

    def one(k, _):
        peer = lax.rem(cell + k, PEERS)
        pl.semaphore_signal(barrier, inc=1, device_id=(region, peer), device_id_type=MESH)
        return 0
    lax.fori_loop(1, PEERS, one, 0)
    pl.semaphore_signal(barrier, inc=1, device_id=(below, cell), device_id_type=MESH)
    pl.semaphore_signal(barrier, inc=1, device_id=(above, cell), device_id_type=MESH)
    return barrier


def remote(src, dst, send_sem, recv_sem, slot, mine, device):
    return pltpu.make_async_remote_copy(
        src_ref=src.at[slot],
        dst_ref=dst.at[mine],
        send_sem=send_sem.at[slot],
        recv_sem=recv_sem.at[mine],
        device_id=device,
        device_id_type=MESH,
    )


def exchange_kernel(counts, send_ref, edge_ref, pair_ref, positions, velocities, mass, smoothing, table, *refs):
    outs, scratch = refs[:NLOCAL], refs[NLOCAL:-5]
    own, payload, send_sem, recv_sem, local_sem = refs[-5:]
    region, cell, below, above = place()
    barrier = greet()
    lane_id = lax.broadcasted_iota(I32, (1, 512), 1)
    for k in range(4):
        live = lane_id < counts[k]
        own[k] = jnp.concatenate(
            [jnp.where(live, mass[k:k + 1], 0.0)]
            + [positions[i, k:k + 1] - 0.5 for i in range(3)]
            + [velocities[i, k:k + 1] for i in range(3)]
            + [smoothing[k:k + 1]],
            axis=0,
        )
        pltpu.make_async_copy(own.at[k], table.at[OWN + k], local_sem.at[k]).start()
    low = (region > 0).astype(F32)
    high = (region < lax.axis_size("region") - 1).astype(F32)
    payload[LOWER] = own[edge_ref[0]] * low
    payload[UPPER] = own[edge_ref[1]] * high
    payload[cell] = jnp.zeros((8, 512), F32)
    pltpu.make_async_copy(payload.at[cell], table.at[cell], local_sem.at[4]).start()
    pl.semaphore_wait(barrier, PEERS + 1)
    remote(payload, table, send_sem, recv_sem, LOWER, UPPER, (below, cell)).start()
    remote(payload, table, send_sem, recv_sem, UPPER, LOWER, (above, cell)).start()

    def push(k, _):
        peer = lax.rem(cell + k, PEERS)
        pick = send_ref[peer]
        payload[peer] = jnp.where(pick >= 0, own[jnp.maximum(pick, 0)], 0.0)
        remote(payload, table, send_sem, recv_sem, peer, cell, (region, peer)).start()
        return 0
    lax.fori_loop(1, PEERS, push, 0)

    local_tiles(pair_ref, own, *scratch)
    copies = [
        pltpu.make_async_copy(src, dst, local_sem.at[5 + i])
        for i, (src, dst) in enumerate(zip(local_results(scratch), outs))
    ]
    for copy in copies:
        copy.start()
    for k in range(4):
        pltpu.make_async_copy(own.at[k], table.at[OWN + k], local_sem.at[k]).wait()
    pltpu.make_async_copy(payload.at[cell], table.at[cell], local_sem.at[4]).wait()

    def finish(k, _):
        peer = lax.rem(cell + k, PEERS)
        copy = remote(payload, table, send_sem, recv_sem, peer, peer, (region, peer))
        copy.wait_recv()
        copy.wait_send()
        return 0
    lax.fori_loop(1, PEERS, finish, 0)
    for slot, device in ((LOWER, (below, cell)), (UPPER, (above, cell))):
        copy = remote(payload, table, send_sem, recv_sem, slot, slot, device)
        copy.wait_recv()
        copy.wait_send()
    for copy in copies:
        copy.wait()


def exchange(counts, send, edge, pairs, positions, velocities, mass, smoothing):
    smem = pl.BlockSpec(memory_space=pltpu.SMEM)
    vmem = pl.BlockSpec(memory_space=pltpu.VMEM)
    hbm = pl.BlockSpec(memory_space=pl.ANY)
    return pl.pallas_call(
        exchange_kernel,
        out_shape=(jax.ShapeDtypeStruct((NSLOT, 8, 512), F32),) + LOCAL_OUT,
        in_specs=[smem] * 4 + [vmem] * 4,
        out_specs=(hbm,) * (1 + NLOCAL),
        scratch_shapes=LOCAL_SCRATCH + [
            pltpu.VMEM((4, 8, 512), F32),
            pltpu.VMEM((34, 8, 512), F32),
            pltpu.SemaphoreType.DMA((34,)),
            pltpu.SemaphoreType.DMA((34,)),
            pltpu.SemaphoreType.DMA((5 + NLOCAL,)),
        ],
        compiler_params=pltpu.CompilerParams(
            collective_id=0, has_side_effects=True, vmem_limit_bytes=60 * MIB
        ),
        name="exchange",
    )(counts, send, edge, pairs, positions, velocities, mass, smoothing)


def return_kernel(counts, send_ref, edge_ref, back, accel, inbox, total, send_sem, recv_sem):
    region, cell, below, above = place()
    barrier = greet()
    pl.semaphore_wait(barrier, PEERS + 1)

    def push(k, _):
        peer = lax.rem(cell + k, PEERS)
        remote(back, inbox, send_sem, recv_sem, peer, cell, (region, peer)).start()
        return 0
    lax.fori_loop(1, PEERS, push, 0)
    remote(back, inbox, send_sem, recv_sem, LOWER, UPPER, (below, cell)).start()
    remote(back, inbox, send_sem, recv_sem, UPPER, LOWER, (above, cell)).start()
    total[...] = jnp.zeros_like(total)

    def gather(slot, device, target):
        copy = remote(back, inbox, send_sem, recv_sem, slot, slot, device)
        copy.wait_recv()
        copy.wait_send()
        rows = inbox[slot]
        for a in range(4):
            total[a] += jnp.where(target == a, rows, 0.0)

    def finish(k, _):
        peer = lax.rem(cell + k, PEERS)
        gather(peer, (region, peer), send_ref[peer])
        return 0
    lax.fori_loop(1, PEERS, finish, 0)
    gather(LOWER, (below, cell), edge_ref[0])
    gather(UPPER, (above, cell), edge_ref[1])
    lane_id = lax.broadcasted_iota(jnp.int32, (1, 512), 1)
    for a in range(4):
        live = lane_id < counts[a]
        for k in range(3):
            accel[k, a:a + 1] = jnp.where(live, total[a, 1 + k:2 + k], 0.0)


def give_back(counts, send, edge, back):
    smem = pl.BlockSpec(memory_space=pltpu.SMEM)
    vmem = pl.BlockSpec(memory_space=pltpu.VMEM)
    return pl.pallas_call(
        return_kernel,
        out_shape=jax.ShapeDtypeStruct((3, 4, 512), F32),
        in_specs=[smem] * 3 + [pl.BlockSpec(memory_space=pl.ANY)],
        out_specs=vmem,
        scratch_shapes=[
            pltpu.VMEM((34, 4, 512), F32),
            pltpu.VMEM((4, 4, 512), F32),
            pltpu.SemaphoreType.DMA((34,)),
            pltpu.SemaphoreType.DMA((34,)),
        ],
        compiler_params=pltpu.CompilerParams(
            collective_id=1, has_side_effects=True, vmem_limit_bytes=60 * MIB
        ),
        name="give_back",
    )(counts, send, edge, back)


def on_device(
    positions, velocities, mass, smoothing, energy, counts, send_cells, local_pairs, edge_cells
):
    send = send_cells.reshape(32)
    edge = edge_cells.reshape(2)
    pairs = local_pairs[0, 0].T
    table, *local = exchange(counts, send, edge, pairs, positions, velocities, mass, smoothing)
    density, part, heat, back = compute(send, pairs, edge, table, energy, local)
    return density, part + give_back(counts, send, edge, back), heat


def solution(mesh):
    placed = (
        P(None, ("region", "cell"), None),
        P(None, ("region", "cell"), None),
        P(("region", "cell"), None),
        P(("region", "cell"), None),
        P(("region", "cell"), None),
        P(("region", "cell")),
        P("region", "cell", None, None),
        P("region", "cell", None, None),
        P("region", "cell", None),
    )
    return jax.shard_map(
        on_device,
        mesh=mesh,
        in_specs=placed,
        out_specs=(
            P(("region", "cell"), None),
            P(None, ("region", "cell"), None),
            P(("region", "cell"), None),
        ),
        check_vma=False,
    )
```

time: 89.2 us -> 82.9 us (0.929)
  the two profiles are of different devices: /device:TPU:193 before, /device:TPU:1 now
where the time goes in v3:
time: 82.9 us; the launch traced here: 81.8 us
  Pallas kernels  79.8 us (96%)
  other arithmetic  1.37 us (2%)
    pallas_call x1, Pallas kernels, exchange(): pl.pallas_call(exchange_kernel, out_shape=(jax.ShapeDtypeStruct((NSLOT, 8...  29.7 us
    pallas_call x1, Pallas kernels, compute(): pl.pallas_call(compute_kernel, out_shape=(jax.ShapeDtypeStruct((4, 512),...  29 us
    pallas_call x1, Pallas kernels, give_back(): pl.pallas_call(return_kernel, out_shape=jax.ShapeDtypeStruct((3, 4, 512),...  21.2 us

profile of v3, /device:TPU:1, one launch (start us, length us, event | category | flops | bytes accessed | tf_op | source)
XLA Modules:
  0.0 81.8 jit_solution(6696133679935633391)
XLA Ops:
  0.6 29.7 %exchange.1 = (f32[38,8,512]{2,1,0:T(8,128)}, bf16[104,128,256]{2,1,0:T(8,128)(2,1)}, f32[32,128,128]{2,1,0:T(8,128)}, f32[32,8,128]{2,1,0:T(8,128)}, f32[32,16,...) custom-call(s32[4]{0:T(128)} %counts.3, s32[32]{0:T(128)} %bitcast.5, ...), custom_call_target="tpu_custom_call" | custom-call | tf_op jit(solution)/shard_map/exchange/pallas_call | solution.py:605
  30.3 29.0 %tiles.1 = (f32[4,512]{1,0:T(4,128)}, f32[3,4,512]{2,1,0:T(4,128)}, f32[4,512]{1,0:T(4,128)}, f32[38,4,512]{2,1,0:T(4,128)}) custom-call(s32[32]{0:T(128)} %bitcast.6, s32[2,4]{1,0:T(2,128)} %bitcast.12, s32[2]{0:T(128)} %bitcast.9, f32[38,8,512]{2,1,0:T(8,128)} %get-tuple-element.15.table, f32[4,512]{1,0:T(4,128)} %energy.1, ...), custom_call_target="tpu_custom_call" | custom-call | tf_op jit(solution)/shard_map/tiles/pallas_call | solution.py:475
  59.3 21.2 %give_back.1 = f32[3,4,512]{2,1,0:T(4,128)} custom-call(s32[4]{0:T(128)} %counts.3, s32[32]{0:T(128)} %bitcast.7, s32[2]{0:T(128)} %bitcast.10, f32[38,4,512]{2,1,0:T(4,128)} %get-tuple-element.25.back), custom_call_target="tpu_custom_call" | custom-call | tf_op jit(solution)/shard_map/give_back/pallas_call | solution.py:663
  80.5 1.4 %add.3 = f32[3,4,512]{2,1,0:T(4,128)} add(f32[3,4,512]{2,1,0:T(4,128)} %get-tuple-element.24, f32[3,4,512]{2,1,0:T(4,128)} %give_back.1) | non-fusion elementwise | flops 6144 | bytes 73728 | tf_op jit(solution)/shard_map/add | solution.py:689

commit v4 on v3

--- a/solution.py
+++ b/solution.py
@@ -14,7 +14,7 @@
 LOWER, UPPER, OWN, NSLOT = 32, 33, 34, 38
 MAXT = 34
 LOCAL = 104
-GBLK = LOCAL + MAXT * 16 + 20 + 6 * U
+GBLK = MAXT * 16 + 20 + 6 * U
 ROOT = math.sqrt(24.0 / math.pi)
 MIB = 1024 * 1024
 MESH = pl.DeviceIdType.MESH
@@ -125,11 +125,14 @@
     return v[:, :128] + v[:, 128:]
 
 
-def local_tiles(pair_ref, own, feat_s, rows_s, lane_s, feat_o, s_o, m_o, rows_o, near_a, near_b,
-                gst, acc_w, row_w, acc_g, row_g):
+def local_features(own, feat_s, rows_s, lane_s, feat_o, s_o, m_o, rows_o, *_):
     for a in range(4):
         store_source(own[a], a * 4, feat_s, rows_s, lane_s)
         store_target(own[a], a * 4, feat_o, s_o, m_o, rows_o)
+
+
+def local_tiles(pair_ref, emit, feat_s, rows_s, lane_s, feat_o, s_o, m_o, rows_o, near_a, near_b,
+                gst, acc_w, row_w, acc_g, row_g):
     acc_w[...] = jnp.zeros_like(acc_w)
     row_w[...] = jnp.zeros_like(row_w)
     acc_g[...] = jnp.zeros_like(acc_g)
@@ -153,17 +156,18 @@
         both = jnp.where(self_ & (i1 == j1), 0.0, 1.0)
         return a * 4 + ib, b * 4 + jb, group * 4 + ib, group * 4 + jb, both
 
-    def distances(buf, n):
+    def group(n):
+        return tuple(where(n + u) for u in range(UL))
+
+    def distances(buf, those):
         for u in range(UL):
-            oi, sj, _, _, _ = where(n + u)
-            buf[u] = nn(feat_o[oi], feat_s[sj])
-
-    def elements(buf, n):
+            buf[u] = nn(feat_o[those[u][0]], feat_s[those[u][1]])
+
+    def elements(buf, those, n):
         for u in range(UL):
-            oi, si, gi, gj, both = where(n + u)
-            both = jnp.where(n + u < LOCAL, both, 0.0)
+            oi, si, gi, gj, both = those[u]
             sj = lane_s[si][0:1]
-            mass = jnp.where(n + u < LOCAL, lane_s[si][1:2], 0.0)
+            mass = lane_s[si][1:2]
             d2 = jnp.maximum(buf[u, :, 0:128], 1e-6)
             inv = lax.rsqrt(d2)
             pi = d2 * inv
@@ -181,39 +185,44 @@
             row_w[gj] += both * jnp.sum(back.reshape(16, 8, 128), axis=0)
             split_store(gst, n + u, (qa - qc + ra - rc) * inv)
 
-    def products(n, slot):
+    def products(those, slot):
         out = []
         for u in range(UL):
-            oi, sj, _, _, _ = where(jnp.maximum(n + u, 0))
             g = gst[slot + u]
-            out.append((nt(rows_s[sj], g), fold(nn(rows_o[oi], g))))
+            out.append((nt(rows_s[those[u][1]], g), fold(nn(rows_o[those[u][0]], g))))
         return out
 
-    def collect(sums, n):
+    def collect(sums, those):
         for u in range(UL):
-            _, _, gi, gj, both = where(jnp.maximum(n + u, 0))
-            good = (n + u >= 0) & (n + u < LOCAL)
-            acc_g[gi] += jnp.where(good, sums[u][0], 0.0)
-            row_g[gj] += jnp.where(good, sums[u][1], 0.0) * both
-
-    distances(near_a, 0)
+            _, _, gi, gj, both = those[u]
+            acc_g[gi] += sums[u][0]
+            row_g[gj] += sums[u][1] * both
+
     step = 2 * UL
 
-    def body(n, _):
+    def body(n, carry):
+        prev, now, later = carry
         base = n * step
         before = jnp.where(n == 0, LOCAL + 2 * UL, base - UL)
-        sums = products(base - UL, before)
-        elements(near_a, base)
-        distances(near_b, base + UL)
-        collect(sums, base - UL)
-        sums = products(base, base)
-        elements(near_b, base + UL)
-        distances(near_a, base + step)
-        collect(sums, base)
-        return 0
-    lax.fori_loop(0, LOCAL // step, body, 0)
-    sums = products(LOCAL - UL, LOCAL - UL)
-    collect(sums, LOCAL - UL)
+        sums = products(prev, before)
+        elements(near_a, now, base)
+        distances(near_b, later)
+        collect(sums, prev)
+        after = group(base + step)
+        sums = products(now, base)
+        elements(near_b, later, base + UL)
+        distances(near_a, after)
+        collect(sums, now)
+        return later, after, group(base + step + UL)
+
+    state = group(I32(0))
+    distances(near_a, state)
+    state = (state, state, group(I32(UL)))
+    marks = (0, 7, 14, 20, LOCAL // step)
+    for part, (low, high) in enumerate(zip(marks[:-1], marks[1:])):
+        state = lax.fori_loop(low, high, body, state)
+        emit(part, low * step, (high - low) * step)
+    collect(products(state[0], LOCAL - UL), state[0])
 
 
 LOCAL_SCRATCH = [
@@ -233,7 +242,6 @@
     pltpu.VMEM((32, 16, 128), F32),
 ]
 LOCAL_OUT = (
-    jax.ShapeDtypeStruct((LOCAL, 128, 256), BF16),
     jax.ShapeDtypeStruct((32, 128, 128), F32),
     jax.ShapeDtypeStruct((32, 8, 128), F32),
     jax.ShapeDtypeStruct((32, 16, 128), F32),
@@ -246,29 +254,26 @@
 
 def local_results(scratch):
     feat_o, s_o = scratch[3], scratch[4]
-    gst, acc_w, row_w, acc_g, row_g = scratch[9:14]
-    return gst.at[pl.ds(0, LOCAL)], acc_w, row_w, acc_g, row_g, feat_o, s_o
-
-
-def compute_kernel(send_ref, pair_ref, edge_ref, table, energy, g_in, w_in, roww_in, gg_in, rowg_in, feat_o, s_o,
-                   rho_out, acc_out, er_out, t_out,
-                   ta, ts, feat_s, rows_s, lane_s, near_a, near_b, gst, acc_g, acc_w, q_rows, q_wide,
-                   cnt_v, n_ref, w_pair, cnt_sem, g_sem, w_sem):
+    return tuple(scratch[10:14]) + (feat_o, s_o)
+
+
+def compute_kernel(send_ref, pair_ref, edge_ref, table, energy, w_in, roww_in, gg_in, rowg_in, feat_o, s_o,
+                   rho_out, acc_out, er_out, t_out, q_rows, q_wide,
+                   ta, ts, feat_s, rows_s, lane_s, near_a, near_b, gst, acc_g, acc_w,
+                   cnt_v, n_ref, w_pair, cnt_sem, w_sem):
     found = jnp.sum((table[:, 0, :] > 0.0).astype(F32), axis=1, keepdims=True)
     cnt_v[...] = jnp.broadcast_to(found, (NSLOT, 128)).astype(I32)
     fetch = pltpu.make_async_copy(cnt_v, n_ref, cnt_sem)
     fetch.start()
-    get_g = pltpu.make_async_copy(g_in, gst.at[pl.ds(0, LOCAL)], g_sem)
     get_w = pltpu.make_async_copy(w_in.at[pl.ds(0, 16)], acc_w, w_sem.at[0])
     get_p = pltpu.make_async_copy(w_in.at[pl.ds(16, 16)], w_pair, w_sem.at[1])
     get_w.start()
     get_p.start()
-    get_g.start()
     row = row_ids()
     for k in range(16):
         acc_g[k] = gg_in[k]
     for u in range(U):
-        gst[LOCAL + u] = jnp.zeros((128, 256), BF16)
+        gst[u] = jnp.zeros((128, 256), BF16)
     t_out[...] = jnp.zeros_like(t_out)
     fetch.wait()
 
@@ -336,10 +341,10 @@
             acc_w[oi] += ((ai + ai) * qa - qc * ci) * mass
             aj = jnp.maximum(sj - pj, 0.0)
             mj = jnp.minimum(pj, aj)
-            split_store(gst, LOCAL + base + U + u, (qa - qc + mj * (aj + aj - mj)) * inv)
+            split_store(gst, base + U + u, (qa - qc + mj * (aj + aj - mj)) * inv)
 
     def products(where, base):
-        return [nt(rows_s[where[u][1]], gst[LOCAL + base + U + u]) for u in range(U)]
+        return [nt(rows_s[where[u][1]], gst[base + U + u]) for u in range(U)]
 
     def collect(sums, where, base):
         for u in range(U):
@@ -369,7 +374,7 @@
     lax.fori_loop(0, steps + 1, body, (walk, first, first, second))
 
     def clear(k, _):
-        gst[LOCAL + (2 * steps + 3) * U + k] = jnp.zeros((128, 256), BF16)
+        gst[(2 * steps + 3) * U + k] = jnp.zeros((128, 256), BF16)
         return 0
     lax.fori_loop(0, 17, clear, 0)
 
@@ -417,55 +422,22 @@
             cut = slice(jb * 128, (jb + 1) * 128)
             q_wide[a * 4 + jb, :, 0:128] = plain[:, cut]
             q_wide[a * 4 + jb, :, 128:256] = plain[:, cut]
-    get_g.wait()
-
-    def settle(s, cut, o, good):
-        o = o[:8] + o[8:]
-        st = table[s][:, cut]
-        extra = st * o[0:1] - o
-        t_out[s, :, cut] += jnp.where(good, extra[0:4], 0.0)
 
     def mirror(step, base):
         for u in range(2):
             tile = 2 * step + u
             a, s, ni, nj = at(tile)
             q = q_rows[a]
+            st = table[s]
+            slot = jnp.where(tile < count, s, OWN)
             for jb in range(4):
-                g = gst[pl.ds(LOCAL + base + jb * ni, 4)].reshape(512, 256)
-                settle(s, slice(jb * 128, (jb + 1) * 128), fold(nn(q, g)), tile < count)
+                cut = slice(jb * 128, (jb + 1) * 128)
+                o = fold(nn(q, gst[pl.ds(base + jb * ni, 4)].reshape(512, 256)))
+                o = o[:8] + o[8:]
+                t_out[slot, :, cut] = (st[:, cut] * o[0:1] - o)[0:4]
             base = base + ni * nj
         return base
     lax.fori_loop(0, (count + 1) // 2, mirror, I32(U))
-
-    for a in range(4):
-        ti = ROOT / (table[OWN + a][7:8] * table[OWN + a][7:8] * table[OWN + a][7:8])
-        for jb in range(4):
-            first = a * 10 + (jb * (jb + 1)) // 2
-            cut = slice(jb * 128, (jb + 1) * 128)
-            g = gst[pl.ds(first, jb + 1)].reshape((jb + 1) * 128, 256)
-            o = fold(nn(q_rows[a, :, 0:(jb + 1) * 128], g))
-            for other in range(jb + 1, 4):
-                at_ = a * 10 + (other * (other + 1)) // 2 + jb
-                o = o + nt(q_wide[a * 4 + other], gst[at_]) * ti[:, cut]
-            settle(OWN + a, cut, o, True)
-    for k in range(4):
-        ka, kb = pair_ref[0, k], pair_ref[1, k]
-        hk = table[OWN + ka][7:8]
-        ti = ROOT / (hk * hk * hk)
-        for jb in range(4):
-            cut = slice(jb * 128, (jb + 1) * 128)
-            first = 40 + k * 16
-            g = gst[pl.ds(first + jb * 4, 4)].reshape(512, 256)
-            settle(OWN + kb, cut, fold(nn(q_rows[ka], g)), True)
-            o = nt(q_wide[kb * 4], gst[first + jb])
-            for other in range(1, 4):
-                o = o + nt(q_wide[kb * 4 + other], gst[first + other * 4 + jb])
-            settle(OWN + ka, cut, o * ti[:, cut], True)
-
-    for a in range(4):
-        live = lane_id < n_ref[OWN + a, 0]
-        for k in range(3):
-            acc_out[k, a:a + 1] += jnp.where(live, t_out[OWN + a, 1 + k:2 + k], 0.0)
 
 
 def compute(send, pairs, edge, table, energy, local):
@@ -478,10 +450,12 @@
             jax.ShapeDtypeStruct((4, 512), F32),
             jax.ShapeDtypeStruct((3, 4, 512), F32),
             jax.ShapeDtypeStruct((4, 512), F32),
-            jax.ShapeDtypeStruct((NSLOT, 4, 512), F32),
+            jax.ShapeDtypeStruct((OWN + 1, 4, 512), F32),
+            jax.ShapeDtypeStruct((4, 16, 512), BF16),
+            jax.ShapeDtypeStruct((16, 16, 256), BF16),
         ),
-        in_specs=[smem] * 3 + [vmem] * 2 + [hbm] * 2 + [vmem] * 5,
-        out_specs=(vmem,) * 4,
+        in_specs=[smem] * 3 + [vmem] * 2 + [hbm] + [vmem] * 5,
+        out_specs=(vmem,) * 6,
         scratch_shapes=[
             pltpu.SMEM((MAXT + 2,), I32),
             pltpu.SMEM((MAXT + 2,), I32),
@@ -493,18 +467,60 @@
             pltpu.VMEM((GBLK, 128, 256), BF16),
             pltpu.VMEM((16, 16, 128), F32),
             pltpu.VMEM((16, 128, 128), F32),
-            pltpu.VMEM((4, 16, 512), BF16),
-            pltpu.VMEM((16, 16, 256), BF16),
             pltpu.VMEM((NSLOT, 128), I32),
             pltpu.SMEM((NSLOT, 128), I32),
             pltpu.VMEM((16, 128, 128), F32),
-            pltpu.SemaphoreType.DMA,
             pltpu.SemaphoreType.DMA,
             pltpu.SemaphoreType.DMA((2,)),
         ],
         compiler_params=pltpu.CompilerParams(vmem_limit_bytes=62 * MIB),
         name="tiles",
     )(send, pairs, edge, table, energy, *local)
+
+
+def local_mirror(pair_ref, own, gst, q_rows, q_wide, self_t, pair_t):
+    def scale(st):
+        return ROOT / (st[7:8] * st[7:8] * st[7:8])
+
+    def settle(st, parts):
+        o = jnp.concatenate(parts, axis=1)
+        o = o[:8] + o[8:]
+        return st * o[0:1] - o
+
+    def one_cell(a, _):
+        st = own[a]
+        ti = scale(st)
+        parts = []
+        for jb in range(4):
+            first = a * 10 + (jb * (jb + 1)) // 2
+            g = gst[pl.ds(first, jb + 1)].reshape((jb + 1) * 128, 256)
+            o = fold(nn(q_rows[a, :, 0:(jb + 1) * 128], g))
+            for other in range(jb + 1, 4):
+                block = gst[a * 10 + (other * (other + 1)) // 2 + jb]
+                o = o + nt(q_wide[a * 4 + other], block) * ti[:, jb * 128:(jb + 1) * 128]
+            parts.append(o)
+        self_t[a] = settle(st, parts)
+        return 0
+    lax.fori_loop(0, 4, one_cell, 0)
+
+    def one_pair(k, _):
+        ka, kb = pair_ref[0, k], pair_ref[1, k]
+        first = 40 + k * 16
+        there, here = [], []
+        q = q_rows[ka]
+        wide = [q_wide[kb * 4 + other] for other in range(4)]
+        for jb in range(4):
+            there.append(fold(nn(q, gst[pl.ds(first + jb * 4, 4)].reshape(512, 256))))
+            o = nt(wide[0], gst[first + jb])
+            for other in range(1, 4):
+                o = o + nt(wide[other], gst[first + other * 4 + jb])
+            here.append(o)
+        st = own[ka]
+        ti = scale(st)
+        pair_t[k] = settle(st, [here[jb] * ti[:, jb * 128:(jb + 1) * 128] for jb in range(4)])
+        pair_t[4 + k] = settle(own[kb], there)
+        return 0
+    lax.fori_loop(0, 4, one_pair, 0)
 
 
 def place():
@@ -538,7 +554,7 @@
     )
 
 
-def exchange_kernel(counts, send_ref, edge_ref, pair_ref, positions, velocities, mass, smoothing, table, *refs):
+def exchange_kernel(counts, send_ref, edge_ref, pair_ref, positions, velocities, mass, smoothing, table, g_out, *refs):
     outs, scratch = refs[:NLOCAL], refs[NLOCAL:-5]
     own, payload, send_sem, recv_sem, local_sem = refs[-5:]
     region, cell, below, above = place()
@@ -560,6 +576,7 @@
     payload[UPPER] = own[edge_ref[1]] * high
     payload[cell] = jnp.zeros((8, 512), F32)
     pltpu.make_async_copy(payload.at[cell], table.at[cell], local_sem.at[4]).start()
+    local_features(own, *scratch)
     pl.semaphore_wait(barrier, PEERS + 1)
     remote(payload, table, send_sem, recv_sem, LOWER, UPPER, (below, cell)).start()
     remote(payload, table, send_sem, recv_sem, UPPER, LOWER, (above, cell)).start()
@@ -572,12 +589,22 @@
         return 0
     lax.fori_loop(1, PEERS, push, 0)
 
-    local_tiles(pair_ref, own, *scratch)
     copies = [
         pltpu.make_async_copy(src, dst, local_sem.at[5 + i])
         for i, (src, dst) in enumerate(zip(local_results(scratch), outs))
     ]
-    for copy in copies:
+    for copy in copies[4:]:
+        copy.start()
+
+    def emit(part, first, size):
+        copy = pltpu.make_async_copy(
+            scratch[9].at[pl.ds(first, size)], g_out.at[pl.ds(first, size)], local_sem.at[5 + NLOCAL + part]
+        )
+        copy.start()
+        copies.append(copy)
+
+    local_tiles(pair_ref, emit, *scratch)
+    for copy in copies[:4]:
         copy.start()
     for k in range(4):
         pltpu.make_async_copy(own.at[k], table.at[OWN + k], local_sem.at[k]).wait()
@@ -604,15 +631,18 @@
     hbm = pl.BlockSpec(memory_space=pl.ANY)
     return pl.pallas_call(
         exchange_kernel,
-        out_shape=(jax.ShapeDtypeStruct((NSLOT, 8, 512), F32),) + LOCAL_OUT,
+        out_shape=(
+            jax.ShapeDtypeStruct((NSLOT, 8, 512), F32),
+            jax.ShapeDtypeStruct((LOCAL, 128, 256), BF16),
+        ) + LOCAL_OUT,
         in_specs=[smem] * 4 + [vmem] * 4,
-        out_specs=(hbm,) * (1 + NLOCAL),
+        out_specs=(hbm,) * (2 + NLOCAL),
         scratch_shapes=LOCAL_SCRATCH + [
             pltpu.VMEM((4, 8, 512), F32),
             pltpu.VMEM((34, 8, 512), F32),
             pltpu.SemaphoreType.DMA((34,)),
             pltpu.SemaphoreType.DMA((34,)),
-            pltpu.SemaphoreType.DMA((5 + NLOCAL,)),
+            pltpu.SemaphoreType.DMA((9 + NLOCAL,)),
         ],
         compiler_params=pltpu.CompilerParams(
             collective_id=0, has_side_effects=True, vmem_limit_bytes=60 * MIB
@@ -621,8 +651,13 @@
     )(counts, send, edge, pairs, positions, velocities, mass, smoothing)
 
 
-def return_kernel(counts, send_ref, edge_ref, back, accel, inbox, total, send_sem, recv_sem):
+def return_kernel(counts, send_ref, edge_ref, pair_ref, back, table, g_in, q_rows, q_wide, accel,
+                  inbox, total, own, gst, self_t, pair_t, send_sem, recv_sem, local_sem):
     region, cell, below, above = place()
+    get_own = pltpu.make_async_copy(table.at[pl.ds(OWN, 4)], own, local_sem.at[0])
+    get_g = pltpu.make_async_copy(g_in, gst, local_sem.at[1])
+    get_own.start()
+    get_g.start()
     barrier = greet()
     pl.semaphore_wait(barrier, PEERS + 1)
 
@@ -633,7 +668,16 @@
     lax.fori_loop(1, PEERS, push, 0)
     remote(back, inbox, send_sem, recv_sem, LOWER, UPPER, (below, cell)).start()
     remote(back, inbox, send_sem, recv_sem, UPPER, LOWER, (above, cell)).start()
-    total[...] = jnp.zeros_like(total)
+
+    get_own.wait()
+    get_g.wait()
+    local_mirror(pair_ref, own, gst, q_rows, q_wide, self_t, pair_t)
+    for a in range(4):
+        t = self_t[a]
+        for k in range(4):
+            t = t + jnp.where(pair_ref[0, k] == a, pair_t[k], 0.0)
+            t = t + jnp.where(pair_ref[1, k] == a, pair_t[4 + k], 0.0)
+        total[a] = t[0:4]
 
     def gather(slot, device, target):
         copy = remote(back, inbox, send_sem, recv_sem, slot, slot, device)
@@ -650,32 +694,38 @@
     lax.fori_loop(1, PEERS, finish, 0)
     gather(LOWER, (below, cell), edge_ref[0])
     gather(UPPER, (above, cell), edge_ref[1])
-    lane_id = lax.broadcasted_iota(jnp.int32, (1, 512), 1)
+    lane_id = lax.broadcasted_iota(I32, (1, 512), 1)
     for a in range(4):
         live = lane_id < counts[a]
         for k in range(3):
             accel[k, a:a + 1] = jnp.where(live, total[a, 1 + k:2 + k], 0.0)
 
 
-def give_back(counts, send, edge, back):
+def give_back(counts, send, edge, pairs, back, table, g, q_rows, q_wide):
     smem = pl.BlockSpec(memory_space=pltpu.SMEM)
     vmem = pl.BlockSpec(memory_space=pltpu.VMEM)
+    hbm = pl.BlockSpec(memory_space=pl.ANY)
     return pl.pallas_call(
         return_kernel,
         out_shape=jax.ShapeDtypeStruct((3, 4, 512), F32),
-        in_specs=[smem] * 3 + [pl.BlockSpec(memory_space=pl.ANY)],
+        in_specs=[smem] * 4 + [hbm] * 3 + [vmem] * 2,
         out_specs=vmem,
         scratch_shapes=[
             pltpu.VMEM((34, 4, 512), F32),
             pltpu.VMEM((4, 4, 512), F32),
+            pltpu.VMEM((4, 8, 512), F32),
+            pltpu.VMEM((LOCAL, 128, 256), BF16),
+            pltpu.VMEM((4, 8, 512), F32),
+            pltpu.VMEM((8, 8, 512), F32),
             pltpu.SemaphoreType.DMA((34,)),
             pltpu.SemaphoreType.DMA((34,)),
+            pltpu.SemaphoreType.DMA((2,)),
         ],
         compiler_params=pltpu.CompilerParams(
             collective_id=1, has_side_effects=True, vmem_limit_bytes=60 * MIB
         ),
         name="give_back",
-    )(counts, send, edge, back)
+    )(counts, send, edge, pairs, back, table, g, q_rows, q_wide)
 
 
 def on_device(
@@ -684,9 +734,10 @@
     send = send_cells.reshape(32)
     edge = edge_cells.reshape(2)
     pairs = local_pairs[0, 0].T
-    table, *local = exchange(counts, send, edge, pairs, positions, velocities, mass, smoothing)
-    density, part, heat, back = compute(send, pairs, edge, table, energy, local)
-    return density, part + give_back(counts, send, edge, back), heat
+    table, g, *local = exchange(counts, send, edge, pairs, positions, velocities, mass, smoothing)
+    density, part, heat, back, q_rows, q_wide = compute(send, pairs, edge, table, energy, local)
+    extra = give_back(counts, send, edge, pairs, back, table, g, q_rows, q_wide)
+    return density, part + extra, heat
 
 
 def solution(mesh):

time: 82.9 us -> 72.6 us (0.88)
  Pallas kernels: 79.8 us -> 70.3 us
    pallas_call x1, Pallas kernels: 29.7 us -> 23.8 us  [exchange(): pl.pallas_call(exchange_kernel, out_shape=(jax.ShapeDtypeStruct((NSLOT, 8...]
    pallas_call x1, Pallas kernels: 21.2 us -> 18.9 us  [give_back(): pl.pallas_call(return_kernel, out_shape=jax.ShapeDtypeStruct((3, 4, 512),...]
    pallas_call x1, Pallas kernels: 29 us -> 27.5 us  [compute(): pl.pallas_call(compute_kernel, out_shape=(jax.ShapeDtypeStruct((4, 512),...]
where the time goes in v4:
time: 72.6 us; the launch traced here: 72.3 us
  Pallas kernels  70.3 us (97%)
  other arithmetic  1.35 us (2%)
    pallas_call x1, Pallas kernels, compute(): pl.pallas_call(compute_kernel, out_shape=(jax.ShapeDtypeStruct((4, 512),...  27.5 us
    pallas_call x1, Pallas kernels, exchange(): pl.pallas_call(exchange_kernel, out_shape=(jax.ShapeDtypeStruct((NSLOT, 8...  23.8 us
    pallas_call x1, Pallas kernels, give_back(): pl.pallas_call(return_kernel, out_shape=jax.ShapeDtypeStruct((3, 4, 512),...  18.9 us

profile of v4, /device:TPU:1, one launch (start us, length us, event | category | flops | bytes accessed | tf_op | source)
XLA Modules:
  0.0 72.3 jit_solution(9623778354739170381)
XLA Ops:
  0.6 23.8 %exchange.1 = (f32[38,8,512]{2,1,0:T(8,128)}, bf16[104,128,256]{2,1,0:T(8,128)(2,1)}, f32[32,128,128]{2,1,0:T(8,128)}, f32[32,8,128]{2,1,0:T(8,128)}, f32[32,16,...) custom-call(s32[4]{0:T(128)} %counts.3, s32[32]{0:T(128)} %bitcast.8, ...), custom_call_target="tpu_custom_call" | custom-call | tf_op jit(solution)/shard_map/exchange/pallas_call | solution.py:632
  24.5 27.5 %tiles.1 = (f32[4,512]{1,0:T(4,128)}, f32[3,4,512]{2,1,0:T(4,128)}, f32[4,512]{1,0:T(4,128)}, f32[35,4,512]{2,1,0:T(4,128)}, bf16[4,16,512]{2,1,0:T(8,128)(2,1)}, /*index=5*/bf16[16,16,256]{2,1,0:T(8,128)(2,1)}) custom-call(s32[32]{0:T(128)} %bitcast.9, s32[2,4]{1,0:T(2,128)} %bitcast.6, s32[2]{0:T(128)} %bitcast.12, f32[38,8,512]{2,1,0:T(8,128)} %get-tuple-element.17.table, ...), custom_call_target="tpu_custom_call" | custom-call | tf_op jit(solution)/shard_map/tiles/pallas_call | solution.py:447
  52.0 0.0 copy-start
  52.0 18.9 %give_back.1 = f32[3,4,512]{2,1,0:T(4,128)} custom-call(s32[4]{0:T(128)} %counts.3, s32[32]{0:T(128)} %bitcast.10, s32[2]{0:T(128)} %bitcast.13, s32[2,4]{1,0:T(2,128)} %bitcast.7, f32[35,4,512]{2,1,0:T(4,128)} %get-tuple-element.26.back, f32[38,8,512]{2,1,0:T(8,128)} %get-tuple-element.17.table, bf16[104,128,256]{2,1,0:T(8,128)(2,1)} %get-tuple-element.27.g_in, ...), custom_call_target="tpu_custom_call" | custom-call | tf_op jit(solution)/shard_map/give_back/pallas_call | solution.py:708
  70.9 0.0 copy-done
  70.9 1.4 %add.3 = f32[3,4,512]{2,1,0:T(4,128)} add(f32[3,4,512]{2,1,0:T(4,128)S(1)} %copy-done, f32[3,4,512]{2,1,0:T(4,128)} %give_back.1) | non-fusion elementwise | flops 6144 | bytes 73728 | tf_op jit(solution)/shard_map/add | solution.py:740
Async XLA Ops:
  52.0 19.0 %copy-start = (f32[3,4,512]{2,1,0:T(4,128)S(1)}, f32[3,4,512]{2,1,0:T(4,128)}, u32[]{:S(2)}) copy-start(f32[3,4,512]{2,1,0:T(4,128)} %get-tuple-element.25) | copy-start | bytes 73732

commit v5 on v4

--- a/solution.py
+++ b/solution.py
@@ -1,3 +1,4 @@
+import functools
 import math
 import jax
 import jax.numpy as jnp
@@ -9,7 +10,7 @@
 GAMMA = 5.0 / 3.0
 F32, BF16, I32 = jnp.float32, jnp.bfloat16, jnp.int32
 U = 3
-UL = 2
+UL = 4
 PEERS = 32
 LOWER, UPPER, OWN, NSLOT = 32, 33, 34, 38
 MAXT = 34
@@ -213,15 +214,14 @@
         elements(near_b, later, base + UL)
         distances(near_a, after)
         collect(sums, now)
+        for part, (_, last, _, _) in enumerate(PARTS):
+            pl.when(n == last // step - 1)(functools.partial(emit, part))
         return later, after, group(base + step + UL)
 
     state = group(I32(0))
     distances(near_a, state)
     state = (state, state, group(I32(UL)))
-    marks = (0, 7, 14, 20, LOCAL // step)
-    for part, (low, high) in enumerate(zip(marks[:-1], marks[1:])):
-        state = lax.fori_loop(low, high, body, state)
-        emit(part, low * step, (high - low) * step)
+    state = lax.fori_loop(0, LOCAL // step, body, state)
     collect(products(state[0], LOCAL - UL), state[0])
 
 
@@ -257,10 +257,19 @@
     return tuple(scratch[10:14]) + (feat_o, s_o)
 
 
-def compute_kernel(send_ref, pair_ref, edge_ref, table, energy, w_in, roww_in, gg_in, rowg_in, feat_o, s_o,
+PARTS = ((0, 40, 0, 16),) + tuple((40 + 16 * k, 56 + 16 * k, 16 + 4 * k, 4) for k in range(4))
+
+
+def compute_kernel(send_ref, pair_ref, edge_ref, table, energy_in, w_in, roww_h, gg_h, rowg_h, feat_h, s_h,
                    rho_out, acc_out, er_out, t_out, q_rows, q_wide,
                    ta, ts, feat_s, rows_s, lane_s, near_a, near_b, gst, acc_g, acc_w,
-                   cnt_v, n_ref, w_pair, cnt_sem, w_sem):
+                   cnt_v, n_ref, w_pair, energy, roww_in, gg_in, rowg_in, feat_o, s_o, cnt_sem, w_sem, in_sem):
+    moves = [
+        pltpu.make_async_copy(src, dst, in_sem.at[i])
+        for i, (src, dst) in enumerate(
+            ((feat_h, feat_o), (s_h, s_o), (gg_h, gg_in), (energy_in, energy), (roww_h, roww_in), (rowg_h, rowg_in))
+        )
+    ]
     found = jnp.sum((table[:, 0, :] > 0.0).astype(F32), axis=1, keepdims=True)
     cnt_v[...] = jnp.broadcast_to(found, (NSLOT, 128)).astype(I32)
     fetch = pltpu.make_async_copy(cnt_v, n_ref, cnt_sem)
@@ -268,10 +277,13 @@
     get_w = pltpu.make_async_copy(w_in.at[pl.ds(0, 16)], acc_w, w_sem.at[0])
     get_p = pltpu.make_async_copy(w_in.at[pl.ds(16, 16)], w_pair, w_sem.at[1])
     get_w.start()
+    for move in moves[:3]:
+        move.start()
     get_p.start()
+    for move in moves[3:]:
+        move.start()
     row = row_ids()
-    for k in range(16):
-        acc_g[k] = gg_in[k]
+    acc_g[...] = jnp.zeros_like(acc_g)
     for u in range(U):
         gst[u] = jnp.zeros((128, 256), BF16)
     t_out[...] = jnp.zeros_like(t_out)
@@ -298,6 +310,8 @@
         return 0
     lax.fori_loop(0, (count + 1) // 2, source_loop, 0)
     get_w.wait()
+    for move in moves[:2]:
+        move.wait()
 
     def at(tile):
         a, s = ta[tile], ts[tile]
@@ -379,6 +393,10 @@
     lax.fori_loop(0, 17, clear, 0)
 
     get_p.wait()
+    for move in moves[2:]:
+        move.wait()
+    for k in range(16):
+        acc_g[k] += gg_in[k]
     lane_id = lax.broadcasted_iota(I32, (1, 512), 1)
     row_sum = [None] * 4
     flat = [None] * 4
@@ -454,7 +472,7 @@
             jax.ShapeDtypeStruct((4, 16, 512), BF16),
             jax.ShapeDtypeStruct((16, 16, 256), BF16),
         ),
-        in_specs=[smem] * 3 + [vmem] * 2 + [hbm] + [vmem] * 5,
+        in_specs=[smem] * 3 + [vmem] + [hbm] * 7,
         out_specs=(vmem,) * 6,
         scratch_shapes=[
             pltpu.SMEM((MAXT + 2,), I32),
@@ -470,8 +488,15 @@
             pltpu.VMEM((NSLOT, 128), I32),
             pltpu.SMEM((NSLOT, 128), I32),
             pltpu.VMEM((16, 128, 128), F32),
+            pltpu.VMEM((4, 512), F32),
+            pltpu.VMEM((32, 8, 128), F32),
+            pltpu.VMEM((32, 16, 128), F32),
+            pltpu.VMEM((32, 16, 128), F32),
+            pltpu.VMEM((16, 128, 48), BF16),
+            pltpu.VMEM((16, 128, 128), F32),
             pltpu.SemaphoreType.DMA,
             pltpu.SemaphoreType.DMA((2,)),
+            pltpu.SemaphoreType.DMA((6,)),
         ],
         compiler_params=pltpu.CompilerParams(vmem_limit_bytes=62 * MIB),
         name="tiles",
@@ -554,11 +579,19 @@
     )
 
 
-def exchange_kernel(counts, send_ref, edge_ref, pair_ref, positions, velocities, mass, smoothing, table, g_out, *refs):
-    outs, scratch = refs[:NLOCAL], refs[NLOCAL:-5]
-    own, payload, send_sem, recv_sem, local_sem = refs[-5:]
+def exchange_kernel(*refs):
+    arrived, table, g_out = refs[:8], refs[8], refs[9]
+    outs, scratch = refs[10:10 + NLOCAL], refs[10 + NLOCAL:-14]
+    own, payload = refs[-14:-12]
+    held, send_sem, recv_sem, local_sem, in_sem = refs[-12:-4], refs[-4], refs[-3], refs[-2], refs[-1]
+    moves = [pltpu.make_async_copy(src, dst, in_sem.at[i]) for i, (src, dst) in enumerate(zip(arrived, held))]
+    for move in moves:
+        move.start()
     region, cell, below, above = place()
     barrier = greet()
+    for move in moves:
+        move.wait()
+    counts, send_ref, edge_ref, pair_ref, positions, velocities, mass, smoothing = held
     lane_id = lax.broadcasted_iota(I32, (1, 512), 1)
     for k in range(4):
         live = lane_id < counts[k]
@@ -589,22 +622,32 @@
         return 0
     lax.fori_loop(1, PEERS, push, 0)
 
-    copies = [
-        pltpu.make_async_copy(src, dst, local_sem.at[5 + i])
-        for i, (src, dst) in enumerate(zip(local_results(scratch), outs))
+    acc_w, row_w, acc_g, row_g, feat_o, s_o = local_results(scratch)
+    first = [
+        pltpu.make_async_copy(feat_o, outs[4], local_sem.at[5]),
+        pltpu.make_async_copy(s_o, outs[5], local_sem.at[6]),
     ]
-    for copy in copies[4:]:
+    rest = [
+        pltpu.make_async_copy(src, dst, local_sem.at[7 + i])
+        for i, (src, dst) in enumerate(((row_w, outs[1]), (acc_g, outs[2]), (row_g, outs[3])))
+    ]
+    for copy in first:
         copy.start()
 
-    def emit(part, first, size):
-        copy = pltpu.make_async_copy(
-            scratch[9].at[pl.ds(first, size)], g_out.at[pl.ds(first, size)], local_sem.at[5 + NLOCAL + part]
+    def part_copies(part):
+        low, high, group, size = PARTS[part]
+        blocks, groups = pl.ds(low, high - low), pl.ds(group, size)
+        return (
+            pltpu.make_async_copy(scratch[9].at[blocks], g_out.at[blocks], local_sem.at[10 + 2 * part]),
+            pltpu.make_async_copy(acc_w.at[groups], outs[0].at[groups], local_sem.at[11 + 2 * part]),
         )
-        copy.start()
-        copies.append(copy)
+
+    def emit(part):
+        for copy in part_copies(part):
+            copy.start()
 
     local_tiles(pair_ref, emit, *scratch)
-    for copy in copies[:4]:
+    for copy in rest:
         copy.start()
     for k in range(4):
         pltpu.make_async_copy(own.at[k], table.at[OWN + k], local_sem.at[k]).wait()
@@ -621,13 +664,14 @@
         copy = remote(payload, table, send_sem, recv_sem, slot, slot, device)
         copy.wait_recv()
         copy.wait_send()
-    for copy in copies:
+    for copy in first + rest:
         copy.wait()
+    for part in range(len(PARTS)):
+        for copy in part_copies(part):
+            copy.wait()
 
 
 def exchange(counts, send, edge, pairs, positions, velocities, mass, smoothing):
-    smem = pl.BlockSpec(memory_space=pltpu.SMEM)
-    vmem = pl.BlockSpec(memory_space=pltpu.VMEM)
     hbm = pl.BlockSpec(memory_space=pl.ANY)
     return pl.pallas_call(
         exchange_kernel,
@@ -635,14 +679,23 @@
             jax.ShapeDtypeStruct((NSLOT, 8, 512), F32),
             jax.ShapeDtypeStruct((LOCAL, 128, 256), BF16),
         ) + LOCAL_OUT,
-        in_specs=[smem] * 4 + [vmem] * 4,
+        in_specs=[hbm] * 8,
         out_specs=(hbm,) * (2 + NLOCAL),
         scratch_shapes=LOCAL_SCRATCH + [
             pltpu.VMEM((4, 8, 512), F32),
             pltpu.VMEM((34, 8, 512), F32),
+            pltpu.SMEM((4,), I32),
+            pltpu.SMEM((32,), I32),
+            pltpu.SMEM((2,), I32),
+            pltpu.SMEM((2, 4), I32),
+            pltpu.VMEM((3, 4, 512), F32),
+            pltpu.VMEM((3, 4, 512), F32),
+            pltpu.VMEM((4, 512), F32),
+            pltpu.VMEM((4, 512), F32),
             pltpu.SemaphoreType.DMA((34,)),
             pltpu.SemaphoreType.DMA((34,)),
-            pltpu.SemaphoreType.DMA((9 + NLOCAL,)),
+            pltpu.SemaphoreType.DMA((20,)),
+            pltpu.SemaphoreType.DMA((8,)),
         ],
         compiler_params=pltpu.CompilerParams(
             collective_id=0, has_side_effects=True, vmem_limit_bytes=60 * MIB
@@ -651,14 +704,21 @@
     )(counts, send, edge, pairs, positions, velocities, mass, smoothing)
 
 
-def return_kernel(counts, send_ref, edge_ref, pair_ref, back, table, g_in, q_rows, q_wide, accel,
-                  inbox, total, own, gst, self_t, pair_t, send_sem, recv_sem, local_sem):
+def return_kernel(counts_h, send_h, edge_h, pair_h, back, table, g_in, q_in, wide_in, accel,
+                  inbox, own, gst, self_t, pair_t, counts, send_ref, edge_ref, pair_ref, q_rows, q_wide,
+                  send_sem, recv_sem, local_sem):
+    moves = [
+        pltpu.make_async_copy(src, dst, local_sem.at[i])
+        for i, (src, dst) in enumerate((
+            (table.at[pl.ds(OWN, 4)], own), (g_in, gst), (q_in, q_rows), (wide_in, q_wide),
+            (counts_h, counts), (send_h, send_ref), (edge_h, edge_ref), (pair_h, pair_ref),
+        ))
+    ]
     region, cell, below, above = place()
-    get_own = pltpu.make_async_copy(table.at[pl.ds(OWN, 4)], own, local_sem.at[0])
-    get_g = pltpu.make_async_copy(g_in, gst, local_sem.at[1])
-    get_own.start()
-    get_g.start()
     barrier = greet()
+    for move in moves:
+        move.start()
+    inbox[cell] = jnp.zeros((4, 512), F32)
     pl.semaphore_wait(barrier, PEERS + 1)
 
     def push(k, _):
@@ -669,57 +729,70 @@
     remote(back, inbox, send_sem, recv_sem, LOWER, UPPER, (below, cell)).start()
     remote(back, inbox, send_sem, recv_sem, UPPER, LOWER, (above, cell)).start()
 
-    get_own.wait()
-    get_g.wait()
+    for move in moves:
+        move.wait()
     local_mirror(pair_ref, own, gst, q_rows, q_wide, self_t, pair_t)
+
+    def arrived(k, _):
+        peer = lax.rem(cell + k, PEERS)
+        remote(back, inbox, send_sem, recv_sem, peer, peer, (region, peer)).wait_recv()
+        return 0
+    lax.fori_loop(1, PEERS, arrived, 0)
+    edges = [
+        remote(back, inbox, send_sem, recv_sem, slot, slot, device)
+        for slot, device in ((LOWER, (below, cell)), (UPPER, (above, cell)))
+    ]
+    for copy in edges:
+        copy.wait_recv()
+    total = []
     for a in range(4):
         t = self_t[a]
         for k in range(4):
             t = t + jnp.where(pair_ref[0, k] == a, pair_t[k], 0.0)
             t = t + jnp.where(pair_ref[1, k] == a, pair_t[4 + k], 0.0)
-        total[a] = t[0:4]
-
-    def gather(slot, device, target):
-        copy = remote(back, inbox, send_sem, recv_sem, slot, slot, device)
-        copy.wait_recv()
-        copy.wait_send()
+        total.append(t[0:4])
+    for slot in range(34):
+        target = send_ref[slot] if slot < PEERS else edge_ref[slot - PEERS]
         rows = inbox[slot]
         for a in range(4):
-            total[a] += jnp.where(target == a, rows, 0.0)
-
-    def finish(k, _):
-        peer = lax.rem(cell + k, PEERS)
-        gather(peer, (region, peer), send_ref[peer])
-        return 0
-    lax.fori_loop(1, PEERS, finish, 0)
-    gather(LOWER, (below, cell), edge_ref[0])
-    gather(UPPER, (above, cell), edge_ref[1])
+            total[a] = total[a] + jnp.where(target == a, rows, 0.0)
     lane_id = lax.broadcasted_iota(I32, (1, 512), 1)
     for a in range(4):
         live = lane_id < counts[a]
         for k in range(3):
-            accel[k, a:a + 1] = jnp.where(live, total[a, 1 + k:2 + k], 0.0)
+            accel[k, a:a + 1] = jnp.where(live, total[a][1 + k:2 + k], 0.0)
+
+    def left(k, _):
+        peer = lax.rem(cell + k, PEERS)
+        remote(back, inbox, send_sem, recv_sem, peer, peer, (region, peer)).wait_send()
+        return 0
+    lax.fori_loop(1, PEERS, left, 0)
+    for copy in edges:
+        copy.wait_send()
 
 
 def give_back(counts, send, edge, pairs, back, table, g, q_rows, q_wide):
-    smem = pl.BlockSpec(memory_space=pltpu.SMEM)
-    vmem = pl.BlockSpec(memory_space=pltpu.VMEM)
     hbm = pl.BlockSpec(memory_space=pl.ANY)
     return pl.pallas_call(
         return_kernel,
         out_shape=jax.ShapeDtypeStruct((3, 4, 512), F32),
-        in_specs=[smem] * 4 + [hbm] * 3 + [vmem] * 2,
-        out_specs=vmem,
+        in_specs=[hbm] * 9,
+        out_specs=pl.BlockSpec(memory_space=pltpu.VMEM),
         scratch_shapes=[
             pltpu.VMEM((34, 4, 512), F32),
-            pltpu.VMEM((4, 4, 512), F32),
             pltpu.VMEM((4, 8, 512), F32),
             pltpu.VMEM((LOCAL, 128, 256), BF16),
             pltpu.VMEM((4, 8, 512), F32),
             pltpu.VMEM((8, 8, 512), F32),
+            pltpu.SMEM((4,), I32),
+            pltpu.SMEM((32,), I32),
+            pltpu.SMEM((2,), I32),
+            pltpu.SMEM((2, 4), I32),
+            pltpu.VMEM((4, 16, 512), BF16),
+            pltpu.VMEM((16, 16, 256), BF16),
             pltpu.SemaphoreType.DMA((34,)),
             pltpu.SemaphoreType.DMA((34,)),
-            pltpu.SemaphoreType.DMA((2,)),
+            pltpu.SemaphoreType.DMA((8,)),
         ],
         compiler_params=pltpu.CompilerParams(
             collective_id=1, has_side_effects=True, vmem_limit_bytes=60 * MIB

time: 72.6 us -> 71.3 us (0.982)
  Pallas kernels: 70.3 us -> 69.1 us
    pallas_call x1, Pallas kernels: 18.9 us -> 22.2 us  [give_back(): pl.pallas_call(return_kernel, out_shape=jax.ShapeDtypeStruct((3, 4, 512),...]
    pallas_call x1, Pallas kernels: 23.8 us -> 21.6 us  [exchange(): pl.pallas_call(exchange_kernel, out_shape=(jax.ShapeDtypeStruct((NSLOT, 8...]
    pallas_call x1, Pallas kernels: 27.5 us -> 25.3 us  [compute(): pl.pallas_call(compute_kernel, out_shape=(jax.ShapeDtypeStruct((4, 512),...]
where the time goes in v5:
time: 71.3 us; the launch traced here: 71.1 us
  Pallas kernels  69.1 us (97%)
  other arithmetic  1.35 us (2%)
    pallas_call x1, Pallas kernels, compute(): pl.pallas_call(compute_kernel, out_shape=(jax.ShapeDtypeStruct((4, 512),...  25.3 us
    pallas_call x1, Pallas kernels, give_back(): pl.pallas_call(return_kernel, out_shape=jax.ShapeDtypeStruct((3, 4, 512),...  22.2 us
    pallas_call x1, Pallas kernels, exchange(): pl.pallas_call(exchange_kernel, out_shape=(jax.ShapeDtypeStruct((NSLOT, 8...  21.6 us

profile of v5, /device:TPU:1, one launch (start us, length us, event | category | flops | bytes accessed | tf_op | source)
XLA Modules:
  0.0 71.1 jit_solution(627272357512387596)
XLA Ops:
  0.6 21.6 %exchange.1 = (f32[38,8,512]{2,1,0:T(8,128)}, bf16[104,128,256]{2,1,0:T(8,128)(2,1)}, f32[32,128,128]{2,1,0:T(8,128)}, f32[32,8,128]{2,1,0:T(8,128)}, f32[32,16,...) custom-call(s32[4]{0:T(128)} %counts_h.1, s32[32]{0:T(128)} %bitcast.8, ...), custom_call_target="tpu_custom_call" | custom-call | tf_op jit(solution)/shard_map/exchange/pallas_call | solution.py:676
  22.2 25.3 %tiles.1 = (f32[4,512]{1,0:T(4,128)}, f32[3,4,512]{2,1,0:T(4,128)}, f32[4,512]{1,0:T(4,128)}, f32[35,4,512]{2,1,0:T(4,128)}, bf16[4,16,512]{2,1,0:T(8,128)(2,1)}, /*index=5*/bf16[16,16,256]{2,1,0:T(8,128)(2,1)}) custom-call(s32[32]{0:T(128)} %bitcast.9, s32[2,4]{1,0:T(2,128)} %bitcast.6, s32[2]{0:T(128)} %bitcast.12, f32[38,8,512]{2,1,0:T(8,128)} %get-tuple-element.17.table, ...), custom_call_target="tpu_custom_call" | custom-call | tf_op jit(solution)/shard_map/tiles/pallas_call | solution.py:465
  47.5 0.0 copy-start
  47.5 22.2 %give_back.1 = f32[3,4,512]{2,1,0:T(4,128)} custom-call(s32[4]{0:T(128)} %counts_h.1, s32[32]{0:T(128)} %bitcast.10, s32[2]{0:T(128)} %bitcast.13, s32[2,4]{1,0:T(2,128)} %bitcast.7, f32[35,4,512]{2,1,0:T(4,128)} %get-tuple-element.26.back, f32[38,8,512]{2,1,0:T(8,128)} %get-tuple-element.17.table, bf16[104,128,256]{2,1,0:T(8,128)(2,1)} %get-tuple-element.27.g_in, ...), custom_call_target="tpu_custom_call" | custom-call | tf_op jit(solution)/shard_map/give_back/pallas_call | solution.py:776
  69.8 0.0 copy-done
  69.8 1.4 %add.3 = f32[3,4,512]{2,1,0:T(4,128)} add(f32[3,4,512]{2,1,0:T(4,128)S(1)} %copy-done, f32[3,4,512]{2,1,0:T(4,128)} %give_back.1) | non-fusion elementwise | flops 6144 | bytes 73728 | tf_op jit(solution)/shard_map/add | solution.py:813
Async XLA Ops:
  47.5 22.2 %copy-start = (f32[3,4,512]{2,1,0:T(4,128)S(1)}, f32[3,4,512]{2,1,0:T(4,128)}, u32[]{:S(2)}) copy-start(f32[3,4,512]{2,1,0:T(4,128)} %get-tuple-element.25) | copy-start | bytes 73732

commit v6 on v5

--- a/solution.py
+++ b/solution.py
@@ -11,6 +11,7 @@
 F32, BF16, I32 = jnp.float32, jnp.bfloat16, jnp.int32
 U = 3
 UL = 4
+EARLY = 2
 PEERS = 32
 LOWER, UPPER, OWN, NSLOT = 32, 33, 34, 38
 MAXT = 34
@@ -132,7 +133,7 @@
         store_target(own[a], a * 4, feat_o, s_o, m_o, rows_o)
 
 
-def local_tiles(pair_ref, emit, feat_s, rows_s, lane_s, feat_o, s_o, m_o, rows_o, near_a, near_b,
+def local_tiles(pair_ref, emit, between, feat_s, rows_s, lane_s, feat_o, s_o, m_o, rows_o, near_a, near_b,
                 gst, acc_w, row_w, acc_g, row_g):
     acc_w[...] = jnp.zeros_like(acc_w)
     row_w[...] = jnp.zeros_like(row_w)
@@ -201,7 +202,7 @@
 
     step = 2 * UL
 
-    def body(n, carry):
+    def body(emits, n, carry):
         prev, now, later = carry
         base = n * step
         before = jnp.where(n == 0, LOCAL + 2 * UL, base - UL)
@@ -214,14 +215,17 @@
         elements(near_b, later, base + UL)
         distances(near_a, after)
         collect(sums, now)
-        for part, (_, last, _, _) in enumerate(PARTS):
-            pl.when(n == last // step - 1)(functools.partial(emit, part))
+        if emits:
+            for part, (_, last, _, _) in enumerate(PARTS):
+                pl.when(n == last // step - 1)(functools.partial(emit, part))
         return later, after, group(base + step + UL)
 
     state = group(I32(0))
     distances(near_a, state)
     state = (state, state, group(I32(UL)))
-    state = lax.fori_loop(0, LOCAL // step, body, state)
+    state = lax.fori_loop(0, EARLY, functools.partial(body, False), state)
+    between()
+    state = lax.fori_loop(EARLY, LOCAL // step, functools.partial(body, True), state)
     collect(products(state[0], LOCAL - UL), state[0])
 
 
@@ -441,21 +445,23 @@
             q_wide[a * 4 + jb, :, 0:128] = plain[:, cut]
             q_wide[a * 4 + jb, :, 128:256] = plain[:, cut]
 
-    def mirror(step, base):
-        for u in range(2):
-            tile = 2 * step + u
-            a, s, ni, nj = at(tile)
-            q = q_rows[a]
-            st = table[s]
+    def mirror(_, state):
+        for u in range(8):
+            tile, jb, a, s, ni, nj, base = state
             slot = jnp.where(tile < count, s, OWN)
-            for jb in range(4):
-                cut = slice(jb * 128, (jb + 1) * 128)
-                o = fold(nn(q, gst[pl.ds(base + jb * ni, 4)].reshape(512, 256)))
-                o = o[:8] + o[8:]
-                t_out[slot, :, cut] = (st[:, cut] * o[0:1] - o)[0:4]
-            base = base + ni * nj
-        return base
-    lax.fori_loop(0, (count + 1) // 2, mirror, I32(U))
+            cut = pl.ds(pl.multiple_of(jb * 128, 128), 128)
+            o = fold(nn(q_rows[a], gst[pl.ds(base, 4)].reshape(512, 256)))
+            o = o[:8] + o[8:]
+            t_out[slot, :, cut] = (table[s, :, cut] * o[0:1] - o)[0:4]
+            jb = jb + 1
+            wrap = jb >= nj
+            jb = jnp.where(wrap, 0, jb)
+            tile = jnp.where(wrap, jnp.minimum(tile + 1, count), tile)
+            base = jnp.where(tile < count, base + ni, base)
+            state = (tile, jb) + at(tile) + (base,)
+        return state
+    panels = lax.fori_loop(0, count, lambda k, v: v + blocks(ts[k]), I32(0))
+    lax.fori_loop(0, (panels + 7) // 8, mirror, (zero, zero) + at(zero) + (I32(U),))
 
 
 def compute(send, pairs, edge, table, energy, local):
@@ -554,15 +560,25 @@
     return region, cell, lax.rem(region + count - 1, count), lax.rem(region + 1, count)
 
 
+def peer_of(cell, k):
+
+    def far(i):
+        return jnp.where(i == 0, 2, jnp.where(i == 1, 1, jnp.where(i == 2, 3, 0)))
+    x = lax.rem(cell // 8 + far(k // 8), 4)
+    y = lax.rem(cell // 2 + far(lax.rem(k // 2, 4)), 4)
+    core = lax.rem(cell + 1 - lax.rem(k, 2), 2)
+    return x * 8 + y * 2 + core
+
+
 def greet():
     region, cell, below, above = place()
     barrier = pltpu.get_barrier_semaphore()
 
     def one(k, _):
-        peer = lax.rem(cell + k, PEERS)
+        peer = peer_of(cell, k)
         pl.semaphore_signal(barrier, inc=1, device_id=(region, peer), device_id_type=MESH)
         return 0
-    lax.fori_loop(1, PEERS, one, 0)
+    lax.fori_loop(0, PEERS - 1, one, 0)
     pl.semaphore_signal(barrier, inc=1, device_id=(below, cell), device_id_type=MESH)
     pl.semaphore_signal(barrier, inc=1, device_id=(above, cell), device_id_type=MESH)
     return barrier
@@ -610,18 +626,6 @@
     payload[cell] = jnp.zeros((8, 512), F32)
     pltpu.make_async_copy(payload.at[cell], table.at[cell], local_sem.at[4]).start()
     local_features(own, *scratch)
-    pl.semaphore_wait(barrier, PEERS + 1)
-    remote(payload, table, send_sem, recv_sem, LOWER, UPPER, (below, cell)).start()
-    remote(payload, table, send_sem, recv_sem, UPPER, LOWER, (above, cell)).start()
-
-    def push(k, _):
-        peer = lax.rem(cell + k, PEERS)
-        pick = send_ref[peer]
-        payload[peer] = jnp.where(pick >= 0, own[jnp.maximum(pick, 0)], 0.0)
-        remote(payload, table, send_sem, recv_sem, peer, cell, (region, peer)).start()
-        return 0
-    lax.fori_loop(1, PEERS, push, 0)
-
     acc_w, row_w, acc_g, row_g, feat_o, s_o = local_results(scratch)
     first = [
         pltpu.make_async_copy(feat_o, outs[4], local_sem.at[5]),
@@ -646,7 +650,20 @@
         for copy in part_copies(part):
             copy.start()
 
-    local_tiles(pair_ref, emit, *scratch)
+    def between():
+        pl.semaphore_wait(barrier, PEERS + 1)
+        remote(payload, table, send_sem, recv_sem, LOWER, UPPER, (below, cell)).start()
+        remote(payload, table, send_sem, recv_sem, UPPER, LOWER, (above, cell)).start()
+
+        def push(k, _):
+            peer = peer_of(cell, k)
+            pick = send_ref[peer]
+            payload[peer] = jnp.where(pick >= 0, own[jnp.maximum(pick, 0)], 0.0)
+            remote(payload, table, send_sem, recv_sem, peer, cell, (region, peer)).start()
+            return 0
+        lax.fori_loop(0, PEERS - 1, push, 0)
+
+    local_tiles(pair_ref, emit, between, *scratch)
     for copy in rest:
         copy.start()
     for k in range(4):
@@ -722,10 +739,10 @@
     pl.semaphore_wait(barrier, PEERS + 1)
 
     def push(k, _):
-        peer = lax.rem(cell + k, PEERS)
+        peer = peer_of(cell, k)
         remote(back, inbox, send_sem, recv_sem, peer, cell, (region, peer)).start()
         return 0
-    lax.fori_loop(1, PEERS, push, 0)
+    lax.fori_loop(0, PEERS - 1, push, 0)
     remote(back, inbox, send_sem, recv_sem, LOWER, UPPER, (below, cell)).start()
     remote(back, inbox, send_sem, recv_sem, UPPER, LOWER, (above, cell)).start()
 

time: 71.3 us -> 69.3 us (0.972); the launches traced: 71.1 us -> 68.2 us
  Pallas kernels: 69.1 us -> 66.2 us
    pallas_call x1, Pallas kernels: 22.2 us -> 18.9 us  [give_back(): pl.pallas_call(return_kernel, out_shape=jax.ShapeDtypeStruct((3, 4, 512),...]
    pallas_call x1, Pallas kernels: 25.3 us -> 26.6 us  [compute(): pl.pallas_call(compute_kernel, out_shape=(jax.ShapeDtypeStruct((4, 512),...]
    pallas_call x1, Pallas kernels: 21.6 us -> 20.7 us  [exchange(): pl.pallas_call(exchange_kernel, out_shape=(jax.ShapeDtypeStruct((NSLOT, 8...]
where the time goes in v6:
time: 69.3 us; the launch traced here: 68.2 us
  Pallas kernels  66.2 us (96%)
  other arithmetic  1.35 us (2%)
    pallas_call x1, Pallas kernels, compute(): pl.pallas_call(compute_kernel, out_shape=(jax.ShapeDtypeStruct((4, 512),...  26.6 us
    pallas_call x1, Pallas kernels, exchange(): pl.pallas_call(exchange_kernel, out_shape=(jax.ShapeDtypeStruct((NSLOT, 8...  20.7 us
    pallas_call x1, Pallas kernels, give_back(): pl.pallas_call(return_kernel, out_shape=jax.ShapeDtypeStruct((3, 4, 512),...  18.9 us

profile of v6, /device:TPU:1, one launch (start us, length us, event | category | flops | bytes accessed | tf_op | source)
XLA Modules:
  0.0 68.2 jit_solution(16374776733804272765)
XLA Ops:
  0.6 20.7 %exchange.1 = (f32[38,8,512]{2,1,0:T(8,128)}, bf16[104,128,256]{2,1,0:T(8,128)(2,1)}, f32[32,128,128]{2,1,0:T(8,128)}, f32[32,8,128]{2,1,0:T(8,128)}, f32[32,16,...) custom-call(s32[4]{0:T(128)} %counts_h.1, s32[32]{0:T(128)} %bitcast.8, ...), custom_call_target="tpu_custom_call" | custom-call | tf_op jit(solution)/shard_map/exchange/pallas_call | solution.py:693
  21.3 26.6 %tiles.1 = (f32[4,512]{1,0:T(4,128)}, f32[3,4,512]{2,1,0:T(4,128)}, f32[4,512]{1,0:T(4,128)}, f32[35,4,512]{2,1,0:T(4,128)}, bf16[4,16,512]{2,1,0:T(8,128)(2,1)}, /*index=5*/bf16[16,16,256]{2,1,0:T(8,128)(2,1)}) custom-call(s32[32]{0:T(128)} %bitcast.9, s32[2,4]{1,0:T(2,128)} %bitcast.6, s32[2]{0:T(128)} %bitcast.12, f32[38,8,512]{2,1,0:T(8,128)} %get-tuple-element.17.table, ...), custom_call_target="tpu_custom_call" | custom-call | tf_op jit(solution)/shard_map/tiles/pallas_call | solution.py:471
  47.9 0.0 copy-start
  47.9 18.9 %give_back.1 = f32[3,4,512]{2,1,0:T(4,128)} custom-call(s32[4]{0:T(128)} %counts_h.1, s32[32]{0:T(128)} %bitcast.10, s32[2]{0:T(128)} %bitcast.13, s32[2,4]{1,0:T(2,128)} %bitcast.7, f32[35,4,512]{2,1,0:T(4,128)} %get-tuple-element.26.back, f32[38,8,512]{2,1,0:T(8,128)} %get-tuple-element.17.table, bf16[104,128,256]{2,1,0:T(8,128)(2,1)} %get-tuple-element.27.g_in, ...), custom_call_target="tpu_custom_call" | custom-call | tf_op jit(solution)/shard_map/give_back/pallas_call | solution.py:793
  66.9 0.0 copy-done
  66.9 1.4 %add.3 = f32[3,4,512]{2,1,0:T(4,128)} add(f32[3,4,512]{2,1,0:T(4,128)S(1)} %copy-done, f32[3,4,512]{2,1,0:T(4,128)} %give_back.1) | non-fusion elementwise | flops 6144 | bytes 73728 | tf_op jit(solution)/shard_map/add | solution.py:830
Async XLA Ops:
  47.9 19.0 %copy-start = (f32[3,4,512]{2,1,0:T(4,128)S(1)}, f32[3,4,512]{2,1,0:T(4,128)}, u32[]{:S(2)}) copy-start(f32[3,4,512]{2,1,0:T(4,128)} %get-tuple-element.25) | copy-start | bytes 73732

commit v7 on v6

--- a/solution.py
+++ b/solution.py
@@ -560,25 +560,20 @@
     return region, cell, lax.rem(region + count - 1, count), lax.rem(region + 1, count)
 
 
-def peer_of(cell, k):
-
-    def far(i):
-        return jnp.where(i == 0, 2, jnp.where(i == 1, 1, jnp.where(i == 2, 3, 0)))
-    x = lax.rem(cell // 8 + far(k // 8), 4)
-    y = lax.rem(cell // 2 + far(lax.rem(k // 2, 4)), 4)
-    core = lax.rem(cell + 1 - lax.rem(k, 2), 2)
-    return x * 8 + y * 2 + core
+def peers_of(cell):
+    order = (2, 1, 3, 0)
+    x, y, core = cell // 8, lax.rem(cell // 2, 4), lax.rem(cell, 2)
+    xs = [lax.rem(x + step, 4) * 8 for step in order]
+    ys = [lax.rem(y + step, 4) * 2 for step in order]
+    return [i + j + k for i in xs for j in ys for k in (1 - core, core)][:-1]
 
 
 def greet():
     region, cell, below, above = place()
     barrier = pltpu.get_barrier_semaphore()
 
-    def one(k, _):
-        peer = peer_of(cell, k)
+    for peer in peers_of(cell):
         pl.semaphore_signal(barrier, inc=1, device_id=(region, peer), device_id_type=MESH)
-        return 0
-    lax.fori_loop(0, PEERS - 1, one, 0)
     pl.semaphore_signal(barrier, inc=1, device_id=(below, cell), device_id_type=MESH)
     pl.semaphore_signal(barrier, inc=1, device_id=(above, cell), device_id_type=MESH)
     return barrier
@@ -655,13 +650,10 @@
         remote(payload, table, send_sem, recv_sem, LOWER, UPPER, (below, cell)).start()
         remote(payload, table, send_sem, recv_sem, UPPER, LOWER, (above, cell)).start()
 
-        def push(k, _):
-            peer = peer_of(cell, k)
+        for peer in peers_of(cell):
             pick = send_ref[peer]
             payload[peer] = jnp.where(pick >= 0, own[jnp.maximum(pick, 0)], 0.0)
             remote(payload, table, send_sem, recv_sem, peer, cell, (region, peer)).start()
-            return 0
-        lax.fori_loop(0, PEERS - 1, push, 0)
 
     local_tiles(pair_ref, emit, between, *scratch)
     for copy in rest:
@@ -738,11 +730,8 @@
     inbox[cell] = jnp.zeros((4, 512), F32)
     pl.semaphore_wait(barrier, PEERS + 1)
 
-    def push(k, _):
-        peer = peer_of(cell, k)
+    for peer in peers_of(cell):
         remote(back, inbox, send_sem, recv_sem, peer, cell, (region, peer)).start()
-        return 0
-    lax.fori_loop(0, PEERS - 1, push, 0)
     remote(back, inbox, send_sem, recv_sem, LOWER, UPPER, (below, cell)).start()
     remote(back, inbox, send_sem, recv_sem, UPPER, LOWER, (above, cell)).start()
 

time: 69.3 us -> 67.8 us (0.978); the launches traced: 68.2 us -> 68 us
    pallas_call x1, Pallas kernels: 18.9 us -> 26.1 us  [give_back(): pl.pallas_call(return_kernel, out_shape=jax.ShapeDtypeStruct((3, 4, 512),...]
    pallas_call x1, Pallas kernels: 26.6 us -> 20.6 us  [compute(): pl.pallas_call(compute_kernel, out_shape=(jax.ShapeDtypeStruct((4, 512),...]
    pallas_call x1, Pallas kernels: 20.7 us -> 19.2 us  [exchange(): pl.pallas_call(exchange_kernel, out_shape=(jax.ShapeDtypeStruct((NSLOT, 8...]
where the time goes in v7:
time: 67.8 us; the launch traced here: 68 us
  Pallas kernels  65.9 us (97%)
  other arithmetic  1.35 us (2%)
    pallas_call x1, Pallas kernels, give_back(): pl.pallas_call(return_kernel, out_shape=jax.ShapeDtypeStruct((3, 4, 512),...  26.1 us
    pallas_call x1, Pallas kernels, compute(): pl.pallas_call(compute_kernel, out_shape=(jax.ShapeDtypeStruct((4, 512),...  20.6 us
    pallas_call x1, Pallas kernels, exchange(): pl.pallas_call(exchange_kernel, out_shape=(jax.ShapeDtypeStruct((NSLOT, 8...  19.2 us

profile of v7, /device:TPU:1, one launch (start us, length us, event | category | flops | bytes accessed | tf_op | source)
XLA Modules:
  0.0 68.0 jit_solution(12932380271456818890)
XLA Ops:
  0.6 19.2 %exchange.1 = (f32[38,8,512]{2,1,0:T(8,128)}, bf16[104,128,256]{2,1,0:T(8,128)(2,1)}, f32[32,128,128]{2,1,0:T(8,128)}, f32[32,8,128]{2,1,0:T(8,128)}, f32[32,16,...) custom-call(s32[4]{0:T(128)} %counts_h.1, s32[32]{0:T(128)} %bitcast.8, ...), custom_call_target="tpu_custom_call" | custom-call | tf_op jit(solution)/shard_map/exchange/pallas_call | solution.py:685
  19.9 20.6 %tiles.1 = (f32[4,512]{1,0:T(4,128)}, f32[3,4,512]{2,1,0:T(4,128)}, f32[4,512]{1,0:T(4,128)}, f32[35,4,512]{2,1,0:T(4,128)}, bf16[4,16,512]{2,1,0:T(8,128)(2,1)}, /*index=5*/bf16[16,16,256]{2,1,0:T(8,128)(2,1)}) custom-call(s32[32]{0:T(128)} %bitcast.9, s32[2,4]{1,0:T(2,128)} %bitcast.6, s32[2]{0:T(128)} %bitcast.12, f32[38,8,512]{2,1,0:T(8,128)} %get-tuple-element.17.table, ...), custom_call_target="tpu_custom_call" | custom-call | tf_op jit(solution)/shard_map/tiles/pallas_call | solution.py:471
  40.5 0.0 copy-start
  40.5 26.1 %give_back.1 = f32[3,4,512]{2,1,0:T(4,128)} custom-call(s32[4]{0:T(128)} %counts_h.1, s32[32]{0:T(128)} %bitcast.10, s32[2]{0:T(128)} %bitcast.13, s32[2,4]{1,0:T(2,128)} %bitcast.7, f32[35,4,512]{2,1,0:T(4,128)} %get-tuple-element.26.back, f32[38,8,512]{2,1,0:T(8,128)} %get-tuple-element.17.table, bf16[104,128,256]{2,1,0:T(8,128)(2,1)} %get-tuple-element.27.g_in, ...), custom_call_target="tpu_custom_call" | custom-call | tf_op jit(solution)/shard_map/give_back/pallas_call | solution.py:782
  66.6 0.0 copy-done
  66.6 1.4 %add.3 = f32[3,4,512]{2,1,0:T(4,128)} add(f32[3,4,512]{2,1,0:T(4,128)S(1)} %copy-done, f32[3,4,512]{2,1,0:T(4,128)} %give_back.1) | non-fusion elementwise | flops 6144 | bytes 73728 | tf_op jit(solution)/shard_map/add | solution.py:819
Async XLA Ops:
  40.5 26.1 %copy-start = (f32[3,4,512]{2,1,0:T(4,128)S(1)}, f32[3,4,512]{2,1,0:T(4,128)}, u32[]{:S(2)}) copy-start(f32[3,4,512]{2,1,0:T(4,128)} %get-tuple-element.25) | copy-start | bytes 73732
